TPU v7x, 512 devices: a whole 4x4x16 slice. The times are simulated.
512 devices in a mesh: space: 128 (over z, x, core), blk: 4 (over y).
Axes of the slice: x: 4, y: 4, z: 16, core: 2. Of those that a mesh axis runs over, the one named last changes fastest.
Arguments:
- pressure: float32 [512, 262144], P('blk', 'space'), may hold values from -6 to 6
- final_steps: float32 [128, 262144], P(None, 'space'), may hold values from -6 to 6
- weights: float32 [262144], P('space'), may hold values from 0.5 to 4.5, as said below
Outputs:
- spectra: bfloat16 [4, 128, 2, 262144], P(None, 'blk', None, 'space')
- csd: float32 [2, 128, 4, 4], P(None, 'blk')
Inputs may be any that keep to these rules, and one draw needn't show every extreme that they name: Positive weights.
All inputs are finite; a program needn't handle non-finite values.
Results may differ from a plain program's by a relative error of at most 0.0055.
Values may be sent and summed in bfloat16 or wider, within the bound.
No kernel may reach another device: no remote copies, remote signals or barrier semaphores. Data moves between devices by JAX's collectives and lax.ppermute only.
A program may use at most 64 MiB of HBM per device.

v0:
```python
import math

import jax
import jax.numpy as jnp
from jax import lax
from jax.sharding import PartitionSpec as P

HOP = 128


def passed_along(value, axis, steps):
    count = lax.axis_size(axis)
    leading, last = (max(0, -steps), min(count, count - steps))
    return lax.ppermute(value, axis, [(source, source + steps) for source in range(leading, last)])


def make_table(blen, nfreq):
    t = jnp.arange(blen, dtype=jnp.int32)
    k = jnp.arange(nfreq, dtype=jnp.int32)
    phase = k[:, None] * t[None, :] % blen
    angle = 2.0 * math.pi / blen * phase.astype(jnp.float32)
    scale = 1.0 / math.sqrt(3.0 * blen / 8.0)
    table = jnp.stack([jnp.cos(angle) * scale, -jnp.sin(angle) * scale], axis=1)
    return table.reshape(2 * nfreq, blen).astype(jnp.bfloat16)


def make_hann(blen):
    t = jnp.arange(blen, dtype=jnp.float32)
    return 0.5 - 0.5 * jnp.cos(2.0 * math.pi / blen * t)


def cross_sums(spectra, weights, count):
    values = spectra.astype(jnp.float32)
    real_part = values[:, :, 0]
    imag_part = values[:, :, 1]
    high = lax.Precision.HIGHEST
    real_w = real_part * weights
    imag_w = imag_part * weights
    first = jnp.einsum("ikn,jkn->kij", real_w, real_part, precision=high) + jnp.einsum(
        "ikn,jkn->kij", imag_w, imag_part, precision=high
    )
    second = jnp.einsum("ikn,jkn->kij", imag_w, real_part, precision=high) - jnp.einsum(
        "ikn,jkn->kij", real_w, imag_part, precision=high
    )
    return jnp.stack([first, second], axis=0) / count


def local(pressure, final_steps, weights):
    blocks_count = lax.axis_size("blk")
    position = lax.axis_index("blk")
    is_last = position == blocks_count - 1
    points = pressure.shape[1]
    own_sum = jnp.sum(pressure, axis=0) + jnp.where(is_last, jnp.sum(final_steps, axis=0), 0.0)
    total = lax.psum(own_sum, "blk")
    mean = total / (HOP * (blocks_count + 1))
    blen = 2 * HOP
    hann = make_hann(blen)
    table = make_table(blen, HOP)
    following = passed_along(pressure, "blk", -1)
    following = jnp.where(is_last, final_steps, following)
    segment = jnp.concatenate([pressure, following], axis=0) - mean
    windowed = (segment * hann[:, None]).astype(jnp.bfloat16)
    coeff = jnp.dot(table, windowed, preferred_element_type=jnp.float32).astype(jnp.bfloat16)
    coeff = coeff.reshape(1, HOP, 2, points)
    spectra = lax.all_to_all(coeff, "blk", split_axis=1, concat_axis=0, tiled=True)
    partial_sums = cross_sums(spectra, weights, float(points * lax.axis_size("space")))
    csd = lax.psum(partial_sums, "space")
    return (spectra, csd)


def solution(mesh):
    return jax.shard_map(
        local,
        mesh=mesh,
        in_specs=(P("blk", "space"), P(None, "space"), P("space")),
        out_specs=(P(None, "blk", None, "space"), P(None, "blk", None, None)),
        check_vma=False,
    )
```

profile of v0, /device:TPU:1, one launch (start us, length us, event | category | flops | bytes accessed | tf_op | source)
XLA Modules:
  0.0 563.5 jit_solution(6257103232243127901)
XLA Ops:
  0.6 0.0 copy-start
  0.6 1.4 collective-permute-start
  2.1 1.3 reduce_sum.18
  3.4 0.0 copy-start.1
  3.4 0.5 multiply_convert_fusion
  3.9 0.1 copy.38
  4.1 0.1 convert_element_type.30
  4.2 17.8 %collective-permute-done = f32[128,2048]{1,0:T(8,128)S(1)} collective-permute-done((f32[128,2048]{1,0:T(8,128)}, f32[128,2048]{1,0:T(8,128)S(1)}, u32[]{:S(2)}, u32[]{:S(2)}) %collective-permute-start) | collective-permute-done | bytes 1048608 | tf_op jit(solution)/shard_map/ppermute | solution.py:14
  22.0 0.0 copy-done
  22.0 1.1 fusion.23
  23.1 13.1 %psum.14 = f32[2048]{0:T(1024)S(1)} all-reduce(f32[2048]{0:T(1024)S(1)} %select_add_fusion), channel_id=1, replica_groups=mesh['space'=128,'blk'=4] {'blk'}, use_global_device_ids=true, to_apply=%region_2.3 | all-reduce | flops 2048 | bytes 16384 | tf_op jit(solution)/shard_map/psum | solution.py:54
  36.2 0.0 copy-done.1
  36.2 1.8 convolution_convert_fusion
  38.0 0.7 reshape.96
  38.7 13.7 %all_to_all.12 = bf16[1,128,2,2048]{3,2,0,1:T(2,128)(2,1)S(1)} all-to-all(bf16[1,128,2,2048]{3,2,0,1:T(2,128)(2,1)S(1)} %bitcast.26), channel_id=1, replica_groups=mesh['space'=128,'blk'=4] {'blk'}, dimensions={1} | all-to-all | bytes 2097152 | tf_op jit(solution)/shard_map/all_to_all | solution.py:65
  52.5 0.3 copy.40
  52.8 0.2 convert_element_type.33
  53.1 0.0 copy-start.2
  53.1 0.1 fusion.22
  53.2 2.0 copy.49
  55.2 0.0 copy-done.2
  55.2 0.2 fusion.6
  55.5 2.8 fusion.13
  58.2 2.8 fusion.9
  61.1 2.4 fusion.3
  63.5 0.1 copy.47
  63.6 2.8 fusion.2
  66.4 0.1 copy.48
  66.5 497.0 %psum.15 = f32[2,32,4,4]{1,3,2,0:T(4,128)} all-reduce(f32[2,32,4,4]{1,3,2,0:T(4,128)S(1)} %maximum_multiply_fusion), channel_id=1, replica_groups=mesh['space'=128,'blk'=4] {'space'}, use_global_device_ids=true, to_apply=%region_3.4 | all-reduce | flops 1024 | bytes 8192 | tf_op jit(solution)/shard_map/psum | solution.py:67
  (5 shorter events, 0.1 us)
Async XLA Ops:
  0.6 21.4 %copy-start = (f32[128,2048]{1,0:T(8,128)S(1)}, f32[128,2048]{1,0:T(8,128)}, u32[]{:S(2)}) copy-start(f32[128,2048]{1,0:T(8,128)} %param.4) | copy-start | bytes 3145732
  0.6 21.4 %collective-permute-start = (f32[128,2048]{1,0:T(8,128)}, f32[128,2048]{1,0:T(8,128)S(1)}, u32[]{:S(2)}, u32[]{:S(2)}) collective-permute-start(f32[128,2048]{1,0:T(8,128)} %param.3), channel_id=1, source_target_pairs={{1,0},{2,1},{3,2},{5,4},{6,5},{7,6},{9,8},{10,9},{11,10},{13,12},{... | collective-permute-start | bytes 3145736 | tf_op jit(solution)/shard_map/ppermute | solution.py:14
  3.4 32.9 %copy-start.1 = (f32[128,2048]{1,0:T(8,128)S(1)}, f32[128,2048]{1,0:T(8,128)}, u32[]{:S(2)}) copy-start(f32[128,2048]{1,0:T(8,128)} %param.3) | copy-start | bytes 3145732
  53.1 2.2 copy-start.2
where the time goes:
time: 567 us; the launch traced here: 563 us
  blocking collectives  524 us (92%)
  waiting for transfers between devices  17.8 us (3%)
  matrix products  12.6 us (2%)
    psum x1, blocking collectives, local(): csd = lax.psum(partial_sums, 'space')  497 us
    ppermute x1, waiting for transfers between devices, passed_along(): lax.ppermute(value, axis, [(source, source + steps) for source in range(l...  17.8 us
    all_to_all x1, blocking collectives, local(): lax.all_to_all(coeff, 'blk', split_axis=1, concat_axis=0, tiled=True)  13.7 us
    psum x1, blocking collectives, local(): total = lax.psum(own_sum, 'blk')  13.1 us
  transfers between devices with their start and end apart: 1, of which 1 were waited for; matrix products, arithmetic and copies ran while one was open for 0% of the time, Pallas kernels for 0%

commit v1 on v0

--- a/solution.py
+++ b/solution.py
@@ -3,9 +3,17 @@
 import jax
 import jax.numpy as jnp
 from jax import lax
+from jax.sharding import Mesh
 from jax.sharding import PartitionSpec as P
 
 HOP = 128
+SPACE = ("z", "x", "core")
+
+
+def summed_over(value, axes):
+    count = lax.axis_size(axes)
+    sent = jnp.broadcast_to(value[None], (count, *value.shape))
+    return jnp.sum(lax.all_to_all(sent, axes, 0, 0, tiled=True), axis=0)
 
 
 def passed_along(value, axis, steps):
@@ -63,16 +71,19 @@
     coeff = jnp.dot(table, windowed, preferred_element_type=jnp.float32).astype(jnp.bfloat16)
     coeff = coeff.reshape(1, HOP, 2, points)
     spectra = lax.all_to_all(coeff, "blk", split_axis=1, concat_axis=0, tiled=True)
-    partial_sums = cross_sums(spectra, weights, float(points * lax.axis_size("space")))
-    csd = lax.psum(partial_sums, "space")
+    partial_sums = cross_sums(spectra, weights, float(points * lax.axis_size(SPACE)))
+    flat = jnp.transpose(partial_sums, (0, 2, 3, 1)).reshape(-1)
+    flat = summed_over(summed_over(flat, ("x", "core")), ("z",))
+    csd = jnp.transpose(flat.reshape(2, blocks_count, blocks_count, -1), (0, 3, 1, 2))
     return (spectra, csd)
 
 
 def solution(mesh):
+    split = Mesh(mesh.devices.reshape(-1, 4, 2, mesh.shape["blk"]), (*SPACE, "blk"))
     return jax.shard_map(
         local,
-        mesh=mesh,
-        in_specs=(P("blk", "space"), P(None, "space"), P("space")),
-        out_specs=(P(None, "blk", None, "space"), P(None, "blk", None, None)),
+        mesh=split,
+        in_specs=(P("blk", SPACE), P(None, SPACE), P(SPACE)),
+        out_specs=(P(None, "blk", None, SPACE), P(None, "blk", None, None)),
         check_vma=False,
     )

time: 567 us -> 107 us (0.19)
  blocking collectives: 524 us -> 40.4 us
  starting transfers between devices: 1.42 us -> 16.3 us
  waiting for transfers between devices: 17.8 us -> 27.3 us
    psum x1 -> x0, blocking collectives: 497 us -> none  [local(): csd = lax.psum(partial_sums, 'space')]
    all_to_all x0 -> x1, starting transfers between devices: none -> 14.9 us  [summed_over(): return jnp.sum(lax.all_to_all(sent, axes, 0, 0, tiled=True), axis=0)]
    all_to_all x0 -> x1, blocking collectives: none -> 13.5 us  [summed_over(): return jnp.sum(lax.all_to_all(sent, axes, 0, 0, tiled=True), axis=0)]
    all_to_all x0 -> x1, waiting for transfers between devices: none -> 9.52 us  [summed_over(): return jnp.sum(lax.all_to_all(sent, axes, 0, 0, tiled=True), axis=0)]
  transfers between devices with their start and end apart: 1 -> 2, of which waited for: 1 -> 2; matrix products, arithmetic and copies ran while one was open for 0% -> 4% of each run, Pallas kernels for 0% -> 0%
where the time goes in v1:
time: 107 us; the launch traced here: 106 us
  blocking collectives  40.4 us (38%)
  waiting for transfers between devices  27.3 us (26%)
  starting transfers between devices  16.3 us (15%)
  matrix products  12.6 us (12%)
  local copies, waits for them, and re-layouts  5.4 us (5%)
  other arithmetic  3.56 us (3%)
    ppermute x1, waiting for transfers between devices, passed_along(): lax.ppermute(value, axis, [(source, source + steps) for source in range(l...  17.8 us
    all_to_all x1, starting transfers between devices, summed_over(): return jnp.sum(lax.all_to_all(sent, axes, 0, 0, tiled=True), axis=0)  14.9 us
    all_to_all x1, blocking collectives, local(): lax.all_to_all(coeff, 'blk', split_axis=1, concat_axis=0, tiled=True)  13.7 us
    all_to_all x1, blocking collectives, summed_over(): return jnp.sum(lax.all_to_all(sent, axes, 0, 0, tiled=True), axis=0)  13.5 us
    psum x1, blocking collectives, local(): total = lax.psum(own_sum, 'blk')  13.1 us
    all_to_all x1, waiting for transfers between devices, summed_over(): return jnp.sum(lax.all_to_all(sent, axes, 0, 0, tiled=True), axis=0)  9.52 us
    dot_general x1, matrix products, cross_sums(): jnp.einsum('ikn,jkn->kij', real_w, imag_part, precision=high)  2.8 us
    dot_general x1, matrix products, cross_sums(): jnp.einsum('ikn,jkn->kij', real_w, real_part, precision=high)  2.8 us
  transfers between devices with their start and end apart: 2, of which 2 were waited for; matrix products, arithmetic and copies ran while one was open for 4% of the time, Pallas kernels for 0%

profile of v1, /device:TPU:1, one launch (start us, length us, event | category | flops | bytes accessed | tf_op | source)
XLA Modules:
  0.0 106.4 jit_solution(12312977914199042446)
XLA Ops:
  0.6 0.0 copy-start
  0.6 1.4 %collective-permute-start = (f32[128,2048]{1,0:T(8,128)}, f32[128,2048]{1,0:T(8,128)S(1)}, u32[]{:S(2)}, u32[]{:S(2)}) collective-permute-start(f32[128,2048]{1,0:T(8,128)} %param.3), channel_id=1, source_target_pairs={{1,0},{2,1},{3,2},{5,4},{6,5},{7,6},{9,8},{10,9},{11,10},{13,12},{... | collective-permute-start | bytes 3145736 | tf_op jit(solution)/shard_map/ppermute | solution.py:22
  2.1 1.3 %reduce_sum.36 = f32[2048]{0:T(1024)S(1)} reduce(f32[128,2048]{1,0:T(8,128)} %param.3, f32[]{:T(128)} %constant.32.clone.1), dimensions={0}, to_apply=%region_0.0 | reduce | flops 260096 | bytes 1056772 | tf_op jit(solution)/shard_map/reduce_sum | solution.py:61
  3.4 0.0 copy-start.1
  3.4 0.5 multiply_convert_fusion
  3.9 0.1 copy.63
  4.1 0.1 convert_element_type.30
  4.2 17.8 %collective-permute-done = f32[128,2048]{1,0:T(8,128)S(1)} collective-permute-done((f32[128,2048]{1,0:T(8,128)}, f32[128,2048]{1,0:T(8,128)S(1)}, u32[]{:S(2)}, u32[]{:S(2)}) %collective-permute-start) | collective-permute-done | bytes 1048608 | tf_op jit(solution)/shard_map/ppermute | solution.py:22
  22.0 0.0 copy-done
  22.0 1.1 %fusion.24 = (f32[2048]{0:T(1024)S(1)}, f32[128,2048]{1,0:T(8,128)}) fusion(f32[128,2048]{1,0:T(8,128)S(1)} %copy-done, f32[128,2048]{1,0:T(8,128)S(1)} %collective-permute-done, pred[]{:T(512)S(6)} %eq.5), kind=kLoop, calls=%fused_computation.42 | loop fusion | flops 522240 | bytes 3153921 | tf_op jit(solution)/shard_map/reduce_sum | solution.py:61
  23.1 13.1 %psum.7 = f32[2048]{0:T(1024)S(1)} all-reduce(f32[2048]{0:T(1024)S(1)} %select_add_fusion), channel_id=1, replica_groups=mesh['z'=16,'x'=4,'core'=2,'blk'=4] {'blk'}, use_global_device_ids=true, to_apply=%region_2.3 | all-reduce | flops 2048 | bytes 16384 | tf_op jit(solution)/shard_map/psum | solution.py:62
  36.2 0.0 copy-done.1
  36.2 1.8 %convolution_convert_fusion = bf16[256,2048]{1,0:T(8,128)(2,1)S(1)} fusion(bf16[256,256]{1,0:T(8,128)(2,1)S(1)} %convert_element_type.30, f32[128,2048]{1,0:T(8,128)} %get-tuple-element.21, f32[128,2048]{1,0:T(8,128)S(1)} %copy-done.1, f32[256]{0:T(256)S(1)} %multiply_subtract_fusion, f32[2048]{0:T(1024)S(1)} %broadcast_multiply_fusion), kind=kOutput, calls=%fused_computation | convolution fusion | flops 271056896 | bytes 3286016 | tf_op jit(solution)/shard_map/dot_general | solution.py:71
  38.0 0.7 reshape.113
  38.7 13.7 %all_to_all.24 = bf16[1,128,2,2048]{3,2,0,1:T(2,128)(2,1)S(1)} all-to-all(bf16[1,128,2,2048]{3,2,0,1:T(2,128)(2,1)S(1)} %bitcast.29), channel_id=1, replica_groups=mesh['z'=16,'x'=4,'core'=2,'blk'=4] {'blk'}, dimensions={1} | all-to-all | bytes 2097152 | tf_op jit(solution)/shard_map/all_to_all | solution.py:73
  52.5 0.3 copy.65
  52.8 0.0 copy-start.2
  52.8 0.2 convert_element_type.33
  53.1 0.1 fusion.23
  53.2 0.3 copy-done.2
  53.5 0.2 fusion.6
  53.8 2.8 %fusion.13 = f32[32,4,4]{2,1,0:T(4,128)S(1)} fusion(f32[4,32,2048]{2,1,0:T(8,128)S(1)} %get-tuple-element.16, bf16[4,32,1,2048]{3,1,0,2:T(8,128)(2,1)S(1)} %get-tuple-element.19), kind=kOutput, calls=%fused_computation.18 | convolution fusion | flops 12582912 | bytes 1574912 | tf_op jit(solution)/shard_map/ikn,jkn->kij/dot_general | solution.py:47
  56.6 2.8 %fusion.9 = f32[32,4,4]{2,1,0:T(4,128)S(1)} fusion(f32[4,32,2048]{2,1,0:T(8,128)S(1)} %get-tuple-element.17, bf16[4,32,1,2048]{3,1,0,2:T(8,128)(2,1)S(1)} %get-tuple-element.19), kind=kOutput, calls=%fused_computation.14 | convolution fusion | flops 12582912 | bytes 1574912 | tf_op jit(solution)/shard_map/ikn,jkn->kij/dot_general | solution.py:50
  59.4 2.4 %fusion.3 = f32[1,32,4,4]{3,2,1,0:T(4,128)S(1)} fusion(f32[32,4,4]{2,1,0:T(4,128)S(1)} %fusion.13, f32[4,32,2048]{2,1,0:T(8,128)S(1)} %get-tuple-element.17, bf16[4,32,1,2048]{3,1,0,2:T(8,128)(2,1)S(1)} %get-tuple-element.18), kind=kOutput, calls=%fused_computation.7 | convolution fusion | flops 12583424 | bytes 1576960 | tf_op jit(solution)/shard_map/ikn,jkn->kij/dot_general | solution.py:47
  61.8 0.1 copy.72
  61.9 2.8 %fusion.2 = f32[1,32,4,4]{3,2,1,0:T(4,128)S(1)} fusion(f32[32,4,4]{2,1,0:T(4,128)S(1)} %fusion.9, f32[4,32,2048]{2,1,0:T(8,128)S(1)} %get-tuple-element.16, bf16[4,32,1,2048]{3,1,0,2:T(8,128)(2,1)S(1)} %get-tuple-element.18), kind=kOutput, calls=%fused_computation.5 | convolution fusion | flops 12583424 | bytes 1576960 | tf_op jit(solution)/shard_map/ikn,jkn->kij/dot_general | solution.py:50
  64.7 0.1 copy.73
  64.8 0.1 broadcast_in_dim.11
  64.9 13.5 %all_to_all.25 = f32[8,1,1024]{2,1,0:T(1,128)S(1)} all-to-all(f32[8,1,1024]{2,1,0:T(1,128)S(1)} %broadcast_in_dim.12), channel_id=1, replica_groups=mesh['z'=16,'x'=4,'core'=2,'blk'=4] {'x','core'}, dimensions={0} | all-to-all | bytes 65536 | tf_op jit(solution)/shard_map/all_to_all | solution.py:16
  78.5 0.7 broadcast_in_dim.13
  79.1 14.9 %all-to-all-start.2 = ((f32[16,1,1024]{2,1,0:T(1,128)}), f32[16,1,1024]{2,1,0:T(1,128)S(1)}, u32[]{:S(2)}, u32[]{:S(2)}) async-start(f32[16,1,1024]{2,1,0:T(1,128)} %broadcast_in_dim.13), calls=%async_computation.2 | async-start | bytes 131072 | tf_op jit(solution)/shard_map/all_to_all | solution.py:16
  94.1 2.0 %copy.76 = bf16[4,32,2,2048]{3,2,1,0:T(2,128)(2,1)} copy(bf16[4,32,2,2048]{3,1,0,2:T(8,128)(2,1)S(1)} %bitcast.28) | data formatting | bytes 2097152
  96.1 9.5 %all-to-all-done.2 = f32[16,1,1024]{2,1,0:T(1,128)S(1)} async-done(((f32[16,1,1024]{2,1,0:T(1,128)}), f32[16,1,1024]{2,1,0:T(1,128)S(1)}, u32[]{:S(2)}, u32[]{:S(2)}) %all-to-all-start.2) | async-done | bytes 65568 | tf_op jit(solution)/shard_map/all_to_all | solution.py:16
  105.6 0.1 reduce_sum.39
  105.7 0.7 reshape.114
  (7 shorter events, 0.1 us)
Async XLA Ops:
  0.6 21.4 %copy-start = (f32[128,2048]{1,0:T(8,128)S(1)}, f32[128,2048]{1,0:T(8,128)}, u32[]{:S(2)}) copy-start(f32[128,2048]{1,0:T(8,128)} %param.4) | copy-start | bytes 3145732
  0.6 21.4 %collective-permute-start = (f32[128,2048]{1,0:T(8,128)}, f32[128,2048]{1,0:T(8,128)S(1)}, u32[]{:S(2)}, u32[]{:S(2)}) collective-permute-start(f32[128,2048]{1,0:T(8,128)} %param.3), channel_id=1, source_target_pairs={{1,0},{2,1},{3,2},{5,4},{6,5},{7,6},{9,8},{10,9},{11,10},{13,12},{... | collective-permute-start | bytes 3145736 | tf_op jit(solution)/shard_map/ppermute | solution.py:22
  3.4 32.9 %copy-start.1 = (f32[128,2048]{1,0:T(8,128)S(1)}, f32[128,2048]{1,0:T(8,128)}, u32[]{:S(2)}) copy-start(f32[128,2048]{1,0:T(8,128)} %param.3) | copy-start | bytes 3145732
  52.8 0.7 copy-start.2
  79.1 26.5 %all-to-all-start.2 = ((f32[16,1,1024]{2,1,0:T(1,128)}), f32[16,1,1024]{2,1,0:T(1,128)S(1)}, u32[]{:S(2)}, u32[]{:S(2)}) async-start(f32[16,1,1024]{2,1,0:T(1,128)} %broadcast_in_dim.13), calls=%async_computation.2 | async-start | bytes 131072 | tf_op jit(solution)/shard_map/all_to_all | solution.py:16

commit v2 on v1

v2 whole, which is shorter than its diff:
```python
import math

import jax
import jax.numpy as jnp
import numpy as np
from jax import lax
from jax.experimental import pallas as pl
from jax.experimental.pallas import tpu as pltpu
from jax.sharding import Mesh
from jax.sharding import PartitionSpec as P

HOP = 128
BLEN = 2 * HOP
BLOCKS = 4
SPACE = ("z", "x", "core")
LIMIT = 48 * 1024 * 1024
MEANS = 16
PAIRS = [(i, j) for i in range(BLOCKS) for j in range(i, BLOCKS)]
CROSS = [(i, j) for i, j in PAIRS if i < j]
SUMS = len(PAIRS) + len(CROSS)

VMEM = pl.BlockSpec(memory_space=pltpu.VMEM)
SMEM = pl.BlockSpec(memory_space=pltpu.SMEM)


def tables():
    t = np.arange(BLEN)
    k = np.arange(HOP)
    angle = 2.0 * math.pi / BLEN * (k[:, None] * t[None, :] % BLEN)
    scale = 1.0 / math.sqrt(3.0 * BLEN / 8.0)
    parts = np.stack([np.cos(angle) * scale, -np.sin(angle) * scale], axis=1)
    hann = 0.5 - 0.5 * np.cos(2.0 * math.pi / BLEN * t)
    return (
        jnp.asarray(parts.reshape(2 * HOP, BLEN), jnp.bfloat16),
        jnp.asarray(parts.swapaxes(0, 1).reshape(2 * HOP, BLEN), jnp.bfloat16),
        jnp.asarray(np.repeat(hann[:, None], 128, axis=1), jnp.float32),
    )


def split_kernel(pressure_ref, out_ref):
    width = out_ref.shape[2]
    for quarter in range(BLOCKS):
        x = pressure_ref[:, quarter * width : (quarter + 1) * width]
        mean = jnp.sum(x, axis=0, keepdims=True) * (1.0 / HOP)
        out_ref[quarter, :HOP] = (x - mean).astype(jnp.bfloat16)
        high = mean.astype(jnp.bfloat16).astype(jnp.float32)
        middle = (mean - high).astype(jnp.bfloat16).astype(jnp.float32)
        low = mean - high - middle
        row = lax.broadcasted_iota(jnp.int32, (MEANS, width), 0)
        rows = jnp.where(row == 0, high, jnp.where(row == 1, middle, jnp.where(row == 2, low, 0.0)))
        out_ref[quarter, HOP:] = rows.astype(jnp.bfloat16)


def spectra_kernel(
    count, pos_ref, got_ref, final_ref, weights_ref, table_ref, split_ref, hann_ref,
    piece0, piece1, piece2, piece3, csd_ref, rotated, coeff, sums,
):
    me = pos_ref[0]
    width = got_ref.shape[2]
    own = pl.ds(pl.multiple_of(me * width, width), width)
    group = 2 * HOP // BLOCKS
    for step in range(BLOCKS):
        rows = pl.multiple_of(lax.rem(me + step, BLOCKS) * group, group)
        rotated[step * group : (step + 1) * group] = table_ref[pl.ds(rows, group), :]

    final = final_ref[:, own]
    means = [
        jnp.sum(got_ref[s, HOP:].astype(jnp.float32), axis=0, keepdims=True) for s in range(BLOCKS)
    ]
    total = jnp.sum(final, axis=0, keepdims=True) + HOP * (means[0] + means[1] + means[2] + means[3])
    mean = total / (HOP * (BLOCKS + 1))
    hann = jnp.concatenate([hann_ref[...]] * (width // 128), axis=1)

    def segment(s):
        if s == BLOCKS:
            return final - mean
        return got_ref[s, :HOP].astype(jnp.float32) + (means[s] - mean)

    for b in range(BLOCKS):
        windowed = jnp.concatenate([segment(b) * hann[:HOP], segment(b + 1) * hann[HOP:]], axis=0)
        windowed = windowed.astype(jnp.bfloat16)
        mixed = jnp.dot(rotated[...], windowed, preferred_element_type=jnp.float32)
        mixed = mixed.astype(jnp.bfloat16)
        for step, piece in enumerate((piece0, piece1, piece2, piece3)):
            piece[b] = mixed[step * group : (step + 1) * group]
        apart = jnp.dot(split_ref[...], windowed, preferred_element_type=jnp.float32)
        coeff[b] = apart.astype(jnp.bfloat16).astype(jnp.float32)

    weights = weights_ref[:, own] * (1.0 / count)
    freqs = HOP // BLOCKS

    def tile(t, carry):
        at = pl.multiple_of(t * 8, 8)
        acc = [None] * SUMS
        for lane in range(0, width, 128):
            cols = slice(lane, lane + 128)
            w = weights[:, cols]
            re = [coeff[b, pl.ds(at, 8), cols] for b in range(BLOCKS)]
            im = [coeff[b, pl.ds(at + HOP, 8), cols] for b in range(BLOCKS)]
            re_w = [v * w for v in re]
            im_w = [v * w for v in im]
            terms = [re_w[i] * re[j] + im_w[i] * im[j] for i, j in PAIRS]
            terms += [im_w[i] * re[j] - re_w[i] * im[j] for i, j in CROSS]
            acc = [v if a is None else a + v for a, v in zip(acc, terms)]
        first = (t // (freqs // 8)) * (SUMS * freqs) + lax.rem(t, freqs // 8) * 8
        for p in range(SUMS):
            sums[pl.ds(pl.multiple_of(first + p * freqs, 8), 8), :] = acc[p]
        return carry

    lax.fori_loop(0, HOP // 8, tile, 0)
    values = sums[...]
    high = values.astype(jnp.bfloat16)
    low = (values - high.astype(jnp.float32)).astype(jnp.bfloat16)
    ones = jnp.ones((8, 128), jnp.bfloat16)
    along = (((1,), (1,)), ((), ()))
    lanes = lax.dot_general(ones, high, along, preferred_element_type=jnp.float32)
    lanes += lax.dot_general(ones, low, along, preferred_element_type=jnp.float32)
    part = SUMS * freqs
    for q in range(BLOCKS):
        csd_ref[q * 8 : (q + 1) * 8] = lanes[:, q * part : (q + 1) * part]


def join_kernel(pos_ref, piece0, piece1, piece2, piece3, out_ref):
    me = pos_ref[0]
    width = piece0.shape[2]
    for step, piece in enumerate((piece0, piece1, piece2, piece3)):
        source = lax.rem(me + BLOCKS - step, BLOCKS)
        out_ref[:, :, pl.ds(pl.multiple_of(source * width, width), width)] = piece[...]


def summed_over(value, axes):
    size = lax.axis_size(axes)
    sent = jnp.broadcast_to(value[None], (size, *value.shape))
    return jnp.sum(lax.all_to_all(sent, axes, 0, 0, tiled=True), axis=0)


def local(pressure, final_steps, weights):
    points = pressure.shape[1]
    width = points // BLOCKS
    freqs = HOP // BLOCKS
    position = lax.axis_index("blk").astype(jnp.int32).reshape(1)
    params = pltpu.CompilerParams(vmem_limit_bytes=LIMIT)
    sent = pl.pallas_call(
        split_kernel,
        out_shape=jax.ShapeDtypeStruct((BLOCKS, HOP + MEANS, width), jnp.bfloat16),
        in_specs=[VMEM],
        out_specs=VMEM,
        compiler_params=params,
    )(pressure)
    got = lax.all_to_all(sent, "blk", 0, 0, tiled=True)
    table, split, hann = tables()
    count = float(points * lax.axis_size(SPACE))
    piece = jax.ShapeDtypeStruct((BLOCKS, 2 * freqs, width), jnp.bfloat16)
    group = lax.axis_size(("blk", "x", "core"))
    *pieces, partial_sums = pl.pallas_call(
        lambda *refs: spectra_kernel(count, *refs),
        out_shape=[piece] * BLOCKS + [jax.ShapeDtypeStruct((8 * BLOCKS, SUMS * freqs), jnp.float32)],
        in_specs=[SMEM] + [VMEM] * 6,
        out_specs=[VMEM] * 5,
        scratch_shapes=[
            pltpu.VMEM((2 * HOP, BLEN), jnp.bfloat16),
            pltpu.VMEM((BLOCKS, 2 * HOP, width), jnp.float32),
            pltpu.VMEM((SUMS * HOP, 128), jnp.float32),
        ],
        compiler_params=params,
    )(position, got, final_steps, weights.reshape(1, points), table, split, hann)
    partial_sums = partial_sums.reshape(BLOCKS, 8, -1)[:, : group // BLOCKS].reshape(group, -1)
    partial_sums = jnp.sum(
        lax.all_to_all(partial_sums, ("blk", "x", "core"), 0, 0, tiled=True), axis=0
    )
    moved = [
        lax.ppermute(value, "blk", [(i, (i + step) % BLOCKS) for i in range(BLOCKS)]) if step else value
        for step, value in enumerate(pieces)
    ]
    spectra = pl.pallas_call(
        join_kernel,
        out_shape=jax.ShapeDtypeStruct((BLOCKS, 2 * freqs, points), jnp.bfloat16),
        in_specs=[SMEM] + [VMEM] * BLOCKS,
        out_specs=VMEM,
        compiler_params=params,
    )(position, *moved)
    spectra = spectra.reshape(BLOCKS, freqs, 2, points)
    rows = summed_over(partial_sums, ("z",)).reshape(SUMS, freqs)
    zero = jnp.zeros_like(rows[0])
    both = []
    for i in range(BLOCKS):
        both += [rows[PAIRS.index((min(i, j), max(i, j)))] for j in range(BLOCKS)]
    for i in range(BLOCKS):
        for j in range(BLOCKS):
            at = len(PAIRS) + (CROSS.index((min(i, j), max(i, j))) if i != j else 0)
            both.append(zero if i == j else rows[at] if i < j else -rows[at])
    csd = jnp.stack(both).reshape(2, BLOCKS, BLOCKS, freqs)
    return (spectra, jnp.transpose(csd, (0, 3, 1, 2)))


def solution(mesh):
    across = min(4, mesh.shape["space"] // 2)
    split = Mesh(mesh.devices.reshape(-1, across, 2, mesh.shape["blk"]), (*SPACE, "blk"))
    return jax.shard_map(
        local,
        mesh=split,
        in_specs=(P("blk", SPACE), P(None, SPACE), P(SPACE)),
        out_specs=(P(None, "blk", None, SPACE), P(None, "blk", None, None)),
        check_vma=False,
    )
```

time: 107 us -> 69.3 us (0.65)
  blocking collectives: 40.4 us -> 16.5 us
  waiting for transfers between devices: 27.3 us -> 14.3 us
  matrix products: 12.6 us -> 0 us
  starting transfers between devices: 16.3 us -> 28.3 us
  other arithmetic: 3.56 us -> 0.18 us
  Pallas kernels: 0 us -> 2.89 us
    ppermute x1 -> x3, waiting for transfers between devices: 17.8 us -> 4.31 us  [local(): lax.ppermute(value, 'blk', [(i, (i + step) % BLOCKS) for i in range(BLOCK...]
    psum x1 -> x0, blocking collectives: 13.1 us -> none  [local(): total = lax.psum(own_sum, 'blk')]
    dot_general x5 -> x0, matrix products: 12.6 us -> none  [the longest x1 2.8 us: cross_sums(): jnp.einsum('ikn,jkn->kij', real_w, imag_part, precision=high)]
    all_to_all x2 -> x1, blocking collectives: 27.3 us -> 16.5 us  [local(): lax.all_to_all(partial_sums, ('blk', 'x', 'core'), 0, 0, tiled=True)]
    ppermute x1 -> x3, starting transfers between devices: 1.42 us -> 8.76 us  [local(): lax.ppermute(value, 'blk', [(i, (i + step) % BLOCKS) for i in range(BLOCK...]
    all_to_all x0 -> x1, waiting for transfers between devices: none -> 7.28 us  [local(): got = lax.all_to_all(sent, 'blk', 0, 0, tiled=True)]
    all_to_all x1, waiting for transfers between devices: 9.52 us -> 2.69 us  [summed_over(): return jnp.sum(lax.all_to_all(sent, axes, 0, 0, tiled=True), axis=0)]
    all_to_all x0 -> x1, starting transfers between devices: none -> 5.14 us  [local(): got = lax.all_to_all(sent, 'blk', 0, 0, tiled=True)]
  transfers between devices with their start and end apart: 2 -> 5, of which waited for: 2 -> 4; matrix products, arithmetic and copies ran while one was open for 4% -> 4% of each run, Pallas kernels for 0% -> 0%
where the time goes in v2:
time: 69.3 us; the launch traced here: 68.9 us
  starting transfers between devices  28.3 us (41%)
  blocking collectives  16.5 us (24%)
  waiting for transfers between devices  14.3 us (21%)
  local copies, waits for them, and re-layouts  5.98 us (9%)
  Pallas kernels  2.89 us (4%)
  between operations  0.71 us (1%)
    all_to_all x1, blocking collectives, local(): lax.all_to_all(partial_sums, ('blk', 'x', 'core'), 0, 0, tiled=True)  16.5 us
    all_to_all x1, starting transfers between devices, summed_over(): return jnp.sum(lax.all_to_all(sent, axes, 0, 0, tiled=True), axis=0)  14.4 us
    ppermute x3, starting transfers between devices, local(): lax.ppermute(value, 'blk', [(i, (i + step) % BLOCKS) for i in range(BLOCK...  8.76 us
    all_to_all x1, waiting for transfers between devices, local(): got = lax.all_to_all(sent, 'blk', 0, 0, tiled=True)  7.28 us
    all_to_all x1, starting transfers between devices, local(): got = lax.all_to_all(sent, 'blk', 0, 0, tiled=True)  5.14 us
    ppermute x3, waiting for transfers between devices, local(): lax.ppermute(value, 'blk', [(i, (i + step) % BLOCKS) for i in range(BLOCK...  4.31 us
    all_to_all x1, waiting for transfers between devices, summed_over(): return jnp.sum(lax.all_to_all(sent, axes, 0, 0, tiled=True), axis=0)  2.69 us
    another operation x1, local copies, waits for them, and re-layouts, local(): csd = jnp.stack(both).reshape(2, BLOCKS, BLOCKS, freqs)  2.44 us
  transfers between devices with their start and end apart: 5, of which 4 were waited for; matrix products, arithmetic and copies ran while one was open for 4% of the time, Pallas kernels for 0%

profile of v2, /device:TPU:1, one launch (start us, length us, event | category | flops | bytes accessed | tf_op | source)
XLA Modules:
  0.0 68.9 jit_solution(9034012368525885543)
XLA Ops:
  0.6 0.0 copy-start
  0.6 1.2 %copy-done = f32[128,2048]{1,0:T(8,128)S(1)} copy-done((f32[128,2048]{1,0:T(8,128)S(1)}, f32[128,2048]{1,0:T(8,128)}, u32[]{:S(2)}) %copy-start) | copy-done | bytes 1048600
  1.9 0.0 copy-start.1
  1.9 1.0 %shard_map.77 = bf16[4,144,512]{2,1,0:T(8,128)(2,1)} custom-call(f32[128,2048]{1,0:T(8,128)S(1)} %copy-done), custom_call_target="tpu_custom_call" | custom-call | tf_op jit(solution)/shard_map/pallas_call | solution.py:143
  2.8 0.0 copy-start.2
  2.8 0.0 copy-start.3
  2.8 0.0 copy-start.4
  2.8 5.1 %all-to-all-start = ((bf16[4,144,512]{2,1,0:T(8,128)(2,1)}), bf16[4,144,512]{2,1,0:T(8,128)(2,1)S(1)}, u32[]{:S(2)}, u32[]{:S(2)}) async-start(bf16[4,144,512]{2,1,0:T(8,128)(2,1)} %shard_map.77), calls=%async_computation | async-start | bytes 1179648 | tf_op jit(solution)/shard_map/all_to_all | solution.py:150
  8.0 0.0 copy-start.5
  8.0 7.3 %all-to-all-done.refs_1_ = bf16[4,144,512]{2,1,0:T(8,128)(2,1)S(1)} async-done(((bf16[4,144,512]{2,1,0:T(8,128)(2,1)}), bf16[4,144,512]{2,1,0:T(8,128)(2,1)S(1)}, u32[]{:S(2)}, u32[]{:S(2)}) %all-to-all-start) | async-done | bytes 589856 | tf_op jit(solution)/shard_map/all_to_all | solution.py:150
  15.3 0.0 copy-done.1
  15.3 0.0 copy-done.2
  15.3 0.0 copy-done.3
  15.3 0.0 copy-done.4
  15.3 0.0 copy-done.5
  15.3 1.9 %shard_map.78 = (bf16[4,64,512]{2,1,0:T(8,128)(2,1)S(1)}, bf16[4,64,512]{2,1,0:T(8,128)(2,1)S(1)}, bf16[4,64,512]{2,1,0:T(8,128)(2,1)S(1)}, bf16[4,64,512]{2,1,0:T(8,128)(2,1)S(1)}, f32[32,512]{1,0:T(8,128)S(1)}) custom-call(s32[1]{0:T(128)} %bitcast.refs_0_.pos_ref, bf16[4,144,512]{2,1,0:T(8,128)(2,1)S(1)} %all-to-all-done.refs_1_, ...), custom_call_target="tpu_custom_call" | custom-call | tf_op jit(solution)/shard_map/pallas_call | solution.py:155
  17.1 0.1 copy.10
  17.2 16.5 %all_to_all.20 = f32[32,1,512]{2,1,0:T(1,128)S(1)} all-to-all(f32[32,1,512]{2,1,0:T(1,128)S(1)} %copy.10), channel_id=1, replica_groups=mesh['z'=16,'x'=4,'core'=2,'blk'=4] {'blk','x','core'}, dimensions={0} | all-to-all | bytes 131072 | tf_op jit(solution)/shard_map/all_to_all | solution.py:169
  33.7 0.1 reduce_sum.18
  33.8 0.6 broadcast_in_dim.2
  34.5 14.4 %all-to-all-start.2 = ((f32[16,1,512]{2,1,0:T(1,128)}), f32[16,1,512]{2,1,0:T(1,128)S(1)}, u32[]{:S(2)}, u32[]{:S(2)}) async-start(f32[16,1,512]{2,1,0:T(1,128)} %broadcast_in_dim.2), calls=%async_computation.2 | async-start | bytes 65536 | tf_op jit(solution)/shard_map/all_to_all | solution.py:134
  48.9 2.2 %collective-permute-start = (bf16[4,64,512]{2,1,0:T(8,128)(2,1)S(1)}, bf16[4,64,512]{2,1,0:T(8,128)(2,1)S(1)}, u32[]{:S(2)}, u32[]{:S(2)}) collective-permute-start(bf16[4,64,512]{2,1,0:T(8,128)(2,1)S(1)} %get-tuple-element.8), channel_id=1, source_target_pairs={{0,1},{1,2},{2,3},{3,0},{4,5},{5,6},{6,7},{7,4},{8,9},{9,10},{10,1... | collective-permute-start | bytes 786440 | tf_op jit(solution)/shard_map/ppermute | solution.py:172
  51.1 3.6 %collective-permute-start.1 = (bf16[4,64,512]{2,1,0:T(8,128)(2,1)S(1)}, bf16[4,64,512]{2,1,0:T(8,128)(2,1)S(1)}, u32[]{:S(2)}, u32[]{:S(2)}) collective-permute-start(bf16[4,64,512]{2,1,0:T(8,128)(2,1)S(1)} %get-tuple-element.9), channel_id=1, source_target_pairs={{0,2},{1,3},{2,0},{3,1},{4,6},{5,7},{6,4},{7,5},{8,10},{9,11},{10,... | collective-permute-start | bytes 786440 | tf_op jit(solution)/shard_map/ppermute | solution.py:172
  54.8 2.9 %collective-permute-start.2 = (bf16[4,64,512]{2,1,0:T(8,128)(2,1)S(1)}, bf16[4,64,512]{2,1,0:T(8,128)(2,1)S(1)}, u32[]{:S(2)}, u32[]{:S(2)}) collective-permute-start(bf16[4,64,512]{2,1,0:T(8,128)(2,1)S(1)} %get-tuple-element.10), channel_id=1, source_target_pairs={{0,3},{1,0},{2,1},{3,2},{4,7},{5,4},{6,5},{7,6},{8,11},{9,8},{10,9... | collective-permute-start | bytes 786440 | tf_op jit(solution)/shard_map/ppermute | solution.py:172
  57.7 2.7 %all-to-all-done.2 = f32[16,1,512]{2,1,0:T(1,128)S(1)} async-done(((f32[16,1,512]{2,1,0:T(1,128)}), f32[16,1,512]{2,1,0:T(1,128)S(1)}, u32[]{:S(2)}, u32[]{:S(2)}) %all-to-all-start.2) | async-done | bytes 32800 | tf_op jit(solution)/shard_map/all_to_all | solution.py:134
  60.4 0.1 slice_bitcast_fusion.7
  60.5 0.1 negate_bitcast_fusion
  60.6 2.4 %stack.2 = f32[32,32]{1,0:T(8,128)} concatenate(f32[1,32]{1,0:T(1,128)S(1)} %get-tuple-element.33, f32[1,32]{1,0:T(1,128)S(1)} %get-tuple-element.32, f32[1,32]{1,0:T(1,128)S(1)} %get-tuple-element.31, f32[1,32]{1,0:T(1,128)S(1)} %get-tuple-element.30, f32[1,32]{1,0:T(1,128)S(1)} %get-tuple-element.32, f32[1,32]{1,0:T(1,128)S(1)} %get-tuple-element.29, ...), dimensions={0} | concatenate | bytes 8192 | tf_op jit(solution)/shard_map/stack | solution.py:192
  63.0 0.0 collective-permute-done.piece1
  63.0 1.2 %collective-permute-done.1.piece2 = bf16[4,64,512]{2,1,0:T(8,128)(2,1)S(1)} collective-permute-done((bf16[4,64,512]{2,1,0:T(8,128)(2,1)S(1)}, bf16[4,64,512]{2,1,0:T(8,128)(2,1)S(1)}, u32[]{:S(2)}, u32[]{:S(2)}) %collective-permute-start.1) | collective-permute-done | bytes 262176 | tf_op jit(solution)/shard_map/ppermute | solution.py:172
  64.2 3.1 %collective-permute-done.2.piece3 = bf16[4,64,512]{2,1,0:T(8,128)(2,1)S(1)} collective-permute-done((bf16[4,64,512]{2,1,0:T(8,128)(2,1)S(1)}, bf16[4,64,512]{2,1,0:T(8,128)(2,1)S(1)}, u32[]{:S(2)}, u32[]{:S(2)}) %collective-permute-start.2) | collective-permute-done | bytes 262176 | tf_op jit(solution)/shard_map/ppermute | solution.py:172
  67.3 0.1 shard_map.79
  67.4 1.5 %reshape.61 = bf16[4,32,2,2048]{3,2,1,0:T(2,128)(2,1)} reshape(bf16[4,64,2048]{2,1,0:T(8,128)(2,1)S(1)} %shard_map.79) | data formatting | bytes 2097152 | tf_op jit(solution)/shard_map/reshape | solution.py:182
  (2 shorter events, 0.0 us)
Async XLA Ops:
  0.6 1.2 %copy-start = (f32[128,2048]{1,0:T(8,128)S(1)}, f32[128,2048]{1,0:T(8,128)}, u32[]{:S(2)}) copy-start(f32[128,2048]{1,0:T(8,128)} %pressure_ref.1) | copy-start | bytes 3145732
  1.9 13.4 %copy-start.1 = (f32[128,2048]{1,0:T(8,128)S(1)}, f32[128,2048]{1,0:T(8,128)}, u32[]{:S(2)}) copy-start(f32[128,2048]{1,0:T(8,128)} %refs_2_.1) | copy-start | bytes 3145732
  2.8 12.4 %copy-start.2 = (f32[256,128]{1,0:T(8,128)S(1)}, f32[256,128]{1,0:T(8,128)}, u32[]{:S(2)}) copy-start(f32[256,128]{1,0:T(8,128)} %constant.15.clone.refs_6_) | copy-start | bytes 393220
  2.8 12.4 %copy-start.3 = (bf16[256,256]{1,0:T(8,128)(2,1)S(1)}, bf16[256,256]{1,0:T(8,128)(2,1)}, u32[]{:S(2)}) copy-start(bf16[256,256]{1,0:T(8,128)(2,1)} %constant.14.clone.refs_5_) | copy-start | bytes 393220
  2.8 12.4 %copy-start.4 = (bf16[256,256]{1,0:T(8,128)(2,1)S(1)}, bf16[256,256]{1,0:T(8,128)(2,1)}, u32[]{:S(2)}) copy-start(bf16[256,256]{1,0:T(8,128)(2,1)} %constant.4.clone.refs_4_) | copy-start | bytes 393220
  2.8 12.4 %all-to-all-start = ((bf16[4,144,512]{2,1,0:T(8,128)(2,1)}), bf16[4,144,512]{2,1,0:T(8,128)(2,1)S(1)}, u32[]{:S(2)}, u32[]{:S(2)}) async-start(bf16[4,144,512]{2,1,0:T(8,128)(2,1)} %shard_map.77), calls=%async_computation | async-start | bytes 1179648 | tf_op jit(solution)/shard_map/all_to_all | solution.py:150
  8.0 7.3 %copy-start.5 = (f32[2048]{0:T(1024)S(1)}, f32[2048]{0:T(1024)}, u32[]{:S(2)}) copy-start(f32[2048]{0:T(1024)} %param.8) | copy-start | bytes 24580
  34.5 25.9 %all-to-all-start.2 = ((f32[16,1,512]{2,1,0:T(1,128)}), f32[16,1,512]{2,1,0:T(1,128)S(1)}, u32[]{:S(2)}, u32[]{:S(2)}) async-start(f32[16,1,512]{2,1,0:T(1,128)} %broadcast_in_dim.2), calls=%async_computation.2 | async-start | bytes 65536 | tf_op jit(solution)/shard_map/all_to_all | solution.py:134
  48.9 14.1 %collective-permute-start = (bf16[4,64,512]{2,1,0:T(8,128)(2,1)S(1)}, bf16[4,64,512]{2,1,0:T(8,128)(2,1)S(1)}, u32[]{:S(2)}, u32[]{:S(2)}) collective-permute-start(bf16[4,64,512]{2,1,0:T(8,128)(2,1)S(1)} %get-tuple-element.8), channel_id=1, source_target_pairs={{0,1},{1,2},{2,3},{3,0},{4,5},{5,6},{6,7},{7,4},{8,9},{9,10},{10,1... | collective-permute-start | bytes 786440 | tf_op jit(solution)/shard_map/ppermute | solution.py:172
  51.1 13.1 %collective-permute-start.1 = (bf16[4,64,512]{2,1,0:T(8,128)(2,1)S(1)}, bf16[4,64,512]{2,1,0:T(8,128)(2,1)S(1)}, u32[]{:S(2)}, u32[]{:S(2)}) collective-permute-start(bf16[4,64,512]{2,1,0:T(8,128)(2,1)S(1)} %get-tuple-element.9), channel_id=1, source_target_pairs={{0,2},{1,3},{2,0},{3,1},{4,6},{5,7},{6,4},{7,5},{8,10},{9,11},{10,... | collective-permute-start | bytes 786440 | tf_op jit(solution)/shard_map/ppermute | solution.py:172
  54.8 12.5 %collective-permute-start.2 = (bf16[4,64,512]{2,1,0:T(8,128)(2,1)S(1)}, bf16[4,64,512]{2,1,0:T(8,128)(2,1)S(1)}, u32[]{:S(2)}, u32[]{:S(2)}) collective-permute-start(bf16[4,64,512]{2,1,0:T(8,128)(2,1)S(1)} %get-tuple-element.10), channel_id=1, source_target_pairs={{0,3},{1,0},{2,1},{3,2},{4,7},{5,4},{6,5},{7,6},{8,11},{9,8},{10,9... | collective-permute-start | bytes 786440 | tf_op jit(solution)/shard_map/ppermute | solution.py:172

commit v3 on v2

v3 whole, which is shorter than its diff:
```python
import functools
import math

import jax
import jax.numpy as jnp
import numpy as np
from jax import lax
from jax.experimental import pallas as pl
from jax.experimental.pallas import tpu as pltpu
from jax.sharding import Mesh
from jax.sharding import PartitionSpec as P

HOP = 128
BLEN = 2 * HOP
BLOCKS = 4
SPACE = ("z", "x", "core")
LIMIT = 48 * 1024 * 1024
WAIT = pl.CostEstimate(flops=10**10, bytes_accessed=10**10, transcendentals=0)
MEANS = 16
PAIRS = [(i, j) for i in range(BLOCKS) for j in range(i, BLOCKS)]
CROSS = [(i, j) for i, j in PAIRS if i < j]
SUMS = len(PAIRS) + len(CROSS)

VMEM = pl.BlockSpec(memory_space=pltpu.VMEM)
SMEM = pl.BlockSpec(memory_space=pltpu.SMEM)
HBM = pl.BlockSpec(memory_space=pltpu.HBM)


def tables():
    t = np.arange(BLEN)
    k = np.arange(HOP)
    angle = 2.0 * math.pi / BLEN * (k[:, None] * t[None, :] % BLEN)
    scale = 1.0 / math.sqrt(3.0 * BLEN / 8.0)
    parts = np.stack([np.cos(angle) * scale, -np.sin(angle) * scale], axis=1)
    hann = 0.5 - 0.5 * np.cos(2.0 * math.pi / BLEN * t)
    return (
        jnp.asarray(parts.reshape(2 * HOP, BLEN), jnp.bfloat16),
        jnp.asarray(parts.swapaxes(0, 1).reshape(2 * HOP, BLEN), jnp.bfloat16),
        jnp.asarray(np.repeat(hann[:, None], 128, axis=1), jnp.float32),
    )


def split_kernel(pressure_ref, out_ref, held, ready, sem_in, sem_out):
    width = out_ref.shape[2]

    def fetch(quarter):
        cols = slice(quarter * width, (quarter + 1) * width)
        return pltpu.make_async_copy(pressure_ref.at[:, cols], held.at[quarter], sem_in.at[quarter])

    def store(quarter):
        return pltpu.make_async_copy(ready.at[quarter], out_ref.at[quarter], sem_out.at[quarter])

    for quarter in range(BLOCKS):
        fetch(quarter).start()
    for quarter in range(BLOCKS):
        fetch(quarter).wait()
        x = held[quarter]
        mean = jnp.sum(x, axis=0, keepdims=True) * (1.0 / HOP)
        ready[quarter, :HOP] = (x - mean).astype(jnp.bfloat16)
        high = mean.astype(jnp.bfloat16).astype(jnp.float32)
        middle = (mean - high).astype(jnp.bfloat16).astype(jnp.float32)
        low = mean - high - middle
        row = lax.broadcasted_iota(jnp.int32, (MEANS, width), 0)
        rows = jnp.where(row == 0, high, jnp.where(row == 1, middle, jnp.where(row == 2, low, 0.0)))
        ready[quarter, HOP:] = rows.astype(jnp.bfloat16)
        store(quarter).start()
    for quarter in range(BLOCKS):
        store(quarter).wait()


def sums_kernel(
    count, pos_ref, got_ref, final_ref, weights_ref, table_ref, hann_ref, windowed_ref, csd_ref, coeff, sums
):
    me = pos_ref[0]
    width = got_ref.shape[2]
    own = pl.ds(pl.multiple_of(me * width, width), width)
    final = final_ref[:, own]
    means = [
        jnp.sum(got_ref[s, HOP:].astype(jnp.float32), axis=0, keepdims=True) for s in range(BLOCKS)
    ]
    total = jnp.sum(final, axis=0, keepdims=True) + HOP * (means[0] + means[1] + means[2] + means[3])
    mean = total / (HOP * (BLOCKS + 1))
    hann = jnp.concatenate([hann_ref[...]] * (width // 128), axis=1)

    def segment(s):
        if s == BLOCKS:
            return final - mean
        return got_ref[s, :HOP].astype(jnp.float32) + (means[s] - mean)

    for b in range(BLOCKS):
        windowed = jnp.concatenate([segment(b) * hann[:HOP], segment(b + 1) * hann[HOP:]], axis=0)
        windowed = windowed.astype(jnp.bfloat16)
        windowed_ref[b] = windowed
        apart = jnp.dot(table_ref[...], windowed, preferred_element_type=jnp.float32)
        coeff[b] = apart.astype(jnp.bfloat16).astype(jnp.float32)

    weights = weights_ref[:, own] * (1.0 / count)
    freqs = HOP // BLOCKS

    def tile(t, carry):
        at = pl.multiple_of(t * 8, 8)
        acc = [None] * SUMS
        for lane in range(0, width, 128):
            cols = slice(lane, lane + 128)
            w = weights[:, cols]
            re = [coeff[b, pl.ds(at, 8), cols] for b in range(BLOCKS)]
            im = [coeff[b, pl.ds(at + HOP, 8), cols] for b in range(BLOCKS)]
            re_w = [v * w for v in re]
            im_w = [v * w for v in im]
            terms = [re_w[i] * re[j] + im_w[i] * im[j] for i, j in PAIRS]
            terms += [im_w[i] * re[j] - re_w[i] * im[j] for i, j in CROSS]
            acc = [v if a is None else a + v for a, v in zip(acc, terms)]
        first = (t // (freqs // 8)) * (SUMS * freqs) + lax.rem(t, freqs // 8) * 8
        for p in range(SUMS):
            sums[pl.ds(pl.multiple_of(first + p * freqs, 8), 8), :] = acc[p]
        return carry

    lax.fori_loop(0, HOP // 8, tile, 0)
    values = sums[...]
    high = values.astype(jnp.bfloat16)
    low = (values - high.astype(jnp.float32)).astype(jnp.bfloat16)
    ones = jnp.ones((8, 128), jnp.bfloat16)
    along = (((1,), (1,)), ((), ()))
    lanes = lax.dot_general(ones, high, along, preferred_element_type=jnp.float32)
    lanes += lax.dot_general(ones, low, along, preferred_element_type=jnp.float32)
    part = SUMS * freqs
    copies = csd_ref.shape[0] // BLOCKS
    for q in range(BLOCKS):
        for copy in range(copies):
            csd_ref[q * copies + copy] = lanes[:1, q * part : (q + 1) * part]


def spectra_kernel(pos_ref, windowed_ref, table_ref, piece0, piece1, piece2, piece3, rotated):
    me = pos_ref[0]
    group = 2 * HOP // BLOCKS
    for step in range(BLOCKS):
        rows = pl.multiple_of(lax.rem(me + step, BLOCKS) * group, group)
        rotated[step * group : (step + 1) * group] = table_ref[pl.ds(rows, group), :]
    for b in range(BLOCKS):
        mixed = jnp.dot(rotated[...], windowed_ref[b], preferred_element_type=jnp.float32)
        mixed = mixed.astype(jnp.bfloat16)
        for step, piece in enumerate((piece0, piece1, piece2, piece3)):
            piece[b] = mixed[step * group : (step + 1) * group]


def repeat_kernel(got_ref, out_ref):
    value = jnp.sum(got_ref[...], axis=0)
    for copy in range(out_ref.shape[0]):
        out_ref[copy] = value


def join_kernel(pos_ref, piece0, piece1, piece2, piece3, out_ref):
    me = pos_ref[0]
    width = piece0.shape[2]
    for step, piece in enumerate((piece0, piece1, piece2, piece3)):
        source = lax.rem(me + BLOCKS - step, BLOCKS)
        out_ref[:, :, pl.ds(pl.multiple_of(source * width, width), width)] = piece[...]


def matrix_kernel(got_ref, spectra_ref, csd_ref):
    freqs = csd_ref.shape[2]
    total = jnp.sum(got_ref[...], axis=0)
    rows = [total[:, p * freqs : (p + 1) * freqs] for p in range(SUMS)]
    for i in range(BLOCKS):
        for j in range(BLOCKS):
            pair = (min(i, j), max(i, j))
            csd_ref[i, j : j + 1] = rows[PAIRS.index(pair)]
            if i == j:
                csd_ref[BLOCKS + i, j : j + 1] = jnp.zeros_like(total[:, :freqs])
            else:
                cross = rows[len(PAIRS) + CROSS.index(pair)]
                csd_ref[BLOCKS + i, j : j + 1] = cross if i < j else -cross


def call(kernel, out, operands, scratch=(), cost=None):
    specs = [o[1] if isinstance(o, tuple) else VMEM for o in operands]
    return pl.pallas_call(
        kernel,
        out_shape=out,
        in_specs=specs,
        out_specs=jax.tree.map(lambda _: VMEM, out),
        scratch_shapes=scratch,
        compiler_params=pltpu.CompilerParams(vmem_limit_bytes=LIMIT),
        cost_estimate=cost,
    )(*[o[0] if isinstance(o, tuple) else o for o in operands])


def local(pressure, final_steps, weights):
    points = pressure.shape[1]
    width = points // BLOCKS
    freqs = HOP // BLOCKS
    here = (lax.axis_index("blk").astype(jnp.int32).reshape(1), SMEM)
    table, apart, hann = tables()
    sent = pl.pallas_call(
        split_kernel,
        out_shape=jax.ShapeDtypeStruct((BLOCKS, HOP + MEANS, width), jnp.bfloat16),
        in_specs=[HBM],
        out_specs=HBM,
        scratch_shapes=[
            pltpu.VMEM((BLOCKS, HOP, width), jnp.float32),
            pltpu.VMEM((BLOCKS, HOP + MEANS, width), jnp.bfloat16),
            pltpu.SemaphoreType.DMA((BLOCKS,)),
            pltpu.SemaphoreType.DMA((BLOCKS,)),
        ],
        compiler_params=pltpu.CompilerParams(vmem_limit_bytes=60 * 1024 * 1024),
    )(pressure)
    got = lax.all_to_all(sent, "blk", 0, 0, tiled=True)

    group = ("blk", "x", "core")
    count = float(points * lax.axis_size(SPACE))
    windowed, sums = call(
        functools.partial(sums_kernel, count),
        [
            jax.ShapeDtypeStruct((BLOCKS, BLEN, width), jnp.bfloat16),
            jax.ShapeDtypeStruct((lax.axis_size(group), 1, SUMS * freqs), jnp.float32),
        ],
        [here, got, final_steps, weights.reshape(1, points), apart, hann],
        [pltpu.VMEM((BLOCKS, 2 * HOP, width), jnp.float32), pltpu.VMEM((SUMS * HOP, 128), jnp.float32)],
    )
    sums = lax.all_to_all(sums, group, 0, 0, tiled=True)
    piece = jax.ShapeDtypeStruct((BLOCKS, 2 * freqs, width), jnp.bfloat16)
    pieces = call(
        spectra_kernel, [piece] * BLOCKS, [here, windowed, table], [pltpu.VMEM((2 * HOP, BLEN), jnp.bfloat16)]
    )
    moved = [
        lax.ppermute(value, "blk", [(i, (i + step) % BLOCKS) for i in range(BLOCKS)]) if step else value
        for step, value in enumerate(pieces)
    ]
    repeated = jax.ShapeDtypeStruct((lax.axis_size("z"), 1, SUMS * freqs), jnp.float32)
    sums = lax.all_to_all(call(repeat_kernel, repeated, [sums], cost=WAIT), "z", 0, 0, tiled=True)
    spectra = call(
        join_kernel, jax.ShapeDtypeStruct((BLOCKS, 2 * freqs, points), jnp.bfloat16), [here, *moved]
    ).reshape(BLOCKS, freqs, 2, points)
    csd = call(
        matrix_kernel, jax.ShapeDtypeStruct((2 * BLOCKS, BLOCKS, freqs), jnp.float32), [sums, (spectra, HBM)]
    )
    csd = csd.reshape(2, BLOCKS, BLOCKS, freqs)
    return (spectra, jnp.transpose(csd, (0, 3, 1, 2)))


def solution(mesh):
    across = min(4, mesh.shape["space"] // 2)
    split = Mesh(mesh.devices.reshape(-1, across, 2, mesh.shape["blk"]), (*SPACE, "blk"))
    return jax.shard_map(
        local,
        mesh=split,
        in_specs=(P("blk", SPACE), P(None, SPACE), P(SPACE)),
        out_specs=(P(None, "blk", None, SPACE), P(None, "blk", None, None)),
        check_vma=False,
    )
```

time: 69.3 us -> 67 us (0.967)
  the two profiles are of different devices: /device:TPU:1 before, /device:TPU:2 now
where the time goes in v3:
time: 67 us; the launch traced here: 66.6 us
  starting transfers between devices  36.9 us (55%)
  waiting for transfers between devices  22 us (33%)
  Pallas kernels  6.23 us (9%)
  between operations  0.79 us (1%)
  local copies, waits for them, and re-layouts  0.75 us (1%)
    all_to_all x1, starting transfers between devices, local(): lax.all_to_all(call(repeat_kernel, repeated, [sums], cost=WAIT), 'z', 0,...  14 us
    all_to_all x1, waiting for transfers between devices, local(): lax.all_to_all(call(repeat_kernel, repeated, [sums], cost=WAIT), 'z', 0,...  11.8 us
    ppermute x3, starting transfers between devices, local(): lax.ppermute(value, 'blk', [(i, (i + step) % BLOCKS) for i in range(BLOCK...  11.4 us
    all_to_all x1, waiting for transfers between devices, local(): got = lax.all_to_all(sent, 'blk', 0, 0, tiled=True)  10.2 us
    all_to_all x1, starting transfers between devices, local(): sums = lax.all_to_all(sums, group, 0, 0, tiled=True)  6.79 us
    all_to_all x1, starting transfers between devices, local(): got = lax.all_to_all(sent, 'blk', 0, 0, tiled=True)  4.61 us
    pallas_call x5, Pallas kernels, call(): pl.pallas_call(kernel, out_shape=out, in_specs=specs, out_specs=jax.tree....  4.18 us
    pallas_call x1, Pallas kernels, local(): pl.pallas_call(split_kernel, out_shape=jax.ShapeDtypeStruct((BLOCKS, HOP...  2.06 us
  transfers between devices with their start and end apart: 6, of which 2 were waited for; matrix products, arithmetic and copies ran while one was open for 1% of the time, Pallas kernels for 2%

profile of v3, /device:TPU:2, one launch (start us, length us, event | category | flops | bytes accessed | tf_op | source)
XLA Modules:
  0.0 66.6 jit_solution(4188673449051674674)
XLA Ops:
  0.6 0.0 copy-start.1
  0.6 2.1 %shard_map.77 = bf16[4,144,512]{2,1,0:T(8,128)(2,1)} custom-call(f32[128,2048]{1,0:T(8,128)} %pressure_ref.1), custom_call_target="tpu_custom_call" | custom-call | tf_op jit(solution)/shard_map/pallas_call | solution.py:194
  2.7 0.0 copy-start.3
  2.7 0.0 copy-start.4
  2.7 4.6 %all-to-all-start = ((bf16[4,144,512]{2,1,0:T(8,128)(2,1)}), bf16[4,144,512]{2,1,0:T(8,128)(2,1)S(1)}, u32[]{:S(2)}, u32[]{:S(2)}) async-start(bf16[4,144,512]{2,1,0:T(8,128)(2,1)} %shard_map.77), calls=%async_computation | async-start | bytes 1179648 | tf_op jit(solution)/shard_map/all_to_all | solution.py:207
  7.3 0.0 copy-start.5
  7.3 10.2 %all-to-all-done.got_ref = bf16[4,144,512]{2,1,0:T(8,128)(2,1)S(1)} async-done(((bf16[4,144,512]{2,1,0:T(8,128)(2,1)}), bf16[4,144,512]{2,1,0:T(8,128)(2,1)S(1)}, u32[]{:S(2)}, u32[]{:S(2)}) %all-to-all-start) | async-done | bytes 589856 | tf_op jit(solution)/shard_map/all_to_all | solution.py:207
  17.5 0.0 copy-done.1
  17.5 0.0 copy-done.3
  17.5 0.0 copy-done.4
  17.5 0.0 copy-done.5
  17.5 2.3 %shard_map.78 = (bf16[4,256,512]{2,1,0:T(8,128)(2,1)S(1)}, f32[32,1,512]{2,1,0:T(1,128)}) custom-call(s32[1]{0:T(128)} %bitcast.pos_ref, bf16[4,144,512]{2,1,0:T(8,128)(2,1)S(1)} %all-to-all-done.got_ref, f32[128,2048]{1,0:T(8,128)S(1)} %copy-done.1, f32[1,2048]{1,0:T(1,128)S(1)} %bitcast.5, bf16[256,256]{1,0:T(8,128)(2,1)S(1)} %copy-done.4, ...), custom_call_target="tpu_custom_call" | custom-call | tf_op jit(solution)/shard_map/pallas_call | solution.py:177
  19.8 0.0 copy-start.2
  19.8 6.8 %all-to-all-start.1 = ((f32[32,1,512]{2,1,0:T(1,128)}), f32[32,1,512]{2,1,0:T(1,128)S(1)}, u32[]{:S(2)}, u32[]{:S(2)}) async-start(f32[32,1,512]{2,1,0:T(1,128)} %get-tuple-element.13), calls=%async_computation.1 | async-start | bytes 131072 | tf_op jit(solution)/shard_map/all_to_all | solution.py:220
  26.6 0.0 copy-done.2
  26.6 0.4 shard_map.79
  27.1 3.4 %collective-permute-start = (bf16[4,64,512]{2,1,0:T(8,128)(2,1)S(1)}, bf16[4,64,512]{2,1,0:T(8,128)(2,1)S(1)}, u32[]{:S(2)}, u32[]{:S(2)}) collective-permute-start(bf16[4,64,512]{2,1,0:T(8,128)(2,1)S(1)} %get-tuple-element.10), channel_id=1, source_target_pairs={{0,1},{1,2},{2,3},{3,0},{4,5},{5,6},{6,7},{7,4},{8,9},{9,10},{10,1... | collective-permute-start | bytes 786440 | tf_op jit(solution)/shard_map/ppermute | solution.py:226
  30.5 4.7 %collective-permute-start.1 = (bf16[4,64,512]{2,1,0:T(8,128)(2,1)S(1)}, bf16[4,64,512]{2,1,0:T(8,128)(2,1)S(1)}, u32[]{:S(2)}, u32[]{:S(2)}) collective-permute-start(bf16[4,64,512]{2,1,0:T(8,128)(2,1)S(1)} %get-tuple-element.11), channel_id=1, source_target_pairs={{0,2},{1,3},{2,0},{3,1},{4,6},{5,7},{6,4},{7,5},{8,10},{9,11},{10,... | collective-permute-start | bytes 786440 | tf_op jit(solution)/shard_map/ppermute | solution.py:226
  35.2 3.3 %collective-permute-start.2 = (bf16[4,64,512]{2,1,0:T(8,128)(2,1)S(1)}, bf16[4,64,512]{2,1,0:T(8,128)(2,1)S(1)}, u32[]{:S(2)}, u32[]{:S(2)}) collective-permute-start(bf16[4,64,512]{2,1,0:T(8,128)(2,1)S(1)} %get-tuple-element.12), channel_id=1, source_target_pairs={{0,3},{1,0},{2,1},{3,2},{4,7},{5,4},{6,5},{7,6},{8,11},{9,8},{10,9... | collective-permute-start | bytes 786440 | tf_op jit(solution)/shard_map/ppermute | solution.py:226
  38.5 0.0 all-to-all-done.1.got_ref
  38.5 0.7 shard_map.81
  39.2 14.0 %all-to-all-start.2 = ((f32[16,1,512]{2,1,0:T(1,128)}), f32[16,1,512]{2,1,0:T(1,128)S(1)}, u32[]{:S(2)}, u32[]{:S(2)}) async-start(f32[16,1,512]{2,1,0:T(1,128)} %shard_map.81), calls=%async_computation.2 | async-start | bytes 65536 | tf_op jit(solution)/shard_map/all_to_all | solution.py:230
  53.2 0.0 collective-permute-done.piece1
  53.2 0.0 collective-permute-done.1.piece2
  53.3 0.0 collective-permute-done.2.piece3
  53.3 0.1 shard_map.80
  53.4 0.7 %reshape.18.spectra_ref = bf16[4,32,2,2048]{3,2,1,0:T(2,128)(2,1)S(1)} reshape(bf16[4,64,2048]{2,1,0:T(8,128)(2,1)S(1)} %shard_map.80) | data formatting | bytes 2097152 | tf_op jit(solution)/shard_map/reshape | solution.py:233
  54.1 0.0 copy-start
  54.1 11.8 %all-to-all-done.2.got_ref = f32[16,1,512]{2,1,0:T(1,128)S(1)} async-done(((f32[16,1,512]{2,1,0:T(1,128)}), f32[16,1,512]{2,1,0:T(1,128)S(1)}, u32[]{:S(2)}, u32[]{:S(2)}) %all-to-all-start.2) | async-done | bytes 32800 | tf_op jit(solution)/shard_map/all_to_all | solution.py:230
  65.9 0.7 %shard_map.82 = f32[8,4,32]{2,1,0:T(4,128)} custom-call(f32[16,1,512]{2,1,0:T(1,128)S(1)} %all-to-all-done.2.got_ref, bf16[4,32,2,2048]{3,2,1,0:T(2,128)(2,1)S(1)} %reshape.18.spectra_ref), custom_call_target="tpu_custom_call" | custom-call | tf_op jit(solution)/shard_map/pallas_call | solution.py:177
  66.6 0.0 copy-done
Async XLA Ops:
  0.6 16.9 %copy-start.1 = (f32[128,2048]{1,0:T(8,128)S(1)}, f32[128,2048]{1,0:T(8,128)}, u32[]{:S(2)}) copy-start(f32[128,2048]{1,0:T(8,128)} %final_ref.1) | copy-start | bytes 3145732
  2.7 14.8 %copy-start.3 = (f32[256,128]{1,0:T(8,128)S(1)}, f32[256,128]{1,0:T(8,128)}, u32[]{:S(2)}) copy-start(f32[256,128]{1,0:T(8,128)} %constant.12.clone.hann_ref) | copy-start | bytes 393220
  2.7 14.8 %copy-start.4 = (bf16[256,256]{1,0:T(8,128)(2,1)S(1)}, bf16[256,256]{1,0:T(8,128)(2,1)}, u32[]{:S(2)}) copy-start(bf16[256,256]{1,0:T(8,128)(2,1)} %constant.11.clone.table_ref) | copy-start | bytes 393220
  2.7 14.8 %all-to-all-start = ((bf16[4,144,512]{2,1,0:T(8,128)(2,1)}), bf16[4,144,512]{2,1,0:T(8,128)(2,1)S(1)}, u32[]{:S(2)}, u32[]{:S(2)}) async-start(bf16[4,144,512]{2,1,0:T(8,128)(2,1)} %shard_map.77), calls=%async_computation | async-start | bytes 1179648 | tf_op jit(solution)/shard_map/all_to_all | solution.py:207
  7.3 10.2 %copy-start.5 = (f32[2048]{0:T(1024)S(1)}, f32[2048]{0:T(1024)}, u32[]{:S(2)}) copy-start(f32[2048]{0:T(1024)} %param.8) | copy-start | bytes 24580
  19.8 6.8 %copy-start.2 = (bf16[256,256]{1,0:T(8,128)(2,1)S(1)}, bf16[256,256]{1,0:T(8,128)(2,1)}, u32[]{:S(2)}) copy-start(bf16[256,256]{1,0:T(8,128)(2,1)} %constant.10.clone.table_ref) | copy-start | bytes 393220
  19.8 18.7 %all-to-all-start.1 = ((f32[32,1,512]{2,1,0:T(1,128)}), f32[32,1,512]{2,1,0:T(1,128)S(1)}, u32[]{:S(2)}, u32[]{:S(2)}) async-start(f32[32,1,512]{2,1,0:T(1,128)} %get-tuple-element.13), calls=%async_computation.1 | async-start | bytes 131072 | tf_op jit(solution)/shard_map/all_to_all | solution.py:220
  27.1 26.2 %collective-permute-start = (bf16[4,64,512]{2,1,0:T(8,128)(2,1)S(1)}, bf16[4,64,512]{2,1,0:T(8,128)(2,1)S(1)}, u32[]{:S(2)}, u32[]{:S(2)}) collective-permute-start(bf16[4,64,512]{2,1,0:T(8,128)(2,1)S(1)} %get-tuple-element.10), channel_id=1, source_target_pairs={{0,1},{1,2},{2,3},{3,0},{4,5},{5,6},{6,7},{7,4},{8,9},{9,10},{10,1... | collective-permute-start | bytes 786440 | tf_op jit(solution)/shard_map/ppermute | solution.py:226
  30.5 22.7 %collective-permute-start.1 = (bf16[4,64,512]{2,1,0:T(8,128)(2,1)S(1)}, bf16[4,64,512]{2,1,0:T(8,128)(2,1)S(1)}, u32[]{:S(2)}, u32[]{:S(2)}) collective-permute-start(bf16[4,64,512]{2,1,0:T(8,128)(2,1)S(1)} %get-tuple-element.11), channel_id=1, source_target_pairs={{0,2},{1,3},{2,0},{3,1},{4,6},{5,7},{6,4},{7,5},{8,10},{9,11},{10,... | collective-permute-start | bytes 786440 | tf_op jit(solution)/shard_map/ppermute | solution.py:226
  35.2 18.1 %collective-permute-start.2 = (bf16[4,64,512]{2,1,0:T(8,128)(2,1)S(1)}, bf16[4,64,512]{2,1,0:T(8,128)(2,1)S(1)}, u32[]{:S(2)}, u32[]{:S(2)}) collective-permute-start(bf16[4,64,512]{2,1,0:T(8,128)(2,1)S(1)} %get-tuple-element.12), channel_id=1, source_target_pairs={{0,3},{1,0},{2,1},{3,2},{4,7},{5,4},{6,5},{7,6},{8,11},{9,8},{10,9... | collective-permute-start | bytes 786440 | tf_op jit(solution)/shard_map/ppermute | solution.py:226
  39.2 26.7 %all-to-all-start.2 = ((f32[16,1,512]{2,1,0:T(1,128)}), f32[16,1,512]{2,1,0:T(1,128)S(1)}, u32[]{:S(2)}, u32[]{:S(2)}) async-start(f32[16,1,512]{2,1,0:T(1,128)} %shard_map.81), calls=%async_computation.2 | async-start | bytes 65536 | tf_op jit(solution)/shard_map/all_to_all | solution.py:230
  54.1 12.5 %copy-start = (bf16[4,32,2,2048]{3,2,1,0:T(2,128)(2,1)}, bf16[4,32,2,2048]{3,2,1,0:T(2,128)(2,1)S(1)}, u32[]{:S(2)}) copy-start(bf16[4,32,2,2048]{3,2,1,0:T(2,128)(2,1)S(1)} %reshape.18.spectra_ref) | copy-start | bytes 3145732

commit v4 on v3

--- a/solution.py
+++ b/solution.py
@@ -14,7 +14,7 @@
 BLEN = 2 * HOP
 BLOCKS = 4
 SPACE = ("z", "x", "core")
-LIMIT = 48 * 1024 * 1024
+LIMIT = 16 * 1024 * 1024
 WAIT = pl.CostEstimate(flops=10**10, bytes_accessed=10**10, transcendentals=0)
 MEANS = 16
 PAIRS = [(i, j) for i in range(BLOCKS) for j in range(i, BLOCKS)]
@@ -24,6 +24,7 @@
 VMEM = pl.BlockSpec(memory_space=pltpu.VMEM)
 SMEM = pl.BlockSpec(memory_space=pltpu.SMEM)
 HBM = pl.BlockSpec(memory_space=pltpu.HBM)
+ANY = pl.BlockSpec(memory_space=pl.ANY)
 
 
 def tables():
@@ -68,29 +69,32 @@
         store(quarter).wait()
 
 
+def windows(segments, final, hann_ref):
+    means = [jnp.sum(ref[HOP:].astype(jnp.float32), axis=0, keepdims=True) for ref in segments]
+    total = jnp.sum(final, axis=0, keepdims=True) + HOP * (means[0] + means[1] + means[2] + means[3])
+    mean = total / (HOP * (BLOCKS + 1))
+    hann = jnp.concatenate([hann_ref[...]] * (final.shape[1] // 128), axis=1)
+
+    def segment(s):
+        if s == BLOCKS:
+            return final - mean
+        return segments[s][:HOP].astype(jnp.float32) + (means[s] - mean)
+
+    blocks = []
+    for b in range(BLOCKS):
+        windowed = jnp.concatenate([segment(b) * hann[:HOP], segment(b + 1) * hann[HOP:]], axis=0)
+        blocks.append(windowed.astype(jnp.bfloat16))
+    return blocks
+
+
 def sums_kernel(
-    count, pos_ref, got_ref, final_ref, weights_ref, table_ref, hann_ref, windowed_ref, csd_ref, coeff, sums
+    count, pos_ref, got_ref, final_ref, weights_ref, table_ref, hann_ref, out_ref, coeff, sums, rows
 ):
     me = pos_ref[0]
     width = got_ref.shape[2]
     own = pl.ds(pl.multiple_of(me * width, width), width)
-    final = final_ref[:, own]
-    means = [
-        jnp.sum(got_ref[s, HOP:].astype(jnp.float32), axis=0, keepdims=True) for s in range(BLOCKS)
-    ]
-    total = jnp.sum(final, axis=0, keepdims=True) + HOP * (means[0] + means[1] + means[2] + means[3])
-    mean = total / (HOP * (BLOCKS + 1))
-    hann = jnp.concatenate([hann_ref[...]] * (width // 128), axis=1)
-
-    def segment(s):
-        if s == BLOCKS:
-            return final - mean
-        return got_ref[s, :HOP].astype(jnp.float32) + (means[s] - mean)
-
-    for b in range(BLOCKS):
-        windowed = jnp.concatenate([segment(b) * hann[:HOP], segment(b + 1) * hann[HOP:]], axis=0)
-        windowed = windowed.astype(jnp.bfloat16)
-        windowed_ref[b] = windowed
+    segments = [got_ref.at[s] for s in range(BLOCKS)]
+    for b, windowed in enumerate(windows(segments, final_ref[:, own], hann_ref)):
         apart = jnp.dot(table_ref[...], windowed, preferred_element_type=jnp.float32)
         coeff[b] = apart.astype(jnp.bfloat16).astype(jnp.float32)
 
@@ -123,66 +127,113 @@
     along = (((1,), (1,)), ((), ()))
     lanes = lax.dot_general(ones, high, along, preferred_element_type=jnp.float32)
     lanes += lax.dot_general(ones, low, along, preferred_element_type=jnp.float32)
-    part = SUMS * freqs
-    copies = csd_ref.shape[0] // BLOCKS
+    for row in range(rows.shape[0]):
+        rows[row : row + 1] = lanes[:1, row * 128 : (row + 1) * 128]
+    value = rows[...].astype(jnp.bfloat16)
+    for copy in range(out_ref.shape[0]):
+        out_ref[copy] = value
+
+
+def fan_kernel(pos_ref, sent_ref, out1, out2, out3, sems):
+    me = pos_ref[0]
+    copies = []
+    for step, out in enumerate((out1, out2, out3), 1):
+        for place in range(BLOCKS - 1):
+            quarter = lax.rem(me + step + 1 + place, BLOCKS)
+            sem = sems.at[step - 1, place]
+            copies.append(pltpu.make_async_copy(sent_ref.at[quarter], out.at[place], sem))
+    for copy in copies:
+        copy.start()
+    for copy in copies:
+        copy.wait()
+
+
+def spectra_kernel(
+    pos_ref, final_ref, table_ref, hann_ref, sent_ref, got_ref, got1, got2, got3, out_ref, held, last, ready, sems, last_sems, out_sems
+):
+    me = pos_ref[0]
+    width = sent_ref.shape[2]
+    own = BLOCKS - 1
+
+    def cols(place):
+        return pl.ds(pl.multiple_of(lax.rem(me + 1 + place, BLOCKS) * width, width), width)
+
+    fetches = []
+    for place in range(BLOCKS):
+        copies = [pltpu.make_async_copy(final_ref.at[:, cols(place)], last.at[place], last_sems.at[place])]
+        if place == own:
+            copies.append(pltpu.make_async_copy(got_ref, held.at[place], sems.at[place, 0]))
+        else:
+            mine = sent_ref.at[lax.rem(me + 1 + place, BLOCKS)]
+            copies.append(pltpu.make_async_copy(mine, held.at[place, me], sems.at[place, 0]))
+            for step, got in enumerate((got1, got2, got3), 1):
+                source = lax.rem(me + BLOCKS - step, BLOCKS)
+                copies.append(
+                    pltpu.make_async_copy(got.at[place], held.at[place, source], sems.at[place, step])
+                )
+        fetches.append(copies)
+    stores = [
+        pltpu.make_async_copy(ready.at[place], out_ref.at[:, :, cols(place)], out_sems.at[place])
+        for place in range(BLOCKS)
+    ]
+    order = [own, *range(own)]
+    for place in order:
+        for copy in fetches[place]:
+            copy.start()
+    group = 2 * HOP // BLOCKS
+    table = table_ref[pl.ds(pl.multiple_of(me * group, group), group), :]
+    for place in order:
+        for copy in fetches[place]:
+            copy.wait()
+        blocks = windows([held.at[place, s] for s in range(BLOCKS)], last[place], hann_ref)
+        for b, windowed in enumerate(blocks):
+            mixed = jnp.dot(table, windowed, preferred_element_type=jnp.float32)
+            ready[place, b] = mixed.astype(jnp.bfloat16)
+        stores[place].start()
+    for place in order:
+        stores[place].wait()
+
+
+def share_kernel(got_ref, out_ref):
+    total = jnp.sum(got_ref[...].astype(jnp.float32), axis=0)
+    part = total.shape[0] // BLOCKS
+    copies = out_ref.shape[0] // BLOCKS
     for q in range(BLOCKS):
         for copy in range(copies):
-            csd_ref[q * copies + copy] = lanes[:1, q * part : (q + 1) * part]
-
-
-def spectra_kernel(pos_ref, windowed_ref, table_ref, piece0, piece1, piece2, piece3, rotated):
-    me = pos_ref[0]
-    group = 2 * HOP // BLOCKS
-    for step in range(BLOCKS):
-        rows = pl.multiple_of(lax.rem(me + step, BLOCKS) * group, group)
-        rotated[step * group : (step + 1) * group] = table_ref[pl.ds(rows, group), :]
-    for b in range(BLOCKS):
-        mixed = jnp.dot(rotated[...], windowed_ref[b], preferred_element_type=jnp.float32)
-        mixed = mixed.astype(jnp.bfloat16)
-        for step, piece in enumerate((piece0, piece1, piece2, piece3)):
-            piece[b] = mixed[step * group : (step + 1) * group]
-
-
-def repeat_kernel(got_ref, out_ref):
-    value = jnp.sum(got_ref[...], axis=0)
-    for copy in range(out_ref.shape[0]):
-        out_ref[copy] = value
-
-
-def join_kernel(pos_ref, piece0, piece1, piece2, piece3, out_ref):
-    me = pos_ref[0]
-    width = piece0.shape[2]
-    for step, piece in enumerate((piece0, piece1, piece2, piece3)):
-        source = lax.rem(me + BLOCKS - step, BLOCKS)
-        out_ref[:, :, pl.ds(pl.multiple_of(source * width, width), width)] = piece[...]
+            out_ref[q * copies + copy] = total[q * part : (q + 1) * part]
 
 
 def matrix_kernel(got_ref, spectra_ref, csd_ref):
     freqs = csd_ref.shape[2]
     total = jnp.sum(got_ref[...], axis=0)
-    rows = [total[:, p * freqs : (p + 1) * freqs] for p in range(SUMS)]
+    each = 128 // freqs
+    rows = [total[p // each : p // each + 1, p % each * freqs : (p % each + 1) * freqs] for p in range(SUMS)]
     for i in range(BLOCKS):
         for j in range(BLOCKS):
             pair = (min(i, j), max(i, j))
             csd_ref[i, j : j + 1] = rows[PAIRS.index(pair)]
             if i == j:
-                csd_ref[BLOCKS + i, j : j + 1] = jnp.zeros_like(total[:, :freqs])
+                csd_ref[BLOCKS + i, j : j + 1] = jnp.zeros_like(rows[0])
             else:
                 cross = rows[len(PAIRS) + CROSS.index(pair)]
                 csd_ref[BLOCKS + i, j : j + 1] = cross if i < j else -cross
 
 
-def call(kernel, out, operands, scratch=(), cost=None):
+def call(kernel, out, operands, scratch=(), cost=None, out_spec=VMEM, limit=LIMIT):
     specs = [o[1] if isinstance(o, tuple) else VMEM for o in operands]
     return pl.pallas_call(
         kernel,
         out_shape=out,
         in_specs=specs,
-        out_specs=jax.tree.map(lambda _: VMEM, out),
+        out_specs=jax.tree.map(lambda _: out_spec, out),
         scratch_shapes=scratch,
-        compiler_params=pltpu.CompilerParams(vmem_limit_bytes=LIMIT),
+        compiler_params=pltpu.CompilerParams(vmem_limit_bytes=limit),
         cost_estimate=cost,
     )(*[o[0] if isinstance(o, tuple) else o for o in operands])
+
+
+def late_first(size):
+    return [(i + size // 2 + 1) % size for i in range(size)]
 
 
 def local(pressure, final_steps, weights):
@@ -205,35 +256,48 @@
         compiler_params=pltpu.CompilerParams(vmem_limit_bytes=60 * 1024 * 1024),
     )(pressure)
     got = lax.all_to_all(sent, "blk", 0, 0, tiled=True)
+    part = jax.ShapeDtypeStruct((BLOCKS - 1, HOP + MEANS, width), jnp.bfloat16)
+    parts = call(
+        fan_kernel, [part] * 3, [here, (sent, ANY)], [pltpu.SemaphoreType.DMA((3, BLOCKS - 1))], out_spec=HBM
+    )
+    moved = [
+        lax.ppermute(value, "blk", [(i, (i + step) % BLOCKS) for i in range(BLOCKS)])
+        for step, value in enumerate(parts, 1)
+    ]
 
     group = ("blk", "x", "core")
     count = float(points * lax.axis_size(SPACE))
-    windowed, sums = call(
+    lines = SUMS * HOP // 128
+    sums = call(
         functools.partial(sums_kernel, count),
+        jax.ShapeDtypeStruct((lax.axis_size("z"), lines, 128), jnp.bfloat16),
+        [here, got, final_steps, weights.reshape(1, points), apart, hann],
         [
-            jax.ShapeDtypeStruct((BLOCKS, BLEN, width), jnp.bfloat16),
-            jax.ShapeDtypeStruct((lax.axis_size(group), 1, SUMS * freqs), jnp.float32),
+            pltpu.VMEM((BLOCKS, 2 * HOP, width), jnp.float32),
+            pltpu.VMEM((SUMS * HOP, 128), jnp.float32),
+            pltpu.VMEM((lines, 128), jnp.float32),
         ],
-        [here, got, final_steps, weights.reshape(1, points), apart, hann],
-        [pltpu.VMEM((BLOCKS, 2 * HOP, width), jnp.float32), pltpu.VMEM((SUMS * HOP, 128), jnp.float32)],
+        cost=WAIT,
     )
-    sums = lax.all_to_all(sums, group, 0, 0, tiled=True)
-    piece = jax.ShapeDtypeStruct((BLOCKS, 2 * freqs, width), jnp.bfloat16)
-    pieces = call(
-        spectra_kernel, [piece] * BLOCKS, [here, windowed, table], [pltpu.VMEM((2 * HOP, BLEN), jnp.bfloat16)]
-    )
-    moved = [
-        lax.ppermute(value, "blk", [(i, (i + step) % BLOCKS) for i in range(BLOCKS)]) if step else value
-        for step, value in enumerate(pieces)
-    ]
-    repeated = jax.ShapeDtypeStruct((lax.axis_size("z"), 1, SUMS * freqs), jnp.float32)
-    sums = lax.all_to_all(call(repeat_kernel, repeated, [sums], cost=WAIT), "z", 0, 0, tiled=True)
+    sums = lax.all_to_all(sums, "z", 0, 0, tiled=True, axis_index_groups=[late_first(lax.axis_size("z"))])
     spectra = call(
-        join_kernel, jax.ShapeDtypeStruct((BLOCKS, 2 * freqs, points), jnp.bfloat16), [here, *moved]
+        spectra_kernel,
+        jax.ShapeDtypeStruct((BLOCKS, 2 * freqs, points), jnp.bfloat16),
+        [here, (final_steps, ANY), table, hann, (sent, ANY), (got, ANY), *((value, ANY) for value in moved)],
+        [
+            pltpu.VMEM((BLOCKS, BLOCKS, HOP + MEANS, width), jnp.bfloat16),
+            pltpu.VMEM((BLOCKS, HOP, width), jnp.float32),
+            pltpu.VMEM((BLOCKS, BLOCKS, 2 * freqs, width), jnp.bfloat16),
+            pltpu.SemaphoreType.DMA((BLOCKS, BLOCKS)),
+            pltpu.SemaphoreType.DMA((BLOCKS,)),
+            pltpu.SemaphoreType.DMA((BLOCKS,)),
+        ],
+        out_spec=ANY,
+        limit=60 * 1024 * 1024,
     ).reshape(BLOCKS, freqs, 2, points)
-    csd = call(
-        matrix_kernel, jax.ShapeDtypeStruct((2 * BLOCKS, BLOCKS, freqs), jnp.float32), [sums, (spectra, HBM)]
-    )
+    shares = jax.ShapeDtypeStruct((lax.axis_size(group), lines // BLOCKS, 128), jnp.float32)
+    sums = lax.all_to_all(call(share_kernel, shares, [sums]), group, 0, 0, tiled=True)
+    csd = call(matrix_kernel, jax.ShapeDtypeStruct((2 * BLOCKS, BLOCKS, freqs), jnp.float32), [sums, (spectra, ANY)])
     csd = csd.reshape(2, BLOCKS, BLOCKS, freqs)
     return (spectra, jnp.transpose(csd, (0, 3, 1, 2)))
 

time: 67 us -> 59.9 us (0.89)
  the two profiles are of different devices: /device:TPU:2 before, /device:TPU:1 now
where the time goes in v4:
time: 59.9 us; the launch traced here: 59.5 us
  starting transfers between devices  23.6 us (39%)
  blocking collectives  21.2 us (35%)
  Pallas kernels  11.2 us (19%)
  local copies, waits for them, and re-layouts  2.64 us (4%)
  between operations  0.83 us (1%)
    all_to_all x1, blocking collectives, local(): lax.all_to_all(sums, 'z', 0, 0, tiled=True, axis_index_groups=[late_first...  21.2 us
    ppermute x3, starting transfers between devices, local(): lax.ppermute(value, 'blk', [(i, (i + step) % BLOCKS) for i in range(BLOCK...  10.8 us
    pallas_call x5, Pallas kernels, call(): pl.pallas_call(kernel, out_shape=out, in_specs=specs, out_specs=jax.tree....  9.26 us
    all_to_all x1, starting transfers between devices, local(): lax.all_to_all(call(share_kernel, shares, [sums]), group, 0, 0, tiled=True)  7.66 us
    all_to_all x1, starting transfers between devices, local(): got = lax.all_to_all(sent, 'blk', 0, 0, tiled=True)  5.16 us
    pallas_call x1, Pallas kernels, local(): pl.pallas_call(split_kernel, out_shape=jax.ShapeDtypeStruct((BLOCKS, HOP...  1.99 us
    reshape x1, local copies, waits for them, and re-layouts, local(): spectra = call(spectra_kernel, jax.ShapeDtypeStruct((BLOCKS, 2 * freqs, p...  1.75 us
  transfers between devices with their start and end apart: 5, of which 0 were waited for; matrix products, arithmetic and copies ran while one was open for 3% of the time, Pallas kernels for 14%

profile of v4, /device:TPU:1, one launch (start us, length us, event | category | flops | bytes accessed | tf_op | source)
XLA Modules:
  0.0 59.5 jit_solution(4628746821991865666)
XLA Ops:
  0.6 0.0 copy-start.6
  0.6 2.0 %shard_map.77.sent_ref = bf16[4,144,512]{2,1,0:T(8,128)(2,1)} custom-call(f32[128,2048]{1,0:T(8,128)} %pressure_ref.1), custom_call_target="tpu_custom_call" | custom-call | tf_op jit(solution)/shard_map/pallas_call | solution.py:245
  2.6 0.0 copy-start
  2.6 0.0 copy-start.3
  2.7 5.2 %all-to-all-start = ((bf16[4,144,512]{2,1,0:T(8,128)(2,1)}), bf16[4,144,512]{2,1,0:T(8,128)(2,1)S(1)}, u32[]{:S(2)}, u32[]{:S(2)}) async-start(bf16[4,144,512]{2,1,0:T(8,128)(2,1)} %shard_map.77.sent_ref), calls=%async_computation | async-start | bytes 1179648 | tf_op jit(solution)/shard_map/all_to_all | solution.py:258
  7.8 0.0 copy-done
  7.8 0.0 copy-start.4
  7.8 0.0 copy-start.5
  7.8 1.2 %shard_map.78 = (bf16[3,144,512]{2,1,0:T(8,128)(2,1)}, bf16[3,144,512]{2,1,0:T(8,128)(2,1)S(1)}, bf16[3,144,512]{2,1,0:T(8,128)(2,1)S(1)}) custom-call(s32[1]{0:T(128)} %bitcast.pos_ref, bf16[4,144,512]{2,1,0:T(8,128)(2,1)S(1)} %copy-done), custom_call_target="tpu_custom_call" | custom-call | tf_op jit(solution)/shard_map/pallas_call | solution.py:224
  9.1 3.4 %collective-permute-start = (bf16[3,144,512]{2,1,0:T(8,128)(2,1)}, bf16[3,144,512]{2,1,0:T(8,128)(2,1)S(1)}, u32[]{:S(2)}, u32[]{:S(2)}) collective-permute-start(bf16[3,144,512]{2,1,0:T(8,128)(2,1)} %get-tuple-element.5), channel_id=1, source_target_pairs={{0,1},{1,2},{2,3},{3,0},{4,5},{5,6},{6,7},{7,4},{8,9},{9,10},{10,1... | collective-permute-start | bytes 1327112 | tf_op jit(solution)/shard_map/ppermute | solution.py:264
  12.5 4.3 %collective-permute-start.1 = (bf16[3,144,512]{2,1,0:T(8,128)(2,1)S(1)}, bf16[3,144,512]{2,1,0:T(8,128)(2,1)}, u32[]{:S(2)}, u32[]{:S(2)}) collective-permute-start(bf16[3,144,512]{2,1,0:T(8,128)(2,1)S(1)} %get-tuple-element.6), channel_id=1, source_target_pairs={{0,2},{1,3},{2,0},{3,1},{4,6},{5,7},{6,4},{7,5},{8,10},{9,11},{10,... | collective-permute-start | bytes 1327112 | tf_op jit(solution)/shard_map/ppermute | solution.py:264
  16.8 3.1 %collective-permute-start.2 = (bf16[3,144,512]{2,1,0:T(8,128)(2,1)S(1)}, bf16[3,144,512]{2,1,0:T(8,128)(2,1)}, u32[]{:S(2)}, u32[]{:S(2)}) collective-permute-start(bf16[3,144,512]{2,1,0:T(8,128)(2,1)S(1)} %get-tuple-element.7), channel_id=1, source_target_pairs={{0,3},{1,0},{2,1},{3,2},{4,7},{5,4},{6,5},{7,6},{8,11},{9,8},{10,9... | collective-permute-start | bytes 1327112 | tf_op jit(solution)/shard_map/ppermute | solution.py:264
  19.9 0.0 all-to-all-done.got_ref
  19.9 0.0 copy-start.2
  19.9 0.0 copy-done.6
  19.9 0.0 copy-done.3
  19.9 0.0 copy-done.4
  19.9 0.0 copy-done.5
  19.9 1.6 %shard_map.80 = bf16[16,16,128]{2,1,0:T(8,128)(2,1)S(1)} custom-call(s32[1]{0:T(128)} %bitcast.pos_ref, bf16[4,144,512]{2,1,0:T(8,128)(2,1)S(1)} %all-to-all-done.got_ref, f32[128,2048]{1,0:T(8,128)S(1)} %copy-done.3, f32[1,2048]{1,0:T(1,128)S(1)} %bitcast.5, bf16[256,256]{1,0:T(8,128)(2,1)S(1)} %copy-done.6, f32[256,128]{1,0:T(8,128)S(1)} %copy-done.4), custom_call_target="tpu_custom_call" | custom-call | flops 10000000000 | bytes 10000000000 | tf_op jit(solution)/shard_map/pallas_call | solution.py:224
  21.5 0.0 copy-done.2
  21.6 21.2 %all_to_all.15.got_ref = bf16[16,16,128]{2,1,0:T(8,128)(2,1)S(1)} all-to-all(bf16[16,16,128]{2,1,0:T(8,128)(2,1)S(1)} %shard_map.80), channel_id=1, replica_groups={{288,320,352,384,416,448,480,0,32,64,96,128,160,192,224,256},{289,321,3..., dimensions={0} | all-to-all | bytes 131072 | tf_op jit(solution)/shard_map/all_to_all | solution.py:282
  42.8 0.7 %shard_map.81 = f32[32,4,128]{2,1,0:T(4,128)} custom-call(bf16[16,16,128]{2,1,0:T(8,128)(2,1)S(1)} %all_to_all.15.got_ref), custom_call_target="tpu_custom_call" | custom-call | tf_op jit(solution)/shard_map/pallas_call | solution.py:224
  43.4 7.7 %all-to-all-start.2 = ((f32[32,4,128]{2,1,0:T(4,128)}), f32[32,4,128]{2,1,0:T(4,128)S(1)}, u32[]{:S(2)}, u32[]{:S(2)}) async-start(f32[32,4,128]{2,1,0:T(4,128)} %shard_map.81), calls=%async_computation.2 | async-start | bytes 131072 | tf_op jit(solution)/shard_map/all_to_all | solution.py:299
  51.1 0.0 collective-permute-done.got1
  51.1 0.0 copy-start.7
  51.1 0.0 collective-permute-done.1.got2
  51.1 0.0 collective-permute-done.2.got3
  51.1 0.7 %copy-done.7 = bf16[3,144,512]{2,1,0:T(8,128)(2,1)} copy-done((bf16[3,144,512]{2,1,0:T(8,128)(2,1)}, bf16[3,144,512]{2,1,0:T(8,128)(2,1)S(1)}, u32[]{:S(2)}) %copy-start.7) | copy-done | bytes 442392
  51.9 4.9 %shard_map.79 = bf16[4,64,2048]{2,1,0:T(8,128)(2,1)} custom-call(s32[1]{0:T(128)} %bitcast.pos_ref, f32[128,2048]{1,0:T(8,128)} %final_ref.3, bf16[256,256]{1,0:T(8,128)(2,1)} %constant.10.clone.table_ref, f32[256,128]{1,0:T(8,128)} %constant.12.clone.hann_ref, bf16[4,144,512]{2,1,0:T(8,128)(2,1)} %shard_map.77.sent_ref, bf16[4,144,512]{2,1,0:T(8,128)(2,1)} %copy-done.2, ...), custom_call_target="tpu_custom_call" | custom-call | tf_op jit(solution)/shard_map/pallas_call | solution.py:224
  56.8 1.7 %reshape.17.spectra_ref = bf16[4,32,2,2048]{3,2,1,0:T(2,128)(2,1)S(1)} reshape(bf16[4,64,2048]{2,1,0:T(8,128)(2,1)} %shard_map.79) | data formatting | bytes 2097152 | tf_op jit(solution)/shard_map/reshape | solution.py:297
  58.5 0.0 copy-start.1
  58.6 0.0 all-to-all-done.2.got_ref
  58.6 0.9 %shard_map.82 = f32[8,4,32]{2,1,0:T(4,128)} custom-call(f32[32,4,128]{2,1,0:T(4,128)S(1)} %all-to-all-done.2.got_ref, bf16[4,32,2,2048]{3,2,1,0:T(2,128)(2,1)S(1)} %reshape.17.spectra_ref), custom_call_target="tpu_custom_call" | custom-call | tf_op jit(solution)/shard_map/pallas_call | solution.py:224
  59.4 0.1 copy-done.1
Async XLA Ops:
  0.6 19.3 %copy-start.6 = (bf16[256,256]{1,0:T(8,128)(2,1)S(1)}, bf16[256,256]{1,0:T(8,128)(2,1)}, u32[]{:S(2)}) copy-start(bf16[256,256]{1,0:T(8,128)(2,1)} %constant.11.clone.table_ref) | copy-start | bytes 393220
  2.6 5.2 %copy-start = (bf16[4,144,512]{2,1,0:T(8,128)(2,1)S(1)}, bf16[4,144,512]{2,1,0:T(8,128)(2,1)}, u32[]{:S(2)}) copy-start(bf16[4,144,512]{2,1,0:T(8,128)(2,1)} %shard_map.77.sent_ref) | copy-start | bytes 1769476
  2.6 17.3 %copy-start.3 = (f32[128,2048]{1,0:T(8,128)S(1)}, f32[128,2048]{1,0:T(8,128)}, u32[]{:S(2)}) copy-start(f32[128,2048]{1,0:T(8,128)} %final_ref.3) | copy-start | bytes 3145732
  2.7 17.2 %all-to-all-start = ((bf16[4,144,512]{2,1,0:T(8,128)(2,1)}), bf16[4,144,512]{2,1,0:T(8,128)(2,1)S(1)}, u32[]{:S(2)}, u32[]{:S(2)}) async-start(bf16[4,144,512]{2,1,0:T(8,128)(2,1)} %shard_map.77.sent_ref), calls=%async_computation | async-start | bytes 1179648 | tf_op jit(solution)/shard_map/all_to_all | solution.py:258
  7.8 12.1 %copy-start.4 = (f32[256,128]{1,0:T(8,128)S(1)}, f32[256,128]{1,0:T(8,128)}, u32[]{:S(2)}) copy-start(f32[256,128]{1,0:T(8,128)} %constant.12.clone.hann_ref) | copy-start | bytes 393220
  7.8 12.1 %copy-start.5 = (f32[2048]{0:T(1024)S(1)}, f32[2048]{0:T(1024)}, u32[]{:S(2)}) copy-start(f32[2048]{0:T(1024)} %param.8) | copy-start | bytes 24580
  9.1 42.0 %collective-permute-start = (bf16[3,144,512]{2,1,0:T(8,128)(2,1)}, bf16[3,144,512]{2,1,0:T(8,128)(2,1)S(1)}, u32[]{:S(2)}, u32[]{:S(2)}) collective-permute-start(bf16[3,144,512]{2,1,0:T(8,128)(2,1)} %get-tuple-element.5), channel_id=1, source_target_pairs={{0,1},{1,2},{2,3},{3,0},{4,5},{5,6},{6,7},{7,4},{8,9},{9,10},{10,1... | collective-permute-start | bytes 1327112 | tf_op jit(solution)/shard_map/ppermute | solution.py:264
  12.5 38.7 %collective-permute-start.1 = (bf16[3,144,512]{2,1,0:T(8,128)(2,1)S(1)}, bf16[3,144,512]{2,1,0:T(8,128)(2,1)}, u32[]{:S(2)}, u32[]{:S(2)}) collective-permute-start(bf16[3,144,512]{2,1,0:T(8,128)(2,1)S(1)} %get-tuple-element.6), channel_id=1, source_target_pairs={{0,2},{1,3},{2,0},{3,1},{4,6},{5,7},{6,4},{7,5},{8,10},{9,11},{10,... | collective-permute-start | bytes 1327112 | tf_op jit(solution)/shard_map/ppermute | solution.py:264
  16.8 34.4 %collective-permute-start.2 = (bf16[3,144,512]{2,1,0:T(8,128)(2,1)S(1)}, bf16[3,144,512]{2,1,0:T(8,128)(2,1)}, u32[]{:S(2)}, u32[]{:S(2)}) collective-permute-start(bf16[3,144,512]{2,1,0:T(8,128)(2,1)S(1)} %get-tuple-element.7), channel_id=1, source_target_pairs={{0,3},{1,0},{2,1},{3,2},{4,7},{5,4},{6,5},{7,6},{8,11},{9,8},{10,9... | collective-permute-start | bytes 1327112 | tf_op jit(solution)/shard_map/ppermute | solution.py:264
  19.9 1.7 %copy-start.2 = (bf16[4,144,512]{2,1,0:T(8,128)(2,1)}, bf16[4,144,512]{2,1,0:T(8,128)(2,1)S(1)}, u32[]{:S(2)}) copy-start(bf16[4,144,512]{2,1,0:T(8,128)(2,1)S(1)} %all-to-all-done.got_ref) | copy-start | bytes 1769476
  43.4 15.1 %all-to-all-start.2 = ((f32[32,4,128]{2,1,0:T(4,128)}), f32[32,4,128]{2,1,0:T(4,128)S(1)}, u32[]{:S(2)}, u32[]{:S(2)}) async-start(f32[32,4,128]{2,1,0:T(4,128)} %shard_map.81), calls=%async_computation.2 | async-start | bytes 131072 | tf_op jit(solution)/shard_map/all_to_all | solution.py:299
  51.1 0.8 %copy-start.7 = (bf16[3,144,512]{2,1,0:T(8,128)(2,1)}, bf16[3,144,512]{2,1,0:T(8,128)(2,1)S(1)}, u32[]{:S(2)}) copy-start(bf16[3,144,512]{2,1,0:T(8,128)(2,1)S(1)} %collective-permute-done.got1) | copy-start | bytes 1327108
  58.5 1.0 %copy-start.1 = (bf16[4,32,2,2048]{3,2,1,0:T(2,128)(2,1)}, bf16[4,32,2,2048]{3,2,1,0:T(2,128)(2,1)S(1)}, u32[]{:S(2)}) copy-start(bf16[4,32,2,2048]{3,2,1,0:T(2,128)(2,1)S(1)} %reshape.17.spectra_ref) | copy-start | bytes 3145732

commit v5 on v4

--- a/solution.py
+++ b/solution.py
@@ -149,7 +149,7 @@
 
 
 def spectra_kernel(
-    pos_ref, final_ref, table_ref, hann_ref, sent_ref, got_ref, got1, got2, got3, out_ref, held, last, ready, sems, last_sems, out_sems
+    pos_ref, after_ref, final_ref, table_ref, hann_ref, sent_ref, got_ref, got1, got2, got3, out_ref, token_ref, held, last, ready, sems, last_sems, out_sems
 ):
     me = pos_ref[0]
     width = sent_ref.shape[2]
@@ -173,7 +173,7 @@
                 )
         fetches.append(copies)
     stores = [
-        pltpu.make_async_copy(ready.at[place], out_ref.at[:, :, cols(place)], out_sems.at[place])
+        pltpu.make_async_copy(ready.at[place], out_ref.at[:, :, :, cols(place)], out_sems.at[place])
         for place in range(BLOCKS)
     ]
     order = [own, *range(own)]
@@ -188,10 +188,15 @@
         blocks = windows([held.at[place, s] for s in range(BLOCKS)], last[place], hann_ref)
         for b, windowed in enumerate(blocks):
             mixed = jnp.dot(table, windowed, preferred_element_type=jnp.float32)
-            ready[place, b] = mixed.astype(jnp.bfloat16)
+            ready[place, b] = mixed.astype(jnp.bfloat16).reshape(ready.shape[2:])
         stores[place].start()
+    token_ref[...] = jnp.zeros_like(token_ref)
     for place in order:
         stores[place].wait()
+
+
+def token_kernel(first_ref, second_ref, token_ref):
+    token_ref[...] = jnp.zeros_like(token_ref)
 
 
 def share_kernel(got_ref, out_ref):
@@ -203,7 +208,7 @@
             out_ref[q * copies + copy] = total[q * part : (q + 1) * part]
 
 
-def matrix_kernel(got_ref, spectra_ref, csd_ref):
+def matrix_kernel(got_ref, csd_ref):
     freqs = csd_ref.shape[2]
     total = jnp.sum(got_ref[...], axis=0)
     each = 128 // freqs
@@ -225,7 +230,7 @@
         kernel,
         out_shape=out,
         in_specs=specs,
-        out_specs=jax.tree.map(lambda _: out_spec, out),
+        out_specs=out_spec,
         scratch_shapes=scratch,
         compiler_params=pltpu.CompilerParams(vmem_limit_bytes=limit),
         cost_estimate=cost,
@@ -258,7 +263,7 @@
     got = lax.all_to_all(sent, "blk", 0, 0, tiled=True)
     part = jax.ShapeDtypeStruct((BLOCKS - 1, HOP + MEANS, width), jnp.bfloat16)
     parts = call(
-        fan_kernel, [part] * 3, [here, (sent, ANY)], [pltpu.SemaphoreType.DMA((3, BLOCKS - 1))], out_spec=HBM
+        fan_kernel, [part] * 3, [here, (sent, ANY)], [pltpu.SemaphoreType.DMA((3, BLOCKS - 1))], out_spec=[HBM] * 3
     )
     moved = [
         lax.ppermute(value, "blk", [(i, (i + step) % BLOCKS) for i in range(BLOCKS)])
@@ -280,24 +285,28 @@
         cost=WAIT,
     )
     sums = lax.all_to_all(sums, "z", 0, 0, tiled=True, axis_index_groups=[late_first(lax.axis_size("z"))])
-    spectra = call(
+    token = jax.ShapeDtypeStruct((8, 128), jnp.float32)
+    after = call(
+        token_kernel, token, [(moved[0], ANY), (moved[1], ANY)], cost=WAIT, limit=60 * 1024 * 1024
+    )
+    spectra, token = call(
         spectra_kernel,
-        jax.ShapeDtypeStruct((BLOCKS, 2 * freqs, points), jnp.bfloat16),
-        [here, (final_steps, ANY), table, hann, (sent, ANY), (got, ANY), *((value, ANY) for value in moved)],
+        [jax.ShapeDtypeStruct((BLOCKS, freqs, 2, points), jnp.bfloat16), token],
+        [here, after, (final_steps, ANY), table, hann, (sent, ANY), (got, ANY), *((value, ANY) for value in moved)],
         [
             pltpu.VMEM((BLOCKS, BLOCKS, HOP + MEANS, width), jnp.bfloat16),
             pltpu.VMEM((BLOCKS, HOP, width), jnp.float32),
-            pltpu.VMEM((BLOCKS, BLOCKS, 2 * freqs, width), jnp.bfloat16),
+            pltpu.VMEM((BLOCKS, BLOCKS, freqs, 2, width), jnp.bfloat16),
             pltpu.SemaphoreType.DMA((BLOCKS, BLOCKS)),
             pltpu.SemaphoreType.DMA((BLOCKS,)),
             pltpu.SemaphoreType.DMA((BLOCKS,)),
         ],
-        out_spec=ANY,
+        out_spec=[ANY, VMEM],
         limit=60 * 1024 * 1024,
-    ).reshape(BLOCKS, freqs, 2, points)
+    )
     shares = jax.ShapeDtypeStruct((lax.axis_size(group), lines // BLOCKS, 128), jnp.float32)
     sums = lax.all_to_all(call(share_kernel, shares, [sums]), group, 0, 0, tiled=True)
-    csd = call(matrix_kernel, jax.ShapeDtypeStruct((2 * BLOCKS, BLOCKS, freqs), jnp.float32), [sums, (spectra, ANY)])
+    csd = call(matrix_kernel, jax.ShapeDtypeStruct((2 * BLOCKS, BLOCKS, freqs), jnp.float32), [sums])
     csd = csd.reshape(2, BLOCKS, BLOCKS, freqs)
     return (spectra, jnp.transpose(csd, (0, 3, 1, 2)))
 

time: 59.9 us -> 59.3 us (0.990)
  blocking collectives: 21.2 us -> 0 us
  starting transfers between devices: 23.6 us -> 42.2 us
  Pallas kernels: 11.2 us -> 13 us
  waiting for transfers between devices: 0.01 us -> 1.24 us
  local copies, waits for them, and re-layouts: 2.64 us -> 1.57 us
    all_to_all x1 -> x0, blocking collectives: 21.2 us -> none  [local(): lax.all_to_all(sums, 'z', 0, 0, tiled=True, axis_index_groups=[late_first...]
    all_to_all x0 -> x1, starting transfers between devices: none -> 17.7 us  [local(): lax.all_to_all(sums, 'z', 0, 0, tiled=True, axis_index_groups=[late_first...]
    reshape x1 -> x0, local copies, waits for them, and re-layouts: 1.75 us -> none  [local(): spectra = call(spectra_kernel, jax.ShapeDtypeStruct((BLOCKS, 2 * freqs, p...]
    pallas_call x5 -> x6, Pallas kernels: 9.26 us -> 11 us  [call(): pl.pallas_call(kernel, out_shape=out, in_specs=specs, out_specs=out_spec,...]
    all_to_all x1, starting transfers between devices: 7.66 us -> 8.92 us  [local(): lax.all_to_all(call(share_kernel, shares, [sums]), group, 0, 0, tiled=True)]
    all_to_all x0 -> x1, waiting for transfers between devices: none -> 1.23 us  [local(): lax.all_to_all(sums, 'z', 0, 0, tiled=True, axis_index_groups=[late_first...]
    unnamed x16, local copies, waits for them, and re-layouts: 0.89 us -> 1.57 us
  transfers between devices with their start and end apart: 5 -> 6, of which waited for: 0 -> 1; matrix products, arithmetic and copies ran while one was open for 3% -> 0% of each run, Pallas kernels for 14% -> 17%
where the time goes in v5:
time: 59.3 us; the launch traced here: 58.8 us
  starting transfers between devices  42.2 us (71%)
  Pallas kernels  13 us (22%)
  local copies, waits for them, and re-layouts  1.57 us (3%)
  waiting for transfers between devices  1.24 us (2%)
  between operations  0.8 us (1%)
    all_to_all x1, starting transfers between devices, local(): lax.all_to_all(sums, 'z', 0, 0, tiled=True, axis_index_groups=[late_first...  17.7 us
    pallas_call x6, Pallas kernels, call(): pl.pallas_call(kernel, out_shape=out, in_specs=specs, out_specs=out_spec,...  11 us
    ppermute x3, starting transfers between devices, local(): lax.ppermute(value, 'blk', [(i, (i + step) % BLOCKS) for i in range(BLOCK...  10.5 us
    all_to_all x1, starting transfers between devices, local(): lax.all_to_all(call(share_kernel, shares, [sums]), group, 0, 0, tiled=True)  8.92 us
    all_to_all x1, starting transfers between devices, local(): got = lax.all_to_all(sent, 'blk', 0, 0, tiled=True)  5.16 us
    pallas_call x1, Pallas kernels, local(): pl.pallas_call(split_kernel, out_shape=jax.ShapeDtypeStruct((BLOCKS, HOP...  2 us
    unnamed x16, local copies, waits for them, and re-layouts  1.57 us
    all_to_all x1, waiting for transfers between devices, local(): lax.all_to_all(sums, 'z', 0, 0, tiled=True, axis_index_groups=[late_first...  1.23 us
  transfers between devices with their start and end apart: 6, of which 1 were waited for; matrix products, arithmetic and copies ran while one was open for 0% of the time, Pallas kernels for 17%

profile of v5, /device:TPU:1, one launch (start us, length us, event | category | flops | bytes accessed | tf_op | source)
XLA Modules:
  0.0 58.8 jit_solution(927776374541382739)
XLA Ops:
  0.6 0.0 copy-start.5
  0.6 2.0 %shard_map.77.sent_ref = bf16[4,144,512]{2,1,0:T(8,128)(2,1)} custom-call(f32[128,2048]{1,0:T(8,128)} %pressure_ref.1), custom_call_target="tpu_custom_call" | custom-call | tf_op jit(solution)/shard_map/pallas_call | solution.py:250
  2.6 0.0 copy-start
  2.7 0.0 copy-start.2
  2.7 5.2 %all-to-all-start = ((bf16[4,144,512]{2,1,0:T(8,128)(2,1)}), bf16[4,144,512]{2,1,0:T(8,128)(2,1)S(1)}, u32[]{:S(2)}, u32[]{:S(2)}) async-start(bf16[4,144,512]{2,1,0:T(8,128)(2,1)} %shard_map.77.sent_ref), calls=%async_computation | async-start | bytes 1179648 | tf_op jit(solution)/shard_map/all_to_all | solution.py:263
  7.8 0.0 copy-done
  7.8 0.0 copy-start.3
  7.8 0.0 copy-start.4
  7.8 1.2 %shard_map.78 = (bf16[3,144,512]{2,1,0:T(8,128)(2,1)}, bf16[3,144,512]{2,1,0:T(8,128)(2,1)S(1)}, bf16[3,144,512]{2,1,0:T(8,128)(2,1)S(1)}) custom-call(s32[1]{0:T(128)} %bitcast.pos_ref, bf16[4,144,512]{2,1,0:T(8,128)(2,1)S(1)} %copy-done), custom_call_target="tpu_custom_call" | custom-call | tf_op jit(solution)/shard_map/pallas_call | solution.py:229
  9.1 3.4 %collective-permute-start = (bf16[3,144,512]{2,1,0:T(8,128)(2,1)}, bf16[3,144,512]{2,1,0:T(8,128)(2,1)S(1)}, u32[]{:S(2)}, u32[]{:S(2)}) collective-permute-start(bf16[3,144,512]{2,1,0:T(8,128)(2,1)} %get-tuple-element.6), channel_id=1, source_target_pairs={{0,1},{1,2},{2,3},{3,0},{4,5},{5,6},{6,7},{7,4},{8,9},{9,10},{10,1... | collective-permute-start | bytes 1327112 | tf_op jit(solution)/shard_map/ppermute | solution.py:269
  12.5 4.3 %collective-permute-start.1 = (bf16[3,144,512]{2,1,0:T(8,128)(2,1)S(1)}, bf16[3,144,512]{2,1,0:T(8,128)(2,1)}, u32[]{:S(2)}, u32[]{:S(2)}) collective-permute-start(bf16[3,144,512]{2,1,0:T(8,128)(2,1)S(1)} %get-tuple-element.7), channel_id=1, source_target_pairs={{0,2},{1,3},{2,0},{3,1},{4,6},{5,7},{6,4},{7,5},{8,10},{9,11},{10,... | collective-permute-start | bytes 1327112 | tf_op jit(solution)/shard_map/ppermute | solution.py:269
  16.8 0.0 all-to-all-done.got_ref
  16.8 0.0 copy-start.1
  16.8 0.0 copy-done.5
  16.8 0.0 copy-done.2
  16.8 0.0 copy-done.3
  16.8 0.0 copy-done.4
  16.8 2.3 %shard_map.81 = bf16[16,16,128]{2,1,0:T(8,128)(2,1)} custom-call(s32[1]{0:T(128)} %bitcast.pos_ref, bf16[4,144,512]{2,1,0:T(8,128)(2,1)S(1)} %all-to-all-done.got_ref, f32[128,2048]{1,0:T(8,128)S(1)} %copy-done.2, f32[1,2048]{1,0:T(1,128)S(1)} %bitcast.5, bf16[256,256]{1,0:T(8,128)(2,1)S(1)} %copy-done.5, f32[256,128]{1,0:T(8,128)S(1)} %copy-done.3), custom_call_target="tpu_custom_call" | custom-call | flops 10000000000 | bytes 10000000000 | tf_op jit(solution)/shard_map/pallas_call | solution.py:229
  19.1 0.0 copy-done.1
  19.1 17.7 %all-to-all-start.1 = ((bf16[16,16,128]{2,1,0:T(8,128)(2,1)}), bf16[16,16,128]{2,1,0:T(8,128)(2,1)S(1)}, u32[]{:S(2)}, u32[]{:S(2)}) async-start(bf16[16,16,128]{2,1,0:T(8,128)(2,1)} %shard_map.81), calls=%async_computation.1 | async-start | bytes 131072 | tf_op jit(solution)/shard_map/all_to_all | solution.py:287
  36.8 2.8 %collective-permute-start.2 = (bf16[3,144,512]{2,1,0:T(8,128)(2,1)S(1)}, bf16[3,144,512]{2,1,0:T(8,128)(2,1)S(1)}, u32[]{:S(2)}, u32[]{:S(2)}) collective-permute-start(bf16[3,144,512]{2,1,0:T(8,128)(2,1)S(1)} %get-tuple-element.8), channel_id=1, source_target_pairs={{0,3},{1,0},{2,1},{3,2},{4,7},{5,4},{6,5},{7,6},{8,11},{9,8},{10,9... | collective-permute-start | bytes 1327112 | tf_op jit(solution)/shard_map/ppermute | solution.py:269
  39.6 1.2 %all-to-all-done.1.got_ref = bf16[16,16,128]{2,1,0:T(8,128)(2,1)S(1)} async-done(((bf16[16,16,128]{2,1,0:T(8,128)(2,1)}), bf16[16,16,128]{2,1,0:T(8,128)(2,1)S(1)}, u32[]{:S(2)}, u32[]{:S(2)}) %all-to-all-start.1) | async-done | bytes 65568 | tf_op jit(solution)/shard_map/all_to_all | solution.py:287
  40.8 0.7 %shard_map.82 = f32[32,4,128]{2,1,0:T(4,128)} custom-call(bf16[16,16,128]{2,1,0:T(8,128)(2,1)S(1)} %all-to-all-done.1.got_ref), custom_call_target="tpu_custom_call" | custom-call | tf_op jit(solution)/shard_map/pallas_call | solution.py:229
  41.5 8.9 %all-to-all-start.2 = ((f32[32,4,128]{2,1,0:T(4,128)}), f32[32,4,128]{2,1,0:T(4,128)S(1)}, u32[]{:S(2)}, u32[]{:S(2)}) async-start(f32[32,4,128]{2,1,0:T(4,128)} %shard_map.82), calls=%async_computation.2 | async-start | bytes 131072 | tf_op jit(solution)/shard_map/all_to_all | solution.py:308
  50.4 0.0 collective-permute-done.first_ref.got1
  50.4 0.0 copy-start.6
  50.4 0.0 collective-permute-done.1.second_ref.got2
  50.4 0.8 %copy-done.6 = bf16[3,144,512]{2,1,0:T(8,128)(2,1)} copy-done((bf16[3,144,512]{2,1,0:T(8,128)(2,1)}, bf16[3,144,512]{2,1,0:T(8,128)(2,1)S(1)}, u32[]{:S(2)}) %copy-start.6) | copy-done | bytes 442392
  51.2 0.6 %shard_map.79.after_ref = f32[8,128]{1,0:T(8,128)} custom-call(bf16[3,144,512]{2,1,0:T(8,128)(2,1)} %copy-done.6, bf16[3,144,512]{2,1,0:T(8,128)(2,1)} %collective-permute-done.1.second_ref.got2), custom_call_target="tpu_custom_call" | custom-call | flops 10000000000 | bytes 10000000000 | tf_op jit(solution)/shard_map/pallas_call | solution.py:229
  51.8 0.0 collective-permute-done.2.got3
  51.8 0.0 copy-start.7
  51.8 0.8 %copy-done.7 = bf16[3,144,512]{2,1,0:T(8,128)(2,1)} copy-done((bf16[3,144,512]{2,1,0:T(8,128)(2,1)}, bf16[3,144,512]{2,1,0:T(8,128)(2,1)S(1)}, u32[]{:S(2)}) %copy-start.7) | copy-done | bytes 442392
  52.6 5.5 %shard_map.80 = (bf16[4,32,2,2048]{3,2,1,0:T(2,128)(2,1)}, f32[8,128]{1,0:T(8,128)}) custom-call(s32[1]{0:T(128)} %bitcast.pos_ref, f32[8,128]{1,0:T(8,128)} %shard_map.79.after_ref, f32[128,2048]{1,0:T(8,128)} %final_ref.3, bf16[256,256]{1,0:T(8,128)(2,1)} %constant.10.clone.table_ref, f32[256,128]{1,0:T(8,128)} %constant.12.clone.hann_ref, ...), custom_call_target="tpu_custom_call" | custom-call | tf_op jit(solution)/shard_map/pallas_call | solution.py:229
  58.1 0.0 all-to-all-done.2.got_ref
  58.1 0.7 %shard_map.83 = f32[8,4,32]{2,1,0:T(4,128)} custom-call(f32[32,4,128]{2,1,0:T(4,128)S(1)} %all-to-all-done.2.got_ref), custom_call_target="tpu_custom_call" | custom-call | tf_op jit(solution)/shard_map/pallas_call | solution.py:229
Async XLA Ops:
  0.6 16.2 %copy-start.5 = (bf16[256,256]{1,0:T(8,128)(2,1)S(1)}, bf16[256,256]{1,0:T(8,128)(2,1)}, u32[]{:S(2)}) copy-start(bf16[256,256]{1,0:T(8,128)(2,1)} %constant.11.clone.table_ref) | copy-start | bytes 393220
  2.6 5.2 %copy-start = (bf16[4,144,512]{2,1,0:T(8,128)(2,1)S(1)}, bf16[4,144,512]{2,1,0:T(8,128)(2,1)}, u32[]{:S(2)}) copy-start(bf16[4,144,512]{2,1,0:T(8,128)(2,1)} %shard_map.77.sent_ref) | copy-start | bytes 1769476
  2.7 14.2 %copy-start.2 = (f32[128,2048]{1,0:T(8,128)S(1)}, f32[128,2048]{1,0:T(8,128)}, u32[]{:S(2)}) copy-start(f32[128,2048]{1,0:T(8,128)} %final_ref.3) | copy-start | bytes 3145732
  2.7 14.1 %all-to-all-start = ((bf16[4,144,512]{2,1,0:T(8,128)(2,1)}), bf16[4,144,512]{2,1,0:T(8,128)(2,1)S(1)}, u32[]{:S(2)}, u32[]{:S(2)}) async-start(bf16[4,144,512]{2,1,0:T(8,128)(2,1)} %shard_map.77.sent_ref), calls=%async_computation | async-start | bytes 1179648 | tf_op jit(solution)/shard_map/all_to_all | solution.py:263
  7.8 9.0 %copy-start.3 = (f32[256,128]{1,0:T(8,128)S(1)}, f32[256,128]{1,0:T(8,128)}, u32[]{:S(2)}) copy-start(f32[256,128]{1,0:T(8,128)} %constant.12.clone.hann_ref) | copy-start | bytes 393220
  7.8 9.0 %copy-start.4 = (f32[2048]{0:T(1024)S(1)}, f32[2048]{0:T(1024)}, u32[]{:S(2)}) copy-start(f32[2048]{0:T(1024)} %param.8) | copy-start | bytes 24580
  9.1 41.3 %collective-permute-start = (bf16[3,144,512]{2,1,0:T(8,128)(2,1)}, bf16[3,144,512]{2,1,0:T(8,128)(2,1)S(1)}, u32[]{:S(2)}, u32[]{:S(2)}) collective-permute-start(bf16[3,144,512]{2,1,0:T(8,128)(2,1)} %get-tuple-element.6), channel_id=1, source_target_pairs={{0,1},{1,2},{2,3},{3,0},{4,5},{5,6},{6,7},{7,4},{8,9},{9,10},{10,1... | collective-permute-start | bytes 1327112 | tf_op jit(solution)/shard_map/ppermute | solution.py:269
  12.5 38.0 %collective-permute-start.1 = (bf16[3,144,512]{2,1,0:T(8,128)(2,1)S(1)}, bf16[3,144,512]{2,1,0:T(8,128)(2,1)}, u32[]{:S(2)}, u32[]{:S(2)}) collective-permute-start(bf16[3,144,512]{2,1,0:T(8,128)(2,1)S(1)} %get-tuple-element.7), channel_id=1, source_target_pairs={{0,2},{1,3},{2,0},{3,1},{4,6},{5,7},{6,4},{7,5},{8,10},{9,11},{10,... | collective-permute-start | bytes 1327112 | tf_op jit(solution)/shard_map/ppermute | solution.py:269
  16.8 2.3 %copy-start.1 = (bf16[4,144,512]{2,1,0:T(8,128)(2,1)}, bf16[4,144,512]{2,1,0:T(8,128)(2,1)S(1)}, u32[]{:S(2)}) copy-start(bf16[4,144,512]{2,1,0:T(8,128)(2,1)S(1)} %all-to-all-done.got_ref) | copy-start | bytes 1769476
  19.1 21.7 %all-to-all-start.1 = ((bf16[16,16,128]{2,1,0:T(8,128)(2,1)}), bf16[16,16,128]{2,1,0:T(8,128)(2,1)S(1)}, u32[]{:S(2)}, u32[]{:S(2)}) async-start(bf16[16,16,128]{2,1,0:T(8,128)(2,1)} %shard_map.81), calls=%async_computation.1 | async-start | bytes 131072 | tf_op jit(solution)/shard_map/all_to_all | solution.py:287
  36.8 15.0 %collective-permute-start.2 = (bf16[3,144,512]{2,1,0:T(8,128)(2,1)S(1)}, bf16[3,144,512]{2,1,0:T(8,128)(2,1)S(1)}, u32[]{:S(2)}, u32[]{:S(2)}) collective-permute-start(bf16[3,144,512]{2,1,0:T(8,128)(2,1)S(1)} %get-tuple-element.8), channel_id=1, source_target_pairs={{0,3},{1,0},{2,1},{3,2},{4,7},{5,4},{6,5},{7,6},{8,11},{9,8},{10,9... | collective-permute-start | bytes 1327112 | tf_op jit(solution)/shard_map/ppermute | solution.py:269
  41.5 16.6 %all-to-all-start.2 = ((f32[32,4,128]{2,1,0:T(4,128)}), f32[32,4,128]{2,1,0:T(4,128)S(1)}, u32[]{:S(2)}, u32[]{:S(2)}) async-start(f32[32,4,128]{2,1,0:T(4,128)} %shard_map.82), calls=%async_computation.2 | async-start | bytes 131072 | tf_op jit(solution)/shard_map/all_to_all | solution.py:308
  50.4 0.8 %copy-start.6 = (bf16[3,144,512]{2,1,0:T(8,128)(2,1)}, bf16[3,144,512]{2,1,0:T(8,128)(2,1)S(1)}, u32[]{:S(2)}) copy-start(bf16[3,144,512]{2,1,0:T(8,128)(2,1)S(1)} %collective-permute-done.first_ref.got1) | copy-start | bytes 1327108
  51.8 0.8 %copy-start.7 = (bf16[3,144,512]{2,1,0:T(8,128)(2,1)}, bf16[3,144,512]{2,1,0:T(8,128)(2,1)S(1)}, u32[]{:S(2)}) copy-start(bf16[3,144,512]{2,1,0:T(8,128)(2,1)S(1)} %collective-permute-done.2.got3) | copy-start | bytes 1327108

commit v6 on v5

--- a/solution.py
+++ b/solution.py
@@ -33,11 +33,9 @@
     angle = 2.0 * math.pi / BLEN * (k[:, None] * t[None, :] % BLEN)
     scale = 1.0 / math.sqrt(3.0 * BLEN / 8.0)
     parts = np.stack([np.cos(angle) * scale, -np.sin(angle) * scale], axis=1)
-    hann = 0.5 - 0.5 * np.cos(2.0 * math.pi / BLEN * t)
     return (
         jnp.asarray(parts.reshape(2 * HOP, BLEN), jnp.bfloat16),
         jnp.asarray(parts.swapaxes(0, 1).reshape(2 * HOP, BLEN), jnp.bfloat16),
-        jnp.asarray(np.repeat(hann[:, None], 128, axis=1), jnp.float32),
     )
 
 
@@ -69,11 +67,20 @@
         store(quarter).wait()
 
 
-def windows(segments, final, hann_ref):
+def window():
+    t = lax.broadcasted_iota(jnp.int32, (BLEN, 128), 0).astype(jnp.float32)
+    square = ((t - HOP) * (math.pi / BLEN)) ** 2
+    cosine = jnp.full_like(square, 1.0 / math.factorial(12))
+    for order in range(10, -1, -2):
+        cosine = cosine * square + (-1.0) ** (order // 2) / math.factorial(order)
+    return cosine * cosine
+
+
+def windows(segments, final, hann):
     means = [jnp.sum(ref[HOP:].astype(jnp.float32), axis=0, keepdims=True) for ref in segments]
     total = jnp.sum(final, axis=0, keepdims=True) + HOP * (means[0] + means[1] + means[2] + means[3])
     mean = total / (HOP * (BLOCKS + 1))
-    hann = jnp.concatenate([hann_ref[...]] * (final.shape[1] // 128), axis=1)
+    hann = jnp.concatenate([hann] * (final.shape[1] // 128), axis=1)
 
     def segment(s):
         if s == BLOCKS:
@@ -88,13 +95,13 @@
 
 
 def sums_kernel(
-    count, pos_ref, got_ref, final_ref, weights_ref, table_ref, hann_ref, out_ref, coeff, sums, rows
+    count, pos_ref, got_ref, final_ref, weights_ref, table_ref, out_ref, coeff, sums, rows
 ):
     me = pos_ref[0]
     width = got_ref.shape[2]
     own = pl.ds(pl.multiple_of(me * width, width), width)
     segments = [got_ref.at[s] for s in range(BLOCKS)]
-    for b, windowed in enumerate(windows(segments, final_ref[:, own], hann_ref)):
+    for b, windowed in enumerate(windows(segments, final_ref[:, own], window())):
         apart = jnp.dot(table_ref[...], windowed, preferred_element_type=jnp.float32)
         coeff[b] = apart.astype(jnp.bfloat16).astype(jnp.float32)
 
@@ -134,14 +141,14 @@
         out_ref[copy] = value
 
 
-def fan_kernel(pos_ref, sent_ref, out1, out2, out3, sems):
+def fan_kernel(steps, pos_ref, sent_ref, *refs):
+    *outs, sems = refs[len(refs) - len(steps) - 1 :]
     me = pos_ref[0]
     copies = []
-    for step, out in enumerate((out1, out2, out3), 1):
+    for at, (step, out) in enumerate(zip(steps, outs)):
         for place in range(BLOCKS - 1):
             quarter = lax.rem(me + step + 1 + place, BLOCKS)
-            sem = sems.at[step - 1, place]
-            copies.append(pltpu.make_async_copy(sent_ref.at[quarter], out.at[place], sem))
+            copies.append(pltpu.make_async_copy(sent_ref.at[quarter], out.at[place], sems.at[at, place]))
     for copy in copies:
         copy.start()
     for copy in copies:
@@ -149,11 +156,12 @@
 
 
 def spectra_kernel(
-    pos_ref, after_ref, final_ref, table_ref, hann_ref, sent_ref, got_ref, got1, got2, got3, out_ref, token_ref, held, last, ready, sems, last_sems, out_sems
+    pos_ref, after_ref, final_ref, table_ref, own_ref, got_ref, got1, got2, got3, out_ref, token_ref, held, last, ready, sems, last_sems, out_sems
 ):
     me = pos_ref[0]
-    width = sent_ref.shape[2]
+    width = own_ref.shape[2]
     own = BLOCKS - 1
+    hann = window()
 
     def cols(place):
         return pl.ds(pl.multiple_of(lax.rem(me + 1 + place, BLOCKS) * width, width), width)
@@ -164,7 +172,7 @@
         if place == own:
             copies.append(pltpu.make_async_copy(got_ref, held.at[place], sems.at[place, 0]))
         else:
-            mine = sent_ref.at[lax.rem(me + 1 + place, BLOCKS)]
+            mine = own_ref.at[lax.rem(me + 1 + place, BLOCKS)]
             copies.append(pltpu.make_async_copy(mine, held.at[place, me], sems.at[place, 0]))
             for step, got in enumerate((got1, got2, got3), 1):
                 source = lax.rem(me + BLOCKS - step, BLOCKS)
@@ -185,7 +193,7 @@
     for place in order:
         for copy in fetches[place]:
             copy.wait()
-        blocks = windows([held.at[place, s] for s in range(BLOCKS)], last[place], hann_ref)
+        blocks = windows([held.at[place, s] for s in range(BLOCKS)], last[place], hann)
         for b, windowed in enumerate(blocks):
             mixed = jnp.dot(table, windowed, preferred_element_type=jnp.float32)
             ready[place, b] = mixed.astype(jnp.bfloat16).reshape(ready.shape[2:])
@@ -246,7 +254,7 @@
     width = points // BLOCKS
     freqs = HOP // BLOCKS
     here = (lax.axis_index("blk").astype(jnp.int32).reshape(1), SMEM)
-    table, apart, hann = tables()
+    table, apart = tables()
     sent = pl.pallas_call(
         split_kernel,
         out_shape=jax.ShapeDtypeStruct((BLOCKS, HOP + MEANS, width), jnp.bfloat16),
@@ -262,13 +270,21 @@
     )(pressure)
     got = lax.all_to_all(sent, "blk", 0, 0, tiled=True)
     part = jax.ShapeDtypeStruct((BLOCKS - 1, HOP + MEANS, width), jnp.bfloat16)
-    parts = call(
-        fan_kernel, [part] * 3, [here, (sent, ANY)], [pltpu.SemaphoreType.DMA((3, BLOCKS - 1))], out_spec=[HBM] * 3
-    )
-    moved = [
-        lax.ppermute(value, "blk", [(i, (i + step) % BLOCKS) for i in range(BLOCKS)])
-        for step, value in enumerate(parts, 1)
-    ]
+
+    def passed_on(steps, near):
+        parts = call(
+            functools.partial(fan_kernel, steps),
+            [part] * len(steps),
+            [here, (sent, ANY), *near],
+            [pltpu.SemaphoreType.DMA((len(steps), BLOCKS - 1))],
+            out_spec=[HBM] * len(steps),
+        )
+        return [
+            lax.ppermute(value, "blk", [(i, (i + step) % BLOCKS) for i in range(BLOCKS)])
+            for step, value in zip(steps, parts)
+        ]
+
+    moved = passed_on((1, 2), [apart, weights.reshape(1, points), table]) + passed_on((3,), [])
 
     group = ("blk", "x", "core")
     count = float(points * lax.axis_size(SPACE))
@@ -276,7 +292,7 @@
     sums = call(
         functools.partial(sums_kernel, count),
         jax.ShapeDtypeStruct((lax.axis_size("z"), lines, 128), jnp.bfloat16),
-        [here, got, final_steps, weights.reshape(1, points), apart, hann],
+        [here, got, final_steps, weights.reshape(1, points), apart],
         [
             pltpu.VMEM((BLOCKS, 2 * HOP, width), jnp.float32),
             pltpu.VMEM((SUMS * HOP, 128), jnp.float32),
@@ -287,12 +303,12 @@
     sums = lax.all_to_all(sums, "z", 0, 0, tiled=True, axis_index_groups=[late_first(lax.axis_size("z"))])
     token = jax.ShapeDtypeStruct((8, 128), jnp.float32)
     after = call(
-        token_kernel, token, [(moved[0], ANY), (moved[1], ANY)], cost=WAIT, limit=60 * 1024 * 1024
+        token_kernel, token, [(moved[0], ANY), (moved[1], ANY)], cost=WAIT
     )
     spectra, token = call(
         spectra_kernel,
         [jax.ShapeDtypeStruct((BLOCKS, freqs, 2, points), jnp.bfloat16), token],
-        [here, after, (final_steps, ANY), table, hann, (sent, ANY), (got, ANY), *((value, ANY) for value in moved)],
+        [here, after, (final_steps, ANY), table, (sent, ANY), (got, ANY), *((value, ANY) for value in moved)],
         [
             pltpu.VMEM((BLOCKS, BLOCKS, HOP + MEANS, width), jnp.bfloat16),
             pltpu.VMEM((BLOCKS, HOP, width), jnp.float32),
@@ -302,7 +318,6 @@
             pltpu.SemaphoreType.DMA((BLOCKS,)),
         ],
         out_spec=[ANY, VMEM],
-        limit=60 * 1024 * 1024,
     )
     shares = jax.ShapeDtypeStruct((lax.axis_size(group), lines // BLOCKS, 128), jnp.float32)
     sums = lax.all_to_all(call(share_kernel, shares, [sums]), group, 0, 0, tiled=True)

time: 59.3 us -> 58.9 us (level)
  waiting for transfers between devices: 1.24 us -> 3.41 us
  local copies, waits for them, and re-layouts: 1.57 us -> 0.03 us
  Pallas kernels: 13 us -> 11.8 us
    all_to_all x1, waiting for transfers between devices: 0.01 us -> 2.77 us  [local(): lax.all_to_all(call(share_kernel, shares, [sums]), group, 0, 0, tiled=True)]
    unnamed x16 -> x10, local copies, waits for them, and re-layouts: 1.57 us -> 0.03 us
    pallas_call x6 -> x7, Pallas kernels: 11 us -> 9.83 us  [call(): pl.pallas_call(kernel, out_shape=out, in_specs=specs, out_specs=out_spec,...]
    all_to_all x1, waiting for transfers between devices: 1.23 us -> 0.62 us  [local(): lax.all_to_all(sums, 'z', 0, 0, tiled=True, axis_index_groups=[late_first...]
  transfers between devices with their start and end apart: 6 -> 6, of which waited for: 1 -> 2; matrix products, arithmetic and copies ran while one was open for 0% -> 0% of each run, Pallas kernels for 17% -> 16%
where the time goes in v6:
time: 58.9 us; the launch traced here: 58.5 us
  starting transfers between devices  42.4 us (72%)
  Pallas kernels  11.8 us (20%)
  waiting for transfers between devices  3.41 us (6%)
  between operations  0.79 us (1%)
    all_to_all x1, starting transfers between devices, local(): lax.all_to_all(sums, 'z', 0, 0, tiled=True, axis_index_groups=[late_first...  17.9 us
    ppermute x3, starting transfers between devices, passed_on(): lax.ppermute(value, 'blk', [(i, (i + step) % BLOCKS) for i in range(BLOCK...  10.5 us
    pallas_call x7, Pallas kernels, call(): pl.pallas_call(kernel, out_shape=out, in_specs=specs, out_specs=out_spec,...  9.83 us
    all_to_all x1, starting transfers between devices, local(): lax.all_to_all(call(share_kernel, shares, [sums]), group, 0, 0, tiled=True)  8.92 us
    all_to_all x1, starting transfers between devices, local(): got = lax.all_to_all(sent, 'blk', 0, 0, tiled=True)  5.16 us
    all_to_all x1, waiting for transfers between devices, local(): lax.all_to_all(call(share_kernel, shares, [sums]), group, 0, 0, tiled=True)  2.77 us
    pallas_call x1, Pallas kernels, local(): pl.pallas_call(split_kernel, out_shape=jax.ShapeDtypeStruct((BLOCKS, HOP...  2.01 us
  transfers between devices with their start and end apart: 6, of which 2 were waited for; matrix products, arithmetic and copies ran while one was open for 0% of the time, Pallas kernels for 16%

profile of v6, /device:TPU:1, one launch (start us, length us, event | category | flops | bytes accessed | tf_op | source)
XLA Modules:
  0.0 58.5 jit_solution(12778685134738878490)
XLA Ops:
  0.6 0.0 copy-start.2
  0.6 0.0 copy-start.3
  0.7 0.0 copy-start.4
  0.7 2.0 %shard_map.68.sent_ref.own_ref = bf16[4,144,512]{2,1,0:T(8,128)(2,1)} custom-call(f32[128,2048]{1,0:T(8,128)} %pressure_ref.1), custom_call_target="tpu_custom_call" | custom-call | tf_op jit(solution)/shard_map/pallas_call | solution.py:258
  2.7 0.0 copy-start
  2.7 0.0 copy-start.1
  2.7 5.2 %all-to-all-start = ((bf16[4,144,512]{2,1,0:T(8,128)(2,1)}), bf16[4,144,512]{2,1,0:T(8,128)(2,1)S(1)}, u32[]{:S(2)}, u32[]{:S(2)}) async-start(bf16[4,144,512]{2,1,0:T(8,128)(2,1)} %shard_map.68.sent_ref.own_ref), calls=%async_computation | async-start | bytes 1179648 | tf_op jit(solution)/shard_map/all_to_all | solution.py:271
  7.9 0.0 copy-done.2
  7.9 0.0 copy-done.3
  7.9 0.0 copy-done.4
  7.9 0.0 copy-done
  7.9 1.0 %shard_map.69 = (bf16[3,144,512]{2,1,0:T(8,128)(2,1)}, bf16[3,144,512]{2,1,0:T(8,128)(2,1)}) custom-call(s32[1]{0:T(128)} %bitcast.pos_ref, bf16[4,144,512]{2,1,0:T(8,128)(2,1)S(1)} %copy-done, bf16[256,256]{1,0:T(8,128)(2,1)S(1)} %copy-done.3, f32[1,2048]{1,0:T(1,128)S(1)} %bitcast.5, bf16[256,256]{1,0:T(8,128)(2,1)S(1)} %copy-done.2), custom_call_target="tpu_custom_call" | custom-call | tf_op jit(solution)/shard_map/pallas_call | solution.py:237
  8.9 3.4 %collective-permute-start = (bf16[3,144,512]{2,1,0:T(8,128)(2,1)}, bf16[3,144,512]{2,1,0:T(8,128)(2,1)S(1)}, u32[]{:S(2)}, u32[]{:S(2)}) collective-permute-start(bf16[3,144,512]{2,1,0:T(8,128)(2,1)} %get-tuple-element.5), channel_id=1, source_target_pairs={{0,1},{1,2},{2,3},{3,0},{4,5},{5,6},{6,7},{7,4},{8,9},{9,10},{10,1... | collective-permute-start | bytes 1327112 | tf_op jit(solution)/shard_map/ppermute | solution.py:283
  12.3 4.3 %collective-permute-start.1 = (bf16[3,144,512]{2,1,0:T(8,128)(2,1)}, bf16[3,144,512]{2,1,0:T(8,128)(2,1)}, u32[]{:S(2)}, u32[]{:S(2)}) collective-permute-start(bf16[3,144,512]{2,1,0:T(8,128)(2,1)} %get-tuple-element.6), channel_id=1, source_target_pairs={{0,2},{1,3},{2,0},{3,1},{4,6},{5,7},{6,4},{7,5},{8,10},{9,11},{10,... | collective-permute-start | bytes 1327112 | tf_op jit(solution)/shard_map/ppermute | solution.py:283
  16.6 0.0 all-to-all-done.got_ref
  16.6 0.0 copy-done.1
  16.6 2.4 %shard_map.73 = bf16[16,16,128]{2,1,0:T(8,128)(2,1)} custom-call(s32[1]{0:T(128)} %bitcast.pos_ref, bf16[4,144,512]{2,1,0:T(8,128)(2,1)S(1)} %all-to-all-done.got_ref, f32[128,2048]{1,0:T(8,128)S(1)} %copy-done.1, f32[1,2048]{1,0:T(1,128)S(1)} %bitcast.6, bf16[256,256]{1,0:T(8,128)(2,1)S(1)} %copy-done.3), custom_call_target="tpu_custom_call" | custom-call | flops 10000000000 | bytes 10000000000 | tf_op jit(solution)/shard_map/pallas_call | solution.py:237
  19.0 17.9 %all-to-all-start.1 = ((bf16[16,16,128]{2,1,0:T(8,128)(2,1)}), bf16[16,16,128]{2,1,0:T(8,128)(2,1)S(1)}, u32[]{:S(2)}, u32[]{:S(2)}) async-start(bf16[16,16,128]{2,1,0:T(8,128)(2,1)} %shard_map.73), calls=%async_computation.1 | async-start | bytes 131072 | tf_op jit(solution)/shard_map/all_to_all | solution.py:303
  36.9 0.6 %shard_map.71 = bf16[3,144,512]{2,1,0:T(8,128)(2,1)S(1)} custom-call(s32[1]{0:T(128)} %bitcast.pos_ref, bf16[4,144,512]{2,1,0:T(8,128)(2,1)S(1)} %copy-done), custom_call_target="tpu_custom_call" | custom-call | tf_op jit(solution)/shard_map/pallas_call | solution.py:237
  37.5 2.8 %collective-permute-start.2 = (bf16[3,144,512]{2,1,0:T(8,128)(2,1)S(1)}, bf16[3,144,512]{2,1,0:T(8,128)(2,1)}, u32[]{:S(2)}, u32[]{:S(2)}) collective-permute-start(bf16[3,144,512]{2,1,0:T(8,128)(2,1)S(1)} %shard_map.71), channel_id=1, source_target_pairs={{0,3},{1,0},{2,1},{3,2},{4,7},{5,4},{6,5},{7,6},{8,11},{9,8},{10,9... | collective-permute-start | bytes 1327112 | tf_op jit(solution)/shard_map/ppermute | solution.py:283
  40.3 0.6 %all-to-all-done.1.got_ref = bf16[16,16,128]{2,1,0:T(8,128)(2,1)S(1)} async-done(((bf16[16,16,128]{2,1,0:T(8,128)(2,1)}), bf16[16,16,128]{2,1,0:T(8,128)(2,1)S(1)}, u32[]{:S(2)}, u32[]{:S(2)}) %all-to-all-start.1) | async-done | bytes 65568 | tf_op jit(solution)/shard_map/all_to_all | solution.py:303
  40.9 0.6 %shard_map.74 = f32[32,4,128]{2,1,0:T(4,128)} custom-call(bf16[16,16,128]{2,1,0:T(8,128)(2,1)S(1)} %all-to-all-done.1.got_ref), custom_call_target="tpu_custom_call" | custom-call | tf_op jit(solution)/shard_map/pallas_call | solution.py:237
  41.6 8.9 %all-to-all-start.2 = ((f32[32,4,128]{2,1,0:T(4,128)}), f32[32,4,128]{2,1,0:T(4,128)S(1)}, u32[]{:S(2)}, u32[]{:S(2)}) async-start(f32[32,4,128]{2,1,0:T(4,128)} %shard_map.74), calls=%async_computation.2 | async-start | bytes 131072 | tf_op jit(solution)/shard_map/all_to_all | solution.py:323
  50.5 0.0 collective-permute-done.first_ref.got1
  50.5 0.0 collective-permute-done.1.second_ref.got2
  50.5 0.0 collective-permute-done.2.got3
  50.5 4.5 %shard_map.72 = (bf16[4,32,2,2048]{3,2,1,0:T(2,128)(2,1)}, f32[8,128]{1,0:T(8,128)}) custom-call(s32[1]{0:T(128)} %bitcast.pos_ref, f32[8,128]{1,0:T(8,128)S(1)} %shard_map.70.after_ref, f32[128,2048]{1,0:T(8,128)S(1)} %copy-done.1, bf16[256,256]{1,0:T(8,128)(2,1)S(1)} %copy-done.2, bf16[4,144,512]{2,1,0:T(8,128)(2,1)S(1)} %copy-done, ...), custom_call_target="tpu_custom_call" | custom-call | tf_op jit(solution)/shard_map/pallas_call | solution.py:237
  55.0 2.8 %all-to-all-done.2.got_ref = f32[32,4,128]{2,1,0:T(4,128)S(1)} async-done(((f32[32,4,128]{2,1,0:T(4,128)}), f32[32,4,128]{2,1,0:T(4,128)S(1)}, u32[]{:S(2)}, u32[]{:S(2)}) %all-to-all-start.2) | async-done | bytes 65568 | tf_op jit(solution)/shard_map/all_to_all | solution.py:323
  57.8 0.7 %shard_map.75 = f32[8,4,32]{2,1,0:T(4,128)} custom-call(f32[32,4,128]{2,1,0:T(4,128)S(1)} %all-to-all-done.2.got_ref), custom_call_target="tpu_custom_call" | custom-call | tf_op jit(solution)/shard_map/pallas_call | solution.py:237
  (1 shorter events, 0.0 us)
Async XLA Ops:
  0.6 7.2 %copy-start.2 = (bf16[256,256]{1,0:T(8,128)(2,1)S(1)}, bf16[256,256]{1,0:T(8,128)(2,1)}, u32[]{:S(2)}) copy-start(bf16[256,256]{1,0:T(8,128)(2,1)} %constant.8.clone.refs_2_.table_ref) | copy-start | bytes 393220
  0.6 7.2 %copy-start.3 = (bf16[256,256]{1,0:T(8,128)(2,1)S(1)}, bf16[256,256]{1,0:T(8,128)(2,1)}, u32[]{:S(2)}) copy-start(bf16[256,256]{1,0:T(8,128)(2,1)} %constant.9.clone.refs_0_.table_ref) | copy-start | bytes 393220
  0.7 7.2 %copy-start.4 = (f32[2048]{0:T(1024)S(1)}, f32[2048]{0:T(1024)}, u32[]{:S(2)}) copy-start(f32[2048]{0:T(1024)} %param.7) | copy-start | bytes 24580
  2.7 5.2 %copy-start = (bf16[4,144,512]{2,1,0:T(8,128)(2,1)S(1)}, bf16[4,144,512]{2,1,0:T(8,128)(2,1)}, u32[]{:S(2)}) copy-start(bf16[4,144,512]{2,1,0:T(8,128)(2,1)} %shard_map.68.sent_ref.own_ref) | copy-start | bytes 1769476
  2.7 13.9 %copy-start.1 = (f32[128,2048]{1,0:T(8,128)S(1)}, f32[128,2048]{1,0:T(8,128)}, u32[]{:S(2)}) copy-start(f32[128,2048]{1,0:T(8,128)} %final_ref.3) | copy-start | bytes 3145732
  2.7 13.9 %all-to-all-start = ((bf16[4,144,512]{2,1,0:T(8,128)(2,1)}), bf16[4,144,512]{2,1,0:T(8,128)(2,1)S(1)}, u32[]{:S(2)}, u32[]{:S(2)}) async-start(bf16[4,144,512]{2,1,0:T(8,128)(2,1)} %shard_map.68.sent_ref.own_ref), calls=%async_computation | async-start | bytes 1179648 | tf_op jit(solution)/shard_map/all_to_all | solution.py:271
  8.9 41.6 %collective-permute-start = (bf16[3,144,512]{2,1,0:T(8,128)(2,1)}, bf16[3,144,512]{2,1,0:T(8,128)(2,1)S(1)}, u32[]{:S(2)}, u32[]{:S(2)}) collective-permute-start(bf16[3,144,512]{2,1,0:T(8,128)(2,1)} %get-tuple-element.5), channel_id=1, source_target_pairs={{0,1},{1,2},{2,3},{3,0},{4,5},{5,6},{6,7},{7,4},{8,9},{9,10},{10,1... | collective-permute-start | bytes 1327112 | tf_op jit(solution)/shard_map/ppermute | solution.py:283
  12.3 38.2 %collective-permute-start.1 = (bf16[3,144,512]{2,1,0:T(8,128)(2,1)}, bf16[3,144,512]{2,1,0:T(8,128)(2,1)}, u32[]{:S(2)}, u32[]{:S(2)}) collective-permute-start(bf16[3,144,512]{2,1,0:T(8,128)(2,1)} %get-tuple-element.6), channel_id=1, source_target_pairs={{0,2},{1,3},{2,0},{3,1},{4,6},{5,7},{6,4},{7,5},{8,10},{9,11},{10,... | collective-permute-start | bytes 1327112 | tf_op jit(solution)/shard_map/ppermute | solution.py:283
  19.0 21.9 %all-to-all-start.1 = ((bf16[16,16,128]{2,1,0:T(8,128)(2,1)}), bf16[16,16,128]{2,1,0:T(8,128)(2,1)S(1)}, u32[]{:S(2)}, u32[]{:S(2)}) async-start(bf16[16,16,128]{2,1,0:T(8,128)(2,1)} %shard_map.73), calls=%async_computation.1 | async-start | bytes 131072 | tf_op jit(solution)/shard_map/all_to_all | solution.py:303
  37.5 13.0 %collective-permute-start.2 = (bf16[3,144,512]{2,1,0:T(8,128)(2,1)S(1)}, bf16[3,144,512]{2,1,0:T(8,128)(2,1)}, u32[]{:S(2)}, u32[]{:S(2)}) collective-permute-start(bf16[3,144,512]{2,1,0:T(8,128)(2,1)S(1)} %shard_map.71), channel_id=1, source_target_pairs={{0,3},{1,0},{2,1},{3,2},{4,7},{5,4},{6,5},{7,6},{8,11},{9,8},{10,9... | collective-permute-start | bytes 1327112 | tf_op jit(solution)/shard_map/ppermute | solution.py:283
  41.6 16.3 %all-to-all-start.2 = ((f32[32,4,128]{2,1,0:T(4,128)}), f32[32,4,128]{2,1,0:T(4,128)S(1)}, u32[]{:S(2)}, u32[]{:S(2)}) async-start(f32[32,4,128]{2,1,0:T(4,128)} %shard_map.74), calls=%async_computation.2 | async-start | bytes 131072 | tf_op jit(solution)/shard_map/all_to_all | solution.py:323

commit v7 on v6

--- a/solution.py
+++ b/solution.py
@@ -127,13 +127,9 @@
         return carry
 
     lax.fori_loop(0, HOP // 8, tile, 0)
-    values = sums[...]
-    high = values.astype(jnp.bfloat16)
-    low = (values - high.astype(jnp.float32)).astype(jnp.bfloat16)
     ones = jnp.ones((8, 128), jnp.bfloat16)
     along = (((1,), (1,)), ((), ()))
-    lanes = lax.dot_general(ones, high, along, preferred_element_type=jnp.float32)
-    lanes += lax.dot_general(ones, low, along, preferred_element_type=jnp.float32)
+    lanes = lax.dot_general(ones, sums[...].astype(jnp.bfloat16), along, preferred_element_type=jnp.float32)
     for row in range(rows.shape[0]):
         rows[row : row + 1] = lanes[:1, row * 128 : (row + 1) * 128]
     value = rows[...].astype(jnp.bfloat16)
@@ -213,12 +209,12 @@
     copies = out_ref.shape[0] // BLOCKS
     for q in range(BLOCKS):
         for copy in range(copies):
-            out_ref[q * copies + copy] = total[q * part : (q + 1) * part]
+            out_ref[q * copies + copy] = total[q * part : (q + 1) * part].astype(out_ref.dtype)
 
 
 def matrix_kernel(got_ref, csd_ref):
     freqs = csd_ref.shape[2]
-    total = jnp.sum(got_ref[...], axis=0)
+    total = jnp.sum(got_ref[...].astype(jnp.float32), axis=0)
     each = 128 // freqs
     rows = [total[p // each : p // each + 1, p % each * freqs : (p % each + 1) * freqs] for p in range(SUMS)]
     for i in range(BLOCKS):
@@ -246,7 +242,7 @@
 
 
 def late_first(size):
-    return [(i + size // 2 + 1) % size for i in range(size)]
+    return [(i + size // 2 + 3) % size for i in range(size)]
 
 
 def local(pressure, final_steps, weights):
@@ -319,7 +315,7 @@
         ],
         out_spec=[ANY, VMEM],
     )
-    shares = jax.ShapeDtypeStruct((lax.axis_size(group), lines // BLOCKS, 128), jnp.float32)
+    shares = jax.ShapeDtypeStruct((lax.axis_size(group), lines // BLOCKS, 128), jnp.bfloat16)
     sums = lax.all_to_all(call(share_kernel, shares, [sums]), group, 0, 0, tiled=True)
     csd = call(matrix_kernel, jax.ShapeDtypeStruct((2 * BLOCKS, BLOCKS, freqs), jnp.float32), [sums])
     csd = csd.reshape(2, BLOCKS, BLOCKS, freqs)

time: 58.9 us -> 58.6 us (level)
  starting transfers between devices: 42.4 us -> 40.6 us
  waiting for transfers between devices: 3.41 us -> 5.09 us
    all_to_all x1, starting transfers between devices: 17.9 us -> 16.1 us  [local(): lax.all_to_all(sums, 'z', 0, 0, tiled=True, axis_index_groups=[late_first...]
    all_to_all x1, waiting for transfers between devices: 0.62 us -> 2.38 us  [local(): lax.all_to_all(sums, 'z', 0, 0, tiled=True, axis_index_groups=[late_first...]
  transfers between devices with their start and end apart: 6 -> 6, of which waited for: 2 -> 2; matrix products, arithmetic and copies ran while one was open for 0% -> 0% of each run, Pallas kernels for 16% -> 15%
where the time goes in v7:
time: 58.6 us; the launch traced here: 58.3 us
  starting transfers between devices  40.6 us (69%)
  Pallas kernels  11.7 us (20%)
  waiting for transfers between devices  5.09 us (9%)
  between operations  0.79 us (1%)
    all_to_all x1, starting transfers between devices, local(): lax.all_to_all(sums, 'z', 0, 0, tiled=True, axis_index_groups=[late_first...  16.1 us
    ppermute x3, starting transfers between devices, passed_on(): lax.ppermute(value, 'blk', [(i, (i + step) % BLOCKS) for i in range(BLOCK...  10.5 us
    pallas_call x7, Pallas kernels, call(): pl.pallas_call(kernel, out_shape=out, in_specs=specs, out_specs=out_spec,...  9.68 us
    all_to_all x1, starting transfers between devices, local(): lax.all_to_all(call(share_kernel, shares, [sums]), group, 0, 0, tiled=True)  8.92 us
    all_to_all x1, starting transfers between devices, local(): got = lax.all_to_all(sent, 'blk', 0, 0, tiled=True)  5.16 us
    all_to_all x1, waiting for transfers between devices, local(): lax.all_to_all(call(share_kernel, shares, [sums]), group, 0, 0, tiled=True)  2.7 us
    all_to_all x1, waiting for transfers between devices, local(): lax.all_to_all(sums, 'z', 0, 0, tiled=True, axis_index_groups=[late_first...  2.38 us
    pallas_call x1, Pallas kernels, local(): pl.pallas_call(split_kernel, out_shape=jax.ShapeDtypeStruct((BLOCKS, HOP...  2.01 us
  transfers between devices with their start and end apart: 6, of which 2 were waited for; matrix products, arithmetic and copies ran while one was open for 0% of the time, Pallas kernels for 15%

profile of v7, /device:TPU:1, one launch (start us, length us, event | category | flops | bytes accessed | tf_op | source)
XLA Modules:
  0.0 58.3 jit_solution(2428207568896423641)
XLA Ops:
  0.6 0.0 copy-start.2
  0.6 0.0 copy-start.3
  0.7 0.0 copy-start.4
  0.7 2.0 %shard_map.68.sent_ref.own_ref = bf16[4,144,512]{2,1,0:T(8,128)(2,1)} custom-call(f32[128,2048]{1,0:T(8,128)} %pressure_ref.1), custom_call_target="tpu_custom_call" | custom-call | tf_op jit(solution)/shard_map/pallas_call | solution.py:254
  2.7 0.0 copy-start
  2.7 0.0 copy-start.1
  2.7 5.2 %all-to-all-start = ((bf16[4,144,512]{2,1,0:T(8,128)(2,1)}), bf16[4,144,512]{2,1,0:T(8,128)(2,1)S(1)}, u32[]{:S(2)}, u32[]{:S(2)}) async-start(bf16[4,144,512]{2,1,0:T(8,128)(2,1)} %shard_map.68.sent_ref.own_ref), calls=%async_computation | async-start | bytes 1179648 | tf_op jit(solution)/shard_map/all_to_all | solution.py:267
  7.9 0.0 copy-done.2
  7.9 0.0 copy-done.3
  7.9 0.0 copy-done.4
  7.9 0.0 copy-done
  7.9 1.0 %shard_map.69 = (bf16[3,144,512]{2,1,0:T(8,128)(2,1)}, bf16[3,144,512]{2,1,0:T(8,128)(2,1)}) custom-call(s32[1]{0:T(128)} %bitcast.pos_ref, bf16[4,144,512]{2,1,0:T(8,128)(2,1)S(1)} %copy-done, bf16[256,256]{1,0:T(8,128)(2,1)S(1)} %copy-done.3, f32[1,2048]{1,0:T(1,128)S(1)} %bitcast.5, bf16[256,256]{1,0:T(8,128)(2,1)S(1)} %copy-done.2), custom_call_target="tpu_custom_call" | custom-call | tf_op jit(solution)/shard_map/pallas_call | solution.py:233
  8.9 3.4 %collective-permute-start = (bf16[3,144,512]{2,1,0:T(8,128)(2,1)}, bf16[3,144,512]{2,1,0:T(8,128)(2,1)S(1)}, u32[]{:S(2)}, u32[]{:S(2)}) collective-permute-start(bf16[3,144,512]{2,1,0:T(8,128)(2,1)} %get-tuple-element.5), channel_id=1, source_target_pairs={{0,1},{1,2},{2,3},{3,0},{4,5},{5,6},{6,7},{7,4},{8,9},{9,10},{10,1... | collective-permute-start | bytes 1327112 | tf_op jit(solution)/shard_map/ppermute | solution.py:279
  12.3 4.3 %collective-permute-start.1 = (bf16[3,144,512]{2,1,0:T(8,128)(2,1)}, bf16[3,144,512]{2,1,0:T(8,128)(2,1)}, u32[]{:S(2)}, u32[]{:S(2)}) collective-permute-start(bf16[3,144,512]{2,1,0:T(8,128)(2,1)} %get-tuple-element.6), channel_id=1, source_target_pairs={{0,2},{1,3},{2,0},{3,1},{4,6},{5,7},{6,4},{7,5},{8,10},{9,11},{10,... | collective-permute-start | bytes 1327112 | tf_op jit(solution)/shard_map/ppermute | solution.py:279
  16.6 0.0 all-to-all-done.got_ref
  16.6 0.0 copy-done.1
  16.6 2.2 %shard_map.73 = bf16[16,16,128]{2,1,0:T(8,128)(2,1)} custom-call(s32[1]{0:T(128)} %bitcast.pos_ref, bf16[4,144,512]{2,1,0:T(8,128)(2,1)S(1)} %all-to-all-done.got_ref, f32[128,2048]{1,0:T(8,128)S(1)} %copy-done.1, f32[1,2048]{1,0:T(1,128)S(1)} %bitcast.6, bf16[256,256]{1,0:T(8,128)(2,1)S(1)} %copy-done.3), custom_call_target="tpu_custom_call" | custom-call | flops 10000000000 | bytes 10000000000 | tf_op jit(solution)/shard_map/pallas_call | solution.py:233
  18.9 16.1 %all-to-all-start.1 = ((bf16[16,16,128]{2,1,0:T(8,128)(2,1)}), bf16[16,16,128]{2,1,0:T(8,128)(2,1)S(1)}, u32[]{:S(2)}, u32[]{:S(2)}) async-start(bf16[16,16,128]{2,1,0:T(8,128)(2,1)} %shard_map.73), calls=%async_computation.1 | async-start | bytes 131072 | tf_op jit(solution)/shard_map/all_to_all | solution.py:299
  34.9 0.6 %shard_map.71 = bf16[3,144,512]{2,1,0:T(8,128)(2,1)S(1)} custom-call(s32[1]{0:T(128)} %bitcast.pos_ref, bf16[4,144,512]{2,1,0:T(8,128)(2,1)S(1)} %copy-done), custom_call_target="tpu_custom_call" | custom-call | tf_op jit(solution)/shard_map/pallas_call | solution.py:233
  35.5 2.8 %collective-permute-start.2 = (bf16[3,144,512]{2,1,0:T(8,128)(2,1)S(1)}, bf16[3,144,512]{2,1,0:T(8,128)(2,1)}, u32[]{:S(2)}, u32[]{:S(2)}) collective-permute-start(bf16[3,144,512]{2,1,0:T(8,128)(2,1)S(1)} %shard_map.71), channel_id=1, source_target_pairs={{0,3},{1,0},{2,1},{3,2},{4,7},{5,4},{6,5},{7,6},{8,11},{9,8},{10,9... | collective-permute-start | bytes 1327112 | tf_op jit(solution)/shard_map/ppermute | solution.py:279
  38.4 2.4 %all-to-all-done.1.got_ref = bf16[16,16,128]{2,1,0:T(8,128)(2,1)S(1)} async-done(((bf16[16,16,128]{2,1,0:T(8,128)(2,1)}), bf16[16,16,128]{2,1,0:T(8,128)(2,1)S(1)}, u32[]{:S(2)}, u32[]{:S(2)}) %all-to-all-start.1) | async-done | bytes 65568 | tf_op jit(solution)/shard_map/all_to_all | solution.py:299
  40.7 0.6 %shard_map.74 = bf16[32,4,128]{2,1,0:T(4,128)(2,1)} custom-call(bf16[16,16,128]{2,1,0:T(8,128)(2,1)S(1)} %all-to-all-done.1.got_ref), custom_call_target="tpu_custom_call" | custom-call | tf_op jit(solution)/shard_map/pallas_call | solution.py:233
  41.4 8.9 %all-to-all-start.2 = ((bf16[32,4,128]{2,1,0:T(4,128)(2,1)}), bf16[32,4,128]{2,1,0:T(4,128)(2,1)S(1)}, u32[]{:S(2)}, u32[]{:S(2)}) async-start(bf16[32,4,128]{2,1,0:T(4,128)(2,1)} %shard_map.74), calls=%async_computation.2 | async-start | bytes 65536 | tf_op jit(solution)/shard_map/all_to_all | solution.py:319
  50.3 0.0 collective-permute-done.first_ref.got1
  50.3 0.0 collective-permute-done.1.second_ref.got2
  50.3 0.0 collective-permute-done.2.got3
  50.3 4.5 %shard_map.72 = (bf16[4,32,2,2048]{3,2,1,0:T(2,128)(2,1)}, f32[8,128]{1,0:T(8,128)}) custom-call(s32[1]{0:T(128)} %bitcast.pos_ref, f32[8,128]{1,0:T(8,128)S(1)} %shard_map.70.after_ref, f32[128,2048]{1,0:T(8,128)S(1)} %copy-done.1, bf16[256,256]{1,0:T(8,128)(2,1)S(1)} %copy-done.2, bf16[4,144,512]{2,1,0:T(8,128)(2,1)S(1)} %copy-done, ...), custom_call_target="tpu_custom_call" | custom-call | tf_op jit(solution)/shard_map/pallas_call | solution.py:233
  54.8 2.7 %all-to-all-done.2.got_ref = bf16[32,4,128]{2,1,0:T(4,128)(2,1)S(1)} async-done(((bf16[32,4,128]{2,1,0:T(4,128)(2,1)}), bf16[32,4,128]{2,1,0:T(4,128)(2,1)S(1)}, u32[]{:S(2)}, u32[]{:S(2)}) %all-to-all-start.2) | async-done | bytes 32800 | tf_op jit(solution)/shard_map/all_to_all | solution.py:319
  57.5 0.7 %shard_map.75 = f32[8,4,32]{2,1,0:T(4,128)} custom-call(bf16[32,4,128]{2,1,0:T(4,128)(2,1)S(1)} %all-to-all-done.2.got_ref), custom_call_target="tpu_custom_call" | custom-call | tf_op jit(solution)/shard_map/pallas_call | solution.py:233
  (1 shorter events, 0.0 us)
Async XLA Ops:
  0.6 7.2 %copy-start.2 = (bf16[256,256]{1,0:T(8,128)(2,1)S(1)}, bf16[256,256]{1,0:T(8,128)(2,1)}, u32[]{:S(2)}) copy-start(bf16[256,256]{1,0:T(8,128)(2,1)} %constant.8.clone.refs_2_.table_ref) | copy-start | bytes 393220
  0.6 7.2 %copy-start.3 = (bf16[256,256]{1,0:T(8,128)(2,1)S(1)}, bf16[256,256]{1,0:T(8,128)(2,1)}, u32[]{:S(2)}) copy-start(bf16[256,256]{1,0:T(8,128)(2,1)} %constant.9.clone.refs_0_.table_ref) | copy-start | bytes 393220
  0.7 7.2 %copy-start.4 = (f32[2048]{0:T(1024)S(1)}, f32[2048]{0:T(1024)}, u32[]{:S(2)}) copy-start(f32[2048]{0:T(1024)} %param.7) | copy-start | bytes 24580
  2.7 5.2 %copy-start = (bf16[4,144,512]{2,1,0:T(8,128)(2,1)S(1)}, bf16[4,144,512]{2,1,0:T(8,128)(2,1)}, u32[]{:S(2)}) copy-start(bf16[4,144,512]{2,1,0:T(8,128)(2,1)} %shard_map.68.sent_ref.own_ref) | copy-start | bytes 1769476
  2.7 13.9 %copy-start.1 = (f32[128,2048]{1,0:T(8,128)S(1)}, f32[128,2048]{1,0:T(8,128)}, u32[]{:S(2)}) copy-start(f32[128,2048]{1,0:T(8,128)} %final_ref.3) | copy-start | bytes 3145732
  2.7 13.9 %all-to-all-start = ((bf16[4,144,512]{2,1,0:T(8,128)(2,1)}), bf16[4,144,512]{2,1,0:T(8,128)(2,1)S(1)}, u32[]{:S(2)}, u32[]{:S(2)}) async-start(bf16[4,144,512]{2,1,0:T(8,128)(2,1)} %shard_map.68.sent_ref.own_ref), calls=%async_computation | async-start | bytes 1179648 | tf_op jit(solution)/shard_map/all_to_all | solution.py:267
  8.9 41.4 %collective-permute-start = (bf16[3,144,512]{2,1,0:T(8,128)(2,1)}, bf16[3,144,512]{2,1,0:T(8,128)(2,1)S(1)}, u32[]{:S(2)}, u32[]{:S(2)}) collective-permute-start(bf16[3,144,512]{2,1,0:T(8,128)(2,1)} %get-tuple-element.5), channel_id=1, source_target_pairs={{0,1},{1,2},{2,3},{3,0},{4,5},{5,6},{6,7},{7,4},{8,9},{9,10},{10,1... | collective-permute-start | bytes 1327112 | tf_op jit(solution)/shard_map/ppermute | solution.py:279
  12.3 38.0 %collective-permute-start.1 = (bf16[3,144,512]{2,1,0:T(8,128)(2,1)}, bf16[3,144,512]{2,1,0:T(8,128)(2,1)}, u32[]{:S(2)}, u32[]{:S(2)}) collective-permute-start(bf16[3,144,512]{2,1,0:T(8,128)(2,1)} %get-tuple-element.6), channel_id=1, source_target_pairs={{0,2},{1,3},{2,0},{3,1},{4,6},{5,7},{6,4},{7,5},{8,10},{9,11},{10,... | collective-permute-start | bytes 1327112 | tf_op jit(solution)/shard_map/ppermute | solution.py:279
  18.9 21.9 %all-to-all-start.1 = ((bf16[16,16,128]{2,1,0:T(8,128)(2,1)}), bf16[16,16,128]{2,1,0:T(8,128)(2,1)S(1)}, u32[]{:S(2)}, u32[]{:S(2)}) async-start(bf16[16,16,128]{2,1,0:T(8,128)(2,1)} %shard_map.73), calls=%async_computation.1 | async-start | bytes 131072 | tf_op jit(solution)/shard_map/all_to_all | solution.py:299
  35.5 14.8 %collective-permute-start.2 = (bf16[3,144,512]{2,1,0:T(8,128)(2,1)S(1)}, bf16[3,144,512]{2,1,0:T(8,128)(2,1)}, u32[]{:S(2)}, u32[]{:S(2)}) collective-permute-start(bf16[3,144,512]{2,1,0:T(8,128)(2,1)S(1)} %shard_map.71), channel_id=1, source_target_pairs={{0,3},{1,0},{2,1},{3,2},{4,7},{5,4},{6,5},{7,6},{8,11},{9,8},{10,9... | collective-permute-start | bytes 1327112 | tf_op jit(solution)/shard_map/ppermute | solution.py:279
  41.4 16.2 %all-to-all-start.2 = ((bf16[32,4,128]{2,1,0:T(4,128)(2,1)}), bf16[32,4,128]{2,1,0:T(4,128)(2,1)S(1)}, u32[]{:S(2)}, u32[]{:S(2)}) async-start(bf16[32,4,128]{2,1,0:T(4,128)(2,1)} %shard_map.74), calls=%async_computation.2 | async-start | bytes 65536 | tf_op jit(solution)/shard_map/all_to_all | solution.py:319

commit v8 on v7

--- a/solution.py
+++ b/solution.py
@@ -280,7 +280,7 @@
             for step, value in zip(steps, parts)
         ]
 
-    moved = passed_on((1, 2), [apart, weights.reshape(1, points), table]) + passed_on((3,), [])
+    moved = passed_on((1,), [apart, weights.reshape(1, points), table]) + passed_on((2,), []) + passed_on((3,), [])
 
     group = ("blk", "x", "core")
     count = float(points * lax.axis_size(SPACE))

time: 58.6 us -> 58.6 us (level)
  starting transfers between devices: 40.6 us -> 39.9 us
  local copies, waits for them, and re-layouts: 0.03 us -> 0.7 us
    unnamed x10, local copies, waits for them, and re-layouts: 0.03 us -> 0.7 us
    pallas_call x7 -> x8, Pallas kernels: 9.68 us -> 9.74 us  [call(): pl.pallas_call(kernel, out_shape=out, in_specs=specs, out_specs=out_spec,...]
  transfers between devices with their start and end apart: 6 -> 6, of which waited for: 2 -> 2; matrix products, arithmetic and copies ran while one was open for 0% -> 0% of each run, Pallas kernels for 15% -> 16%
where the time goes in v8:
time: 58.6 us; the launch traced here: 58.2 us
  starting transfers between devices  39.9 us (68%)
  Pallas kernels  11.7 us (20%)
  waiting for transfers between devices  5.12 us (9%)
  between operations  0.79 us (1%)
  local copies, waits for them, and re-layouts  0.7 us (1%)
    all_to_all x1, starting transfers between devices, local(): lax.all_to_all(sums, 'z', 0, 0, tiled=True, axis_index_groups=[late_first...  15.6 us
    ppermute x3, starting transfers between devices, passed_on(): lax.ppermute(value, 'blk', [(i, (i + step) % BLOCKS) for i in range(BLOCK...  10.8 us
    pallas_call x8, Pallas kernels, call(): pl.pallas_call(kernel, out_shape=out, in_specs=specs, out_specs=out_spec,...  9.74 us
    all_to_all x1, starting transfers between devices, local(): lax.all_to_all(call(share_kernel, shares, [sums]), group, 0, 0, tiled=True)  8.36 us
    all_to_all x1, starting transfers between devices, local(): got = lax.all_to_all(sent, 'blk', 0, 0, tiled=True)  5.16 us
    all_to_all x1, waiting for transfers between devices, local(): lax.all_to_all(call(share_kernel, shares, [sums]), group, 0, 0, tiled=True)  3.03 us
    all_to_all x1, waiting for transfers between devices, local(): lax.all_to_all(sums, 'z', 0, 0, tiled=True, axis_index_groups=[late_first...  2.08 us
    pallas_call x1, Pallas kernels, local(): pl.pallas_call(split_kernel, out_shape=jax.ShapeDtypeStruct((BLOCKS, HOP...  1.97 us
  transfers between devices with their start and end apart: 6, of which 2 were waited for; matrix products, arithmetic and copies ran while one was open for 0% of the time, Pallas kernels for 16%

profile of v8, /device:TPU:1, one launch (start us, length us, event | category | flops | bytes accessed | tf_op | source)
XLA Modules:
  0.0 58.2 jit_solution(13005932299331532829)
XLA Ops:
  0.6 2.0 %shard_map.68.sent_ref.own_ref = bf16[4,144,512]{2,1,0:T(8,128)(2,1)} custom-call(f32[128,2048]{1,0:T(8,128)} %pressure_ref.1), custom_call_target="tpu_custom_call" | custom-call | tf_op jit(solution)/shard_map/pallas_call | solution.py:254
  2.6 0.0 copy-start
  2.6 0.0 copy-start.2
  2.6 0.0 copy-start.3
  2.6 5.2 %all-to-all-start = ((bf16[4,144,512]{2,1,0:T(8,128)(2,1)}), bf16[4,144,512]{2,1,0:T(8,128)(2,1)S(1)}, u32[]{:S(2)}, u32[]{:S(2)}) async-start(bf16[4,144,512]{2,1,0:T(8,128)(2,1)} %shard_map.68.sent_ref.own_ref), calls=%async_computation | async-start | bytes 1179648 | tf_op jit(solution)/shard_map/all_to_all | solution.py:267
  7.8 0.0 copy-start.4
  7.8 0.0 copy-done
  7.8 0.0 copy-done.2
  7.8 0.0 copy-done.3
  7.8 0.7 %copy-done.4 = f32[2048]{0:T(1024)S(1)} copy-done((f32[2048]{0:T(1024)S(1)}, f32[2048]{0:T(1024)}, u32[]{:S(2)}) %copy-start.4) | copy-done | bytes 8216
  8.5 0.0 copy-start.1
  8.5 0.8 %shard_map.69 = bf16[3,144,512]{2,1,0:T(8,128)(2,1)} custom-call(s32[1]{0:T(128)} %bitcast.pos_ref, bf16[4,144,512]{2,1,0:T(8,128)(2,1)S(1)} %copy-done, bf16[256,256]{1,0:T(8,128)(2,1)S(1)} %copy-done.3, f32[1,2048]{1,0:T(1,128)S(1)} %bitcast.5, bf16[256,256]{1,0:T(8,128)(2,1)S(1)} %copy-done.2), custom_call_target="tpu_custom_call" | custom-call | tf_op jit(solution)/shard_map/pallas_call | solution.py:233
  9.3 3.4 %collective-permute-start = (bf16[3,144,512]{2,1,0:T(8,128)(2,1)}, bf16[3,144,512]{2,1,0:T(8,128)(2,1)}, u32[]{:S(2)}, u32[]{:S(2)}) collective-permute-start(bf16[3,144,512]{2,1,0:T(8,128)(2,1)} %shard_map.69), channel_id=1, source_target_pairs={{0,1},{1,2},{2,3},{3,0},{4,5},{5,6},{6,7},{7,4},{8,9},{9,10},{10,1... | collective-permute-start | bytes 1327112 | tf_op jit(solution)/shard_map/ppermute | solution.py:279
  12.7 0.6 %shard_map.70 = bf16[3,144,512]{2,1,0:T(8,128)(2,1)S(1)} custom-call(s32[1]{0:T(128)} %bitcast.pos_ref, bf16[4,144,512]{2,1,0:T(8,128)(2,1)S(1)} %copy-done), custom_call_target="tpu_custom_call" | custom-call | tf_op jit(solution)/shard_map/pallas_call | solution.py:233
  13.3 4.3 %collective-permute-start.1 = (bf16[3,144,512]{2,1,0:T(8,128)(2,1)S(1)}, bf16[3,144,512]{2,1,0:T(8,128)(2,1)}, u32[]{:S(2)}, u32[]{:S(2)}) collective-permute-start(bf16[3,144,512]{2,1,0:T(8,128)(2,1)S(1)} %shard_map.70), channel_id=1, source_target_pairs={{0,2},{1,3},{2,0},{3,1},{4,6},{5,7},{6,4},{7,5},{8,10},{9,11},{10,... | collective-permute-start | bytes 1327112 | tf_op jit(solution)/shard_map/ppermute | solution.py:279
  17.6 0.0 all-to-all-done.got_ref
  17.6 0.0 copy-done.1
  17.6 2.2 %shard_map.74 = bf16[16,16,128]{2,1,0:T(8,128)(2,1)} custom-call(s32[1]{0:T(128)} %bitcast.pos_ref, bf16[4,144,512]{2,1,0:T(8,128)(2,1)S(1)} %all-to-all-done.got_ref, f32[128,2048]{1,0:T(8,128)S(1)} %copy-done.1, f32[1,2048]{1,0:T(1,128)S(1)} %bitcast.6, bf16[256,256]{1,0:T(8,128)(2,1)S(1)} %copy-done.3), custom_call_target="tpu_custom_call" | custom-call | flops 10000000000 | bytes 10000000000 | tf_op jit(solution)/shard_map/pallas_call | solution.py:233
  19.8 15.6 %all-to-all-start.1 = ((bf16[16,16,128]{2,1,0:T(8,128)(2,1)}), bf16[16,16,128]{2,1,0:T(8,128)(2,1)S(1)}, u32[]{:S(2)}, u32[]{:S(2)}) async-start(bf16[16,16,128]{2,1,0:T(8,128)(2,1)} %shard_map.74), calls=%async_computation.1 | async-start | bytes 131072 | tf_op jit(solution)/shard_map/all_to_all | solution.py:299
  35.4 0.6 %shard_map.72 = bf16[3,144,512]{2,1,0:T(8,128)(2,1)S(1)} custom-call(s32[1]{0:T(128)} %bitcast.pos_ref, bf16[4,144,512]{2,1,0:T(8,128)(2,1)S(1)} %copy-done), custom_call_target="tpu_custom_call" | custom-call | tf_op jit(solution)/shard_map/pallas_call | solution.py:233
  36.0 3.1 %collective-permute-start.2 = (bf16[3,144,512]{2,1,0:T(8,128)(2,1)S(1)}, bf16[3,144,512]{2,1,0:T(8,128)(2,1)}, u32[]{:S(2)}, u32[]{:S(2)}) collective-permute-start(bf16[3,144,512]{2,1,0:T(8,128)(2,1)S(1)} %shard_map.72), channel_id=1, source_target_pairs={{0,3},{1,0},{2,1},{3,2},{4,7},{5,4},{6,5},{7,6},{8,11},{9,8},{10,9... | collective-permute-start | bytes 1327112 | tf_op jit(solution)/shard_map/ppermute | solution.py:279
  39.2 2.1 %all-to-all-done.1.got_ref = bf16[16,16,128]{2,1,0:T(8,128)(2,1)S(1)} async-done(((bf16[16,16,128]{2,1,0:T(8,128)(2,1)}), bf16[16,16,128]{2,1,0:T(8,128)(2,1)S(1)}, u32[]{:S(2)}, u32[]{:S(2)}) %all-to-all-start.1) | async-done | bytes 65568 | tf_op jit(solution)/shard_map/all_to_all | solution.py:299
  41.2 0.6 %shard_map.75 = bf16[32,4,128]{2,1,0:T(4,128)(2,1)} custom-call(bf16[16,16,128]{2,1,0:T(8,128)(2,1)S(1)} %all-to-all-done.1.got_ref), custom_call_target="tpu_custom_call" | custom-call | tf_op jit(solution)/shard_map/pallas_call | solution.py:233
  41.9 8.4 %all-to-all-start.2 = ((bf16[32,4,128]{2,1,0:T(4,128)(2,1)}), bf16[32,4,128]{2,1,0:T(4,128)(2,1)S(1)}, u32[]{:S(2)}, u32[]{:S(2)}) async-start(bf16[32,4,128]{2,1,0:T(4,128)(2,1)} %shard_map.75), calls=%async_computation.2 | async-start | bytes 65536 | tf_op jit(solution)/shard_map/all_to_all | solution.py:319
  50.2 0.0 collective-permute-done.first_ref.got1
  50.3 0.0 collective-permute-done.1.second_ref.got2
  50.3 0.0 collective-permute-done.2.got3
  50.3 4.2 %shard_map.73 = (bf16[4,32,2,2048]{3,2,1,0:T(2,128)(2,1)}, f32[8,128]{1,0:T(8,128)}) custom-call(s32[1]{0:T(128)} %bitcast.pos_ref, f32[8,128]{1,0:T(8,128)S(1)} %shard_map.71.after_ref, f32[128,2048]{1,0:T(8,128)S(1)} %copy-done.1, bf16[256,256]{1,0:T(8,128)(2,1)S(1)} %copy-done.2, bf16[4,144,512]{2,1,0:T(8,128)(2,1)S(1)} %copy-done, ...), custom_call_target="tpu_custom_call" | custom-call | tf_op jit(solution)/shard_map/pallas_call | solution.py:233
  54.5 3.0 %all-to-all-done.2.got_ref = bf16[32,4,128]{2,1,0:T(4,128)(2,1)S(1)} async-done(((bf16[32,4,128]{2,1,0:T(4,128)(2,1)}), bf16[32,4,128]{2,1,0:T(4,128)(2,1)S(1)}, u32[]{:S(2)}, u32[]{:S(2)}) %all-to-all-start.2) | async-done | bytes 32800 | tf_op jit(solution)/shard_map/all_to_all | solution.py:319
  57.5 0.7 %shard_map.76 = f32[8,4,32]{2,1,0:T(4,128)} custom-call(bf16[32,4,128]{2,1,0:T(4,128)(2,1)S(1)} %all-to-all-done.2.got_ref), custom_call_target="tpu_custom_call" | custom-call | tf_op jit(solution)/shard_map/pallas_call | solution.py:233
  (1 shorter events, 0.0 us)
Async XLA Ops:
  2.6 5.2 %copy-start = (bf16[4,144,512]{2,1,0:T(8,128)(2,1)S(1)}, bf16[4,144,512]{2,1,0:T(8,128)(2,1)}, u32[]{:S(2)}) copy-start(bf16[4,144,512]{2,1,0:T(8,128)(2,1)} %shard_map.68.sent_ref.own_ref) | copy-start | bytes 1769476
  2.6 5.2 %copy-start.2 = (bf16[256,256]{1,0:T(8,128)(2,1)S(1)}, bf16[256,256]{1,0:T(8,128)(2,1)}, u32[]{:S(2)}) copy-start(bf16[256,256]{1,0:T(8,128)(2,1)} %constant.8.clone.refs_2_.table_ref) | copy-start | bytes 393220
  2.6 5.2 %copy-start.3 = (bf16[256,256]{1,0:T(8,128)(2,1)S(1)}, bf16[256,256]{1,0:T(8,128)(2,1)}, u32[]{:S(2)}) copy-start(bf16[256,256]{1,0:T(8,128)(2,1)} %constant.9.clone.refs_0_.table_ref) | copy-start | bytes 393220
  2.6 15.0 %all-to-all-start = ((bf16[4,144,512]{2,1,0:T(8,128)(2,1)}), bf16[4,144,512]{2,1,0:T(8,128)(2,1)S(1)}, u32[]{:S(2)}, u32[]{:S(2)}) async-start(bf16[4,144,512]{2,1,0:T(8,128)(2,1)} %shard_map.68.sent_ref.own_ref), calls=%async_computation | async-start | bytes 1179648 | tf_op jit(solution)/shard_map/all_to_all | solution.py:267
  7.8 0.7 %copy-start.4 = (f32[2048]{0:T(1024)S(1)}, f32[2048]{0:T(1024)}, u32[]{:S(2)}) copy-start(f32[2048]{0:T(1024)} %param.7) | copy-start | bytes 24580
  8.5 9.1 %copy-start.1 = (f32[128,2048]{1,0:T(8,128)S(1)}, f32[128,2048]{1,0:T(8,128)}, u32[]{:S(2)}) copy-start(f32[128,2048]{1,0:T(8,128)} %final_ref.3) | copy-start | bytes 3145732
  9.3 40.9 %collective-permute-start = (bf16[3,144,512]{2,1,0:T(8,128)(2,1)}, bf16[3,144,512]{2,1,0:T(8,128)(2,1)}, u32[]{:S(2)}, u32[]{:S(2)}) collective-permute-start(bf16[3,144,512]{2,1,0:T(8,128)(2,1)} %shard_map.69), channel_id=1, source_target_pairs={{0,1},{1,2},{2,3},{3,0},{4,5},{5,6},{6,7},{7,4},{8,9},{9,10},{10,1... | collective-permute-start | bytes 1327112 | tf_op jit(solution)/shard_map/ppermute | solution.py:279
  13.3 36.9 %collective-permute-start.1 = (bf16[3,144,512]{2,1,0:T(8,128)(2,1)S(1)}, bf16[3,144,512]{2,1,0:T(8,128)(2,1)}, u32[]{:S(2)}, u32[]{:S(2)}) collective-permute-start(bf16[3,144,512]{2,1,0:T(8,128)(2,1)S(1)} %shard_map.70), channel_id=1, source_target_pairs={{0,2},{1,3},{2,0},{3,1},{4,6},{5,7},{6,4},{7,5},{8,10},{9,11},{10,... | collective-permute-start | bytes 1327112 | tf_op jit(solution)/shard_map/ppermute | solution.py:279
  19.8 21.4 %all-to-all-start.1 = ((bf16[16,16,128]{2,1,0:T(8,128)(2,1)}), bf16[16,16,128]{2,1,0:T(8,128)(2,1)S(1)}, u32[]{:S(2)}, u32[]{:S(2)}) async-start(bf16[16,16,128]{2,1,0:T(8,128)(2,1)} %shard_map.74), calls=%async_computation.1 | async-start | bytes 131072 | tf_op jit(solution)/shard_map/all_to_all | solution.py:299
  36.0 14.2 %collective-permute-start.2 = (bf16[3,144,512]{2,1,0:T(8,128)(2,1)S(1)}, bf16[3,144,512]{2,1,0:T(8,128)(2,1)}, u32[]{:S(2)}, u32[]{:S(2)}) collective-permute-start(bf16[3,144,512]{2,1,0:T(8,128)(2,1)S(1)} %shard_map.72), channel_id=1, source_target_pairs={{0,3},{1,0},{2,1},{3,2},{4,7},{5,4},{6,5},{7,6},{8,11},{9,8},{10,9... | collective-permute-start | bytes 1327112 | tf_op jit(solution)/shard_map/ppermute | solution.py:279
  41.9 15.6 %all-to-all-start.2 = ((bf16[32,4,128]{2,1,0:T(4,128)(2,1)}), bf16[32,4,128]{2,1,0:T(4,128)(2,1)S(1)}, u32[]{:S(2)}, u32[]{:S(2)}) async-start(bf16[32,4,128]{2,1,0:T(4,128)(2,1)} %shard_map.75), calls=%async_computation.2 | async-start | bytes 65536 | tf_op jit(solution)/shard_map/all_to_all | solution.py:319

commit v9 on v8

--- a/solution.py
+++ b/solution.py
@@ -280,7 +280,8 @@
             for step, value in zip(steps, parts)
         ]
 
-    moved = passed_on((1,), [apart, weights.reshape(1, points), table]) + passed_on((2,), []) + passed_on((3,), [])
+    two_on = passed_on((2,), [apart, weights.reshape(1, points), table])
+    moved = passed_on((1,), []) + two_on + passed_on((3,), [])
 
     group = ("blk", "x", "core")
     count = float(points * lax.axis_size(SPACE))

time: 58.6 us -> 65.3 us (1.11)
  starting transfers between devices: 39.9 us -> 47.7 us
  waiting for transfers between devices: 5.12 us -> 3.95 us
    all_to_all x1, starting transfers between devices: 8.36 us -> 15.6 us  [local(): lax.all_to_all(call(share_kernel, shares, [sums]), group, 0, 0, tiled=True)]
    all_to_all x1, waiting for transfers between devices: 2.08 us -> 0.91 us  [local(): lax.all_to_all(sums, 'z', 0, 0, tiled=True, axis_index_groups=[late_first...]
  transfers between devices with their start and end apart: 6 -> 6, of which waited for: 2 -> 2; matrix products, arithmetic and copies ran while one was open for 0% -> 0% of each run, Pallas kernels for 16% -> 14%
where the time goes in v9:
time: 65.3 us; the launch traced here: 64.9 us
  starting transfers between devices  47.7 us (73%)
  Pallas kernels  11.7 us (18%)
  waiting for transfers between devices  3.95 us (6%)
  between operations  0.79 us (1%)
  local copies, waits for them, and re-layouts  0.7 us (1%)
    all_to_all x1, starting transfers between devices, local(): lax.all_to_all(sums, 'z', 0, 0, tiled=True, axis_index_groups=[late_first...  15.6 us
    all_to_all x1, starting transfers between devices, local(): lax.all_to_all(call(share_kernel, shares, [sums]), group, 0, 0, tiled=True)  15.6 us
    ppermute x3, starting transfers between devices, passed_on(): lax.ppermute(value, 'blk', [(i, (i + step) % BLOCKS) for i in range(BLOCK...  11.3 us
    pallas_call x8, Pallas kernels, call(): pl.pallas_call(kernel, out_shape=out, in_specs=specs, out_specs=out_spec,...  9.74 us
    all_to_all x1, starting transfers between devices, local(): got = lax.all_to_all(sent, 'blk', 0, 0, tiled=True)  5.16 us
    all_to_all x1, waiting for transfers between devices, local(): lax.all_to_all(call(share_kernel, shares, [sums]), group, 0, 0, tiled=True)  3.03 us
    pallas_call x1, Pallas kernels, local(): pl.pallas_call(split_kernel, out_shape=jax.ShapeDtypeStruct((BLOCKS, HOP...  1.97 us
  transfers between devices with their start and end apart: 6, of which 2 were waited for; matrix products, arithmetic and copies ran while one was open for 0% of the time, Pallas kernels for 14%

profile of v9, /device:TPU:1, one launch (start us, length us, event | category | flops | bytes accessed | tf_op | source)
XLA Modules:
  0.0 64.9 jit_solution(15159003376931172053)
XLA Ops:
  0.6 2.0 %shard_map.68.sent_ref.own_ref = bf16[4,144,512]{2,1,0:T(8,128)(2,1)} custom-call(f32[128,2048]{1,0:T(8,128)} %pressure_ref.1), custom_call_target="tpu_custom_call" | custom-call | tf_op jit(solution)/shard_map/pallas_call | solution.py:254
  2.6 0.0 copy-start
  2.6 0.0 copy-start.2
  2.6 0.0 copy-start.3
  2.6 5.2 %all-to-all-start = ((bf16[4,144,512]{2,1,0:T(8,128)(2,1)}), bf16[4,144,512]{2,1,0:T(8,128)(2,1)S(1)}, u32[]{:S(2)}, u32[]{:S(2)}) async-start(bf16[4,144,512]{2,1,0:T(8,128)(2,1)} %shard_map.68.sent_ref.own_ref), calls=%async_computation | async-start | bytes 1179648 | tf_op jit(solution)/shard_map/all_to_all | solution.py:267
  7.8 0.0 copy-start.4
  7.8 0.0 copy-done
  7.8 0.0 copy-done.2
  7.8 0.0 copy-done.3
  7.8 0.7 %copy-done.4 = f32[2048]{0:T(1024)S(1)} copy-done((f32[2048]{0:T(1024)S(1)}, f32[2048]{0:T(1024)}, u32[]{:S(2)}) %copy-start.4) | copy-done | bytes 8216
  8.5 0.0 copy-start.1
  8.5 0.8 %shard_map.70 = bf16[3,144,512]{2,1,0:T(8,128)(2,1)} custom-call(s32[1]{0:T(128)} %bitcast.pos_ref, bf16[4,144,512]{2,1,0:T(8,128)(2,1)S(1)} %copy-done, bf16[256,256]{1,0:T(8,128)(2,1)S(1)} %copy-done.3, f32[1,2048]{1,0:T(1,128)S(1)} %bitcast.5, bf16[256,256]{1,0:T(8,128)(2,1)S(1)} %copy-done.2), custom_call_target="tpu_custom_call" | custom-call | tf_op jit(solution)/shard_map/pallas_call | solution.py:233
  9.3 4.9 %collective-permute-start.1 = (bf16[3,144,512]{2,1,0:T(8,128)(2,1)}, bf16[3,144,512]{2,1,0:T(8,128)(2,1)}, u32[]{:S(2)}, u32[]{:S(2)}) collective-permute-start(bf16[3,144,512]{2,1,0:T(8,128)(2,1)} %shard_map.70), channel_id=1, source_target_pairs={{0,2},{1,3},{2,0},{3,1},{4,6},{5,7},{6,4},{7,5},{8,10},{9,11},{10,... | collective-permute-start | bytes 1327112 | tf_op jit(solution)/shard_map/ppermute | solution.py:279
  14.2 0.6 shard_map.69
  14.8 2.2 %collective-permute-start = (bf16[3,144,512]{2,1,0:T(8,128)(2,1)S(1)}, bf16[3,144,512]{2,1,0:T(8,128)(2,1)}, u32[]{:S(2)}, u32[]{:S(2)}) collective-permute-start(bf16[3,144,512]{2,1,0:T(8,128)(2,1)S(1)} %shard_map.69), channel_id=1, source_target_pairs={{0,1},{1,2},{2,3},{3,0},{4,5},{5,6},{6,7},{7,4},{8,9},{9,10},{10,1... | collective-permute-start | bytes 1327112 | tf_op jit(solution)/shard_map/ppermute | solution.py:279
  17.0 0.0 all-to-all-done.got_ref
  17.0 0.0 copy-done.1
  17.0 2.2 %shard_map.74 = bf16[16,16,128]{2,1,0:T(8,128)(2,1)} custom-call(s32[1]{0:T(128)} %bitcast.pos_ref, bf16[4,144,512]{2,1,0:T(8,128)(2,1)S(1)} %all-to-all-done.got_ref, f32[128,2048]{1,0:T(8,128)S(1)} %copy-done.1, f32[1,2048]{1,0:T(1,128)S(1)} %bitcast.6, bf16[256,256]{1,0:T(8,128)(2,1)S(1)} %copy-done.3), custom_call_target="tpu_custom_call" | custom-call | flops 10000000000 | bytes 10000000000 | tf_op jit(solution)/shard_map/pallas_call | solution.py:233
  19.2 15.6 %all-to-all-start.1 = ((bf16[16,16,128]{2,1,0:T(8,128)(2,1)}), bf16[16,16,128]{2,1,0:T(8,128)(2,1)S(1)}, u32[]{:S(2)}, u32[]{:S(2)}) async-start(bf16[16,16,128]{2,1,0:T(8,128)(2,1)} %shard_map.74), calls=%async_computation.1 | async-start | bytes 131072 | tf_op jit(solution)/shard_map/all_to_all | solution.py:300
  34.9 0.6 shard_map.72
  35.5 4.3 %collective-permute-start.2 = (bf16[3,144,512]{2,1,0:T(8,128)(2,1)S(1)}, bf16[3,144,512]{2,1,0:T(8,128)(2,1)}, u32[]{:S(2)}, u32[]{:S(2)}) collective-permute-start(bf16[3,144,512]{2,1,0:T(8,128)(2,1)S(1)} %shard_map.72), channel_id=1, source_target_pairs={{0,3},{1,0},{2,1},{3,2},{4,7},{5,4},{6,5},{7,6},{8,11},{9,8},{10,9... | collective-permute-start | bytes 1327112 | tf_op jit(solution)/shard_map/ppermute | solution.py:279
  39.8 0.9 %all-to-all-done.1.got_ref = bf16[16,16,128]{2,1,0:T(8,128)(2,1)S(1)} async-done(((bf16[16,16,128]{2,1,0:T(8,128)(2,1)}), bf16[16,16,128]{2,1,0:T(8,128)(2,1)S(1)}, u32[]{:S(2)}, u32[]{:S(2)}) %all-to-all-start.1) | async-done | bytes 65568 | tf_op jit(solution)/shard_map/all_to_all | solution.py:300
  40.7 0.6 shard_map.75
  41.3 15.6 %all-to-all-start.2 = ((bf16[32,4,128]{2,1,0:T(4,128)(2,1)}), bf16[32,4,128]{2,1,0:T(4,128)(2,1)S(1)}, u32[]{:S(2)}, u32[]{:S(2)}) async-start(bf16[32,4,128]{2,1,0:T(4,128)(2,1)} %shard_map.75), calls=%async_computation.2 | async-start | bytes 65536 | tf_op jit(solution)/shard_map/all_to_all | solution.py:320
  56.9 0.0 collective-permute-done.1.second_ref.got2
  56.9 0.0 collective-permute-done.first_ref.got1
  57.0 0.0 collective-permute-done.2.got3
  57.0 4.2 %shard_map.73 = (bf16[4,32,2,2048]{3,2,1,0:T(2,128)(2,1)}, f32[8,128]{1,0:T(8,128)}) custom-call(s32[1]{0:T(128)} %bitcast.pos_ref, f32[8,128]{1,0:T(8,128)S(1)} %shard_map.71.after_ref, f32[128,2048]{1,0:T(8,128)S(1)} %copy-done.1, bf16[256,256]{1,0:T(8,128)(2,1)S(1)} %copy-done.2, bf16[4,144,512]{2,1,0:T(8,128)(2,1)S(1)} %copy-done, ...), custom_call_target="tpu_custom_call" | custom-call | tf_op jit(solution)/shard_map/pallas_call | solution.py:233
  61.1 3.0 %all-to-all-done.2.got_ref = bf16[32,4,128]{2,1,0:T(4,128)(2,1)S(1)} async-done(((bf16[32,4,128]{2,1,0:T(4,128)(2,1)}), bf16[32,4,128]{2,1,0:T(4,128)(2,1)S(1)}, u32[]{:S(2)}, u32[]{:S(2)}) %all-to-all-start.2) | async-done | bytes 32800 | tf_op jit(solution)/shard_map/all_to_all | solution.py:320
  64.2 0.7 %shard_map.76 = f32[8,4,32]{2,1,0:T(4,128)} custom-call(bf16[32,4,128]{2,1,0:T(4,128)(2,1)S(1)} %all-to-all-done.2.got_ref), custom_call_target="tpu_custom_call" | custom-call | tf_op jit(solution)/shard_map/pallas_call | solution.py:233
  (1 shorter events, 0.0 us)
Async XLA Ops:
  2.6 5.2 %copy-start = (bf16[4,144,512]{2,1,0:T(8,128)(2,1)S(1)}, bf16[4,144,512]{2,1,0:T(8,128)(2,1)}, u32[]{:S(2)}) copy-start(bf16[4,144,512]{2,1,0:T(8,128)(2,1)} %shard_map.68.sent_ref.own_ref) | copy-start | bytes 1769476
  2.6 5.2 %copy-start.2 = (bf16[256,256]{1,0:T(8,128)(2,1)S(1)}, bf16[256,256]{1,0:T(8,128)(2,1)}, u32[]{:S(2)}) copy-start(bf16[256,256]{1,0:T(8,128)(2,1)} %constant.8.clone.refs_2_.table_ref) | copy-start | bytes 393220
  2.6 5.2 %copy-start.3 = (bf16[256,256]{1,0:T(8,128)(2,1)S(1)}, bf16[256,256]{1,0:T(8,128)(2,1)}, u32[]{:S(2)}) copy-start(bf16[256,256]{1,0:T(8,128)(2,1)} %constant.9.clone.refs_0_.table_ref) | copy-start | bytes 393220
  2.6 14.4 %all-to-all-start = ((bf16[4,144,512]{2,1,0:T(8,128)(2,1)}), bf16[4,144,512]{2,1,0:T(8,128)(2,1)S(1)}, u32[]{:S(2)}, u32[]{:S(2)}) async-start(bf16[4,144,512]{2,1,0:T(8,128)(2,1)} %shard_map.68.sent_ref.own_ref), calls=%async_computation | async-start | bytes 1179648 | tf_op jit(solution)/shard_map/all_to_all | solution.py:267
  7.8 0.7 %copy-start.4 = (f32[2048]{0:T(1024)S(1)}, f32[2048]{0:T(1024)}, u32[]{:S(2)}) copy-start(f32[2048]{0:T(1024)} %param.7) | copy-start | bytes 24580
  8.5 8.5 %copy-start.1 = (f32[128,2048]{1,0:T(8,128)S(1)}, f32[128,2048]{1,0:T(8,128)}, u32[]{:S(2)}) copy-start(f32[128,2048]{1,0:T(8,128)} %final_ref.3) | copy-start | bytes 3145732
  9.3 47.6 %collective-permute-start.1 = (bf16[3,144,512]{2,1,0:T(8,128)(2,1)}, bf16[3,144,512]{2,1,0:T(8,128)(2,1)}, u32[]{:S(2)}, u32[]{:S(2)}) collective-permute-start(bf16[3,144,512]{2,1,0:T(8,128)(2,1)} %shard_map.70), channel_id=1, source_target_pairs={{0,2},{1,3},{2,0},{3,1},{4,6},{5,7},{6,4},{7,5},{8,10},{9,11},{10,... | collective-permute-start | bytes 1327112 | tf_op jit(solution)/shard_map/ppermute | solution.py:279
  14.8 42.1 %collective-permute-start = (bf16[3,144,512]{2,1,0:T(8,128)(2,1)S(1)}, bf16[3,144,512]{2,1,0:T(8,128)(2,1)}, u32[]{:S(2)}, u32[]{:S(2)}) collective-permute-start(bf16[3,144,512]{2,1,0:T(8,128)(2,1)S(1)} %shard_map.69), channel_id=1, source_target_pairs={{0,1},{1,2},{2,3},{3,0},{4,5},{5,6},{6,7},{7,4},{8,9},{9,10},{10,1... | collective-permute-start | bytes 1327112 | tf_op jit(solution)/shard_map/ppermute | solution.py:279
  19.2 21.4 %all-to-all-start.1 = ((bf16[16,16,128]{2,1,0:T(8,128)(2,1)}), bf16[16,16,128]{2,1,0:T(8,128)(2,1)S(1)}, u32[]{:S(2)}, u32[]{:S(2)}) async-start(bf16[16,16,128]{2,1,0:T(8,128)(2,1)} %shard_map.74), calls=%async_computation.1 | async-start | bytes 131072 | tf_op jit(solution)/shard_map/all_to_all | solution.py:300
  35.5 21.5 %collective-permute-start.2 = (bf16[3,144,512]{2,1,0:T(8,128)(2,1)S(1)}, bf16[3,144,512]{2,1,0:T(8,128)(2,1)}, u32[]{:S(2)}, u32[]{:S(2)}) collective-permute-start(bf16[3,144,512]{2,1,0:T(8,128)(2,1)S(1)} %shard_map.72), channel_id=1, source_target_pairs={{0,3},{1,0},{2,1},{3,2},{4,7},{5,4},{6,5},{7,6},{8,11},{9,8},{10,9... | collective-permute-start | bytes 1327112 | tf_op jit(solution)/shard_map/ppermute | solution.py:279
  41.3 22.9 %all-to-all-start.2 = ((bf16[32,4,128]{2,1,0:T(4,128)(2,1)}), bf16[32,4,128]{2,1,0:T(4,128)(2,1)S(1)}, u32[]{:S(2)}, u32[]{:S(2)}) async-start(bf16[32,4,128]{2,1,0:T(4,128)(2,1)} %shard_map.75), calls=%async_computation.2 | async-start | bytes 65536 | tf_op jit(solution)/shard_map/all_to_all | solution.py:320
